TPU v7x, 32 devices: a whole 2x2x4 slice. The times are simulated.
32 devices in a mesh: dp: 8 (over z, x), seq: 4 (over y, core).
Axes of the slice: x: 2, y: 2, z: 4, core: 2. Of those that a mesh axis runs over, the one named last changes fastest.
Arguments:
- queries: bfloat16 [8192, 2560], P(('dp', 'seq')), may hold values from -200 to 200
- keys: bfloat16 [8192, 2560], P(('dp', 'seq')), may hold values from -200 to 200
- values: bfloat16 [8192, 2560], P(('dp', 'seq')), may hold values from -6 to 6
- gain_q: float32 [2560], replicated, may hold values from 0.5 to 1.5
- gain_k: float32 [2560], replicated, may hold values from 0.5 to 1.5
- tile_pairs: int32 [16, 8], replicated, may hold values from 0 to 15, as said below
- tile_lens: int32 [8, 16], P('dp'), may hold values from 40 to 64
- out_grad: bfloat16 [8192, 5120], P(('dp', 'seq')), may hold values from -6 to 6
- w_out: bfloat16 [5120, 2560], P('dp', 'seq'), may hold values from -0.125 to 0.125
Outputs:
- grad_q: bfloat16 [8192, 2560], P(('dp', 'seq'))
- grad_k: bfloat16 [8192, 2560], P(('dp', 'seq'))
- grad_v: bfloat16 [8192, 2560], P(('dp', 'seq'))
- grad_w: float32 [5120, 2560], P('dp', 'seq')
Inputs may be any that keep to these rules, and one draw needn't show every extreme that they name: `tile_pairs`: row a lists 8 different tiles of the window, with tile a first.
All inputs are finite; a program needn't handle non-finite values.
Results may differ from a plain program's by a relative error of at most 0.02.
Values may be sent and summed in bfloat16 or wider, within the bound.
A program may use at most 128 MiB of HBM per device.

v0:
```python
import math

import jax
import jax.numpy as jnp
from jax import lax
from jax.sharding import PartitionSpec as P

HEAD_DIM = 128


EPS = 1e-06


def multiply(pattern, left, right):
    return jnp.einsum(pattern, left, right, preferred_element_type=jnp.float32)


def normalize(field, gain):
    values_f = field.astype(jnp.float32)
    row_scale = lax.rsqrt(jnp.mean(values_f * values_f, axis=-1, keepdims=True) + EPS)
    return ((values_f * row_scale * gain).astype(jnp.bfloat16), row_scale)


def norm_finish(values_f, row_scale, gated, inner, width):
    return (row_scale * gated - values_f * row_scale**3 * inner / width).astype(jnp.bfloat16)


def tile_attention(query_tiles, key_tiles, value_tiles, grad_tiles, tile_pairs, live_lengths):
    tile_count, tile_rows, head_width = query_tiles.shape
    neighbours = tile_pairs.shape[1]
    factor = 1.0 / math.sqrt(head_width)
    key_near = jnp.take(key_tiles, tile_pairs, axis=0).reshape(
        tile_count, neighbours * tile_rows, head_width
    )
    value_near = jnp.take(value_tiles, tile_pairs, axis=0).reshape(
        tile_count, neighbours * tile_rows, head_width
    )
    near_lengths = jnp.take(live_lengths, tile_pairs, axis=0)
    live = (
        jnp.arange(tile_rows, dtype=jnp.int32)[None, None, :] < near_lengths[:, :, None]
    ).reshape(tile_count, neighbours * tile_rows)
    scores = multiply("aqd,akd->aqk", query_tiles, key_near) * factor
    scores = jnp.where(live[:, None, :], scores, -jnp.inf)
    row_max = jnp.max(scores, axis=-1, keepdims=True)
    weights = jnp.exp(scores - row_max)
    probs = weights / jnp.sum(weights, axis=-1, keepdims=True)
    probs_low = probs.astype(jnp.bfloat16)
    attended = multiply("aqk,akd->aqd", probs_low, value_near).astype(jnp.bfloat16)
    grad_probs = multiply("aqd,akd->aqk", grad_tiles, value_near)
    delta = jnp.sum(probs * grad_probs, axis=-1, keepdims=True)
    grad_scores = (probs * (grad_probs - delta)).astype(jnp.bfloat16)
    grad_query = (multiply("aqk,akd->aqd", grad_scores, key_near) * factor).astype(jnp.bfloat16)
    grad_key_near = multiply("aqk,aqd->akd", grad_scores, query_tiles) * factor
    grad_value_near = multiply("aqk,aqd->akd", probs_low, grad_tiles)
    owners = (
        tile_pairs[:, :, None] == jnp.arange(tile_count, dtype=jnp.int32)[None, None, :]
    ).astype(jnp.float32)
    grad_key = jnp.einsum(
        "anb,antd->btd",
        owners,
        grad_key_near.reshape(tile_count, neighbours, tile_rows, head_width),
        precision=lax.Precision.HIGHEST,
    ).astype(jnp.bfloat16)
    grad_value = jnp.einsum(
        "anb,antd->btd",
        owners,
        grad_value_near.reshape(tile_count, neighbours, tile_rows, head_width),
        precision=lax.Precision.HIGHEST,
    ).astype(jnp.bfloat16)
    return (attended, grad_query, grad_key, grad_value)


def per_device(queries, keys, values, gain_q, gain_k, tile_pairs, tile_lens, out_grad, w_out):
    seq_count = lax.axis_size("seq")
    dp_count = lax.axis_size("dp")
    tok_rows = queries.shape[0]
    width = queries.shape[1]
    local_width = width // seq_count
    clip_rows = tok_rows * seq_count
    tile_count = tile_pairs.shape[0]
    tile_rows = clip_rows // tile_count
    head_count = local_width // HEAD_DIM
    clip_lengths = tile_lens[0]
    query_normed, query_scale = normalize(queries, gain_q)
    key_normed, key_scale = normalize(keys, gain_k)
    query_heads, key_heads, value_heads = (
        lax.all_to_all(query_normed, "seq", split_axis=1, concat_axis=0, tiled=True),
        lax.all_to_all(key_normed, "seq", split_axis=1, concat_axis=0, tiled=True),
        lax.all_to_all(values, "seq", split_axis=1, concat_axis=0, tiled=True),
    )
    cot_all = lax.all_gather(out_grad, "seq", axis=0, tiled=True)
    columns = cot_all
    grad_attended = jnp.dot(
        columns, lax.all_gather(w_out, "dp", axis=0, tiled=True), preferred_element_type=jnp.float32
    ).astype(jnp.bfloat16)

    def split(field):
        return field.reshape(tile_count, tile_rows, head_count, HEAD_DIM).transpose(2, 0, 1, 3)

    def merge(field):
        return field.transpose(1, 2, 0, 3).reshape(clip_rows, local_width)

    def one_head(group):
        return tile_attention(group[0], group[1], group[2], group[3], tile_pairs, clip_lengths)

    attended, grad_qn, grad_kn, grad_vh = lax.map(
        one_head, (split(query_heads), split(key_heads), split(value_heads), split(grad_attended))
    )
    attended = merge(attended)
    grad_qn = merge(grad_qn)
    grad_kn = merge(grad_kn)
    grad_vh = merge(grad_vh)
    columns = cot_all
    grad_w = lax.psum_scatter(
        (
            jnp.einsum("td,te->de", columns, attended, preferred_element_type=jnp.float32)
            / dp_count
        ).astype(jnp.bfloat16),
        "dp",
        scatter_dimension=0,
        tiled=True,
    ).astype(jnp.float32)
    grad_qt, grad_kt, grad_v = (
        lax.all_to_all(grad_qn, "seq", split_axis=0, concat_axis=1, tiled=True),
        lax.all_to_all(grad_kn, "seq", split_axis=0, concat_axis=1, tiled=True),
        lax.all_to_all(grad_vh, "seq", split_axis=0, concat_axis=1, tiled=True),
    )
    query_full = queries.astype(jnp.float32)
    key_full = keys.astype(jnp.float32)
    gated_q = gain_q * grad_qt.astype(jnp.float32)
    gated_k = gain_k * grad_kt.astype(jnp.float32)
    inner_q = jnp.sum(gated_q * query_full, axis=-1, keepdims=True)
    inner_k = jnp.sum(gated_k * key_full, axis=-1, keepdims=True)
    grad_q = norm_finish(query_full, query_scale, gated_q, inner_q, width)
    grad_k = norm_finish(key_full, key_scale, gated_k, inner_k, width)
    return (grad_q, grad_k, grad_v, grad_w)


def solution(mesh):
    return jax.shard_map(
        per_device,
        mesh=mesh,
        in_specs=(
            P(("dp", "seq"), None),
            P(("dp", "seq"), None),
            P(("dp", "seq"), None),
            P(),
            P(),
            P(),
            P("dp", None),
            P(("dp", "seq"), None),
            P("dp", "seq"),
        ),
        out_specs=(
            P(("dp", "seq"), None),
            P(("dp", "seq"), None),
            P(("dp", "seq"), None),
            P("dp", "seq"),
        ),
        check_vma=False,
    )
```

profile of v0, /device:TPU:0, one launch (start us, length us, event | category | flops | bytes accessed | tf_op | source)
XLA Modules:
  0.0 541.2 jit_solution(65529981299238920)
XLA Ops:
  12.3 4.2 all-to-all-start
  20.6 2.5 copy.75
  23.1 10.7 %all-to-all-done = bf16[256,4,640]{2,0,1:T(8,128)(2,1)S(1)} async-done(((bf16[256,4,640]{2,0,1:T(8,128)(2,1)}), bf16[256,4,640]{2,0,1:T(8,128)(2,1)S(1)}, u32[]{:S(2)}, u32[]{:S(2)}) %all-to-all-start) | async-done | bytes 1310752 | tf_op jit(solution)/shard_map/all_to_all | solution.py:87
  33.8 3.5 all-to-all-start.1
  37.4 2.5 copy.126
  39.9 14.7 %all-to-all-done.1 = bf16[256,4,640]{2,0,1:T(8,128)(2,1)S(1)} async-done(((bf16[256,4,640]{2,0,1:T(8,128)(2,1)}), bf16[256,4,640]{2,0,1:T(8,128)(2,1)S(1)}, u32[]{:S(2)}, u32[]{:S(2)}) %all-to-all-start.1) | async-done | bytes 1310752 | tf_op jit(solution)/shard_map/all_to_all | solution.py:88
  54.6 4.4 all-to-all-start.2
  62.5 3.1 reshape.159
  67.1 9.3 %all-to-all-done.2 = bf16[256,4,640]{2,0,1:T(8,128)(2,1)} async-done(((bf16[256,4,640]{2,0,1:T(8,128)(2,1)}), bf16[256,4,640]{2,0,1:T(8,128)(2,1)}, u32[]{:S(2)}, u32[]{:S(2)}) %all-to-all-start.2) | async-done | bytes 1310752 | tf_op jit(solution)/shard_map/all_to_all | solution.py:89
  76.4 3.1 reshape.160
  80.9 34.3 %all-gather.5.cloned.1.call-done = bf16[5120,640]{1,0:T(8,128)(2,1)} async-done(((bf16[640,640]{1,0:T(8,128)(2,1)}), bf16[5120,640]{1,0:T(8,128)(2,1)}) %all-gather.5.cloned.1.call-update) | async-done | bytes 6553616 | tf_op jit(solution)/shard_map/all_gather | solution.py:94
  115.2 69.9 %all-gather.3.cloned.1.call-done = bf16[1024,5120]{1,0:T(8,128)(2,1)} async-done(((bf16[256,5120]{1,0:T(8,128)(2,1)}), bf16[1024,5120]{1,0:T(8,128)(2,1)}) %all-gather.3.cloned.1.call-update) | async-done | bytes 10485776 | tf_op jit(solution)/shard_map/all_gather | solution.py:91
  185.1 13.7 %convolution_convert_fusion.1 = bf16[1024,640]{1,0:T(8,128)(2,1)} fusion(bf16[1024,5120]{1,0:T(8,128)(2,1)} %all-gather.3.cloned.1.call-done, bf16[5120,640]{1,0:T(8,128)(2,1)} %all-gather.5.cloned.1.call-done), kind=kOutput, calls=%fused_computation.95 | convolution fusion | flops 6711541760 | bytes 18350080 | tf_op jit(solution)/shard_map/dot_general | solution.py:93
  198.9 3.1 reshape.161
  203.4 182.2 %while.18 = (s32[]{:T(128)}, bf16[5,16,64,128]{3,2,1,0:T(8,128)(2,1)}, bf16[5,16,64,128]{3,2,1,0:T(8,128)(2,1)}, bf16[5,16,64,128]{3,1,2,0:T(8,128)(2,1)}, bf16[...) while((s32[]{:T(128)}, ...), condition=%wide.region_6.8_spmd, body=%wide.region_2.7_spmd.sunk | while | flops 1219638656 | bytes 88276472 | solution.py:106
  209.0 4.0 broadcast_select_fusion.6
  213.3 2.3 fusion.135
  215.6 3.6 fusion.136
  222.7 2.8 convolution_multiply_fusion.3
  225.6 7.3 %fusion.138 = bf16[5,16,64,128]{3,1,2,0:T(8,128)(2,1)} fusion(bf16[5,16,64,128]{3,1,2,0:T(8,128)(2,1)} %get-tuple-element.341, s32[]{:T(128)S(6)} %copy.142, f32[16,8,64,128]{3,2,1,0:T(8,128)} %bitcast.172, s32[16,8]{0,1:T(8,128)S(1)} %copy.132), kind=kOutput, calls=%fused_computation.26.clone.1 | convolution fusion | flops 201459712 | bytes 4456964 | tf_op jit(solution)/shard_map/while/body/eval_jaxpr/anb,antd->btd/dot_general | solution.py:58
  234.8 5.2 fusion.140
  245.4 4.0 broadcast_select_fusion.6
  252.0 3.6 fusion.136
  259.1 2.8 convolution_multiply_fusion.3
  262.0 7.3 %fusion.138 = bf16[5,16,64,128]{3,1,2,0:T(8,128)(2,1)} fusion(bf16[5,16,64,128]{3,1,2,0:T(8,128)(2,1)} %get-tuple-element.341, s32[]{:T(128)S(6)} %copy.142, f32[16,8,64,128]{3,2,1,0:T(8,128)} %bitcast.172, s32[16,8]{0,1:T(8,128)S(1)} %copy.132), kind=kOutput, calls=%fused_computation.26.clone.1 | convolution fusion | flops 201459712 | bytes 4456964 | tf_op jit(solution)/shard_map/while/body/eval_jaxpr/anb,antd->btd/dot_general | solution.py:58
  271.2 5.2 fusion.140
  281.8 4.0 broadcast_select_fusion.6
  286.1 2.3 fusion.135
  288.4 3.6 fusion.136
  295.5 2.8 convolution_multiply_fusion.3
  298.4 7.3 %fusion.138 = bf16[5,16,64,128]{3,1,2,0:T(8,128)(2,1)} fusion(bf16[5,16,64,128]{3,1,2,0:T(8,128)(2,1)} %get-tuple-element.341, s32[]{:T(128)S(6)} %copy.142, f32[16,8,64,128]{3,2,1,0:T(8,128)} %bitcast.172, s32[16,8]{0,1:T(8,128)S(1)} %copy.132), kind=kOutput, calls=%fused_computation.26.clone.1 | convolution fusion | flops 201459712 | bytes 4456964 | tf_op jit(solution)/shard_map/while/body/eval_jaxpr/anb,antd->btd/dot_general | solution.py:58
  307.6 5.1 fusion.140
  318.2 4.0 broadcast_select_fusion.6
  324.7 3.6 fusion.136
  331.9 2.8 convolution_multiply_fusion.3
  334.8 7.3 %fusion.138 = bf16[5,16,64,128]{3,1,2,0:T(8,128)(2,1)} fusion(bf16[5,16,64,128]{3,1,2,0:T(8,128)(2,1)} %get-tuple-element.341, s32[]{:T(128)S(6)} %copy.142, f32[16,8,64,128]{3,2,1,0:T(8,128)} %bitcast.172, s32[16,8]{0,1:T(8,128)S(1)} %copy.132), kind=kOutput, calls=%fused_computation.26.clone.1 | convolution fusion | flops 201459712 | bytes 4456964 | tf_op jit(solution)/shard_map/while/body/eval_jaxpr/anb,antd->btd/dot_general | solution.py:58
  343.9 5.2 fusion.140
  354.5 4.0 broadcast_select_fusion.6
  358.8 2.3 fusion.135
  361.1 3.6 fusion.136
  368.3 2.8 convolution_multiply_fusion.3
  371.2 7.3 %fusion.138 = bf16[5,16,64,128]{3,1,2,0:T(8,128)(2,1)} fusion(bf16[5,16,64,128]{3,1,2,0:T(8,128)(2,1)} %get-tuple-element.341, s32[]{:T(128)S(6)} %copy.142, f32[16,8,64,128]{3,2,1,0:T(8,128)} %bitcast.172, s32[16,8]{0,1:T(8,128)S(1)} %copy.132), kind=kOutput, calls=%fused_computation.26.clone.1 | convolution fusion | flops 201459712 | bytes 4456964 | tf_op jit(solution)/shard_map/while/body/eval_jaxpr/anb,antd->btd/dot_general | solution.py:58
  380.3 5.2 fusion.140
  385.7 2.4 copy.90
  388.1 11.5 %fusion.68 = bf16[5120,640]{0,1:T(8,128)(2,1)} fusion(bf16[1024,5120]{1,0:T(8,128)(2,1)} %all-gather.3.cloned.1.call-done, bf16[128,8,5,128]{3,2,1,0:T(8,128)(2,1)S(1)} %bitcast.191), kind=kOutput, calls=%fused_computation.66 | convolution fusion | flops 6717440000 | bytes 18350080 | tf_op jit(solution)/shard_map/td,te->de/dot_general | solution.py:116
  399.6 9.5 %copy.97 = bf16[5120,640]{1,0:T(8,128)(2,1)} copy(bf16[5120,640]{0,1:T(8,128)(2,1)} %fusion.68) | data formatting | bytes 13107200
  411.4 2.4 all_to_all.79
  413.8 3.6 all-to-all-start.3
  419.8 2.4 all_to_all.81
  424.4 2.5 all_to_all.83
  426.9 7.8 %all-to-all-done.3 = bf16[4,256,640]{2,1,0:T(8,128)(2,1)S(1)} async-done(((bf16[4,256,640]{2,1,0:T(8,128)(2,1)}), bf16[4,256,640]{2,1,0:T(8,128)(2,1)S(1)}, u32[]{:S(2)}, u32[]{:S(2)}) %all-to-all-start.3) | async-done | bytes 1310752 | tf_op jit(solution)/shard_map/all_to_all | solution.py:124
  435.8 3.8 all-to-all-start.4
  439.6 3.1 convert_bitcast_fusion.1
  442.7 3.3 copy.85
  446.0 2.5 fusion.76
  450.5 2.4 copy.91
  452.9 3.9 all-to-all-done.4
  457.9 3.5 all-to-all-start.5
  461.4 3.0 convert_bitcast_fusion
  464.4 3.4 copy.87
  467.8 2.4 fusion.84
  472.2 2.4 copy.92
  474.6 4.0 all-to-all-done.5
  480.9 50.0 %reduce-scatter.4.cloned.1.call-done = bf16[640,640]{1,0:T(8,128)(2,1)} async-done(((bf16[5120,640]{1,0:T(8,128)(2,1)}), bf16[640,640]{1,0:T(8,128)(2,1)}) %reduce-scatter.4.cloned.1.call-update) | async-done | bytes 819216
  (200 shorter events, 95.9 us)
Async XLA Ops:
  7.2 52.2 %copy-start = (s32[1,16]{1,0:T(1,128)S(1)}, s32[1,16]{1,0:T(1,128)}, u32[]{:S(2)}) copy-start(s32[1,16]{1,0:T(1,128)} %param.19) | copy-start | bytes 196
  7.2 1.5 copy-start.14
  7.2 108.0 %all-gather.5.cloned.1.call-start = ((), (), s32[]{:S(2)}) async-start(), calls=%async_computation.8 | async-start | bytes 7372800 | tf_op jit(solution)/shard_map/all_gather | solution.py:94
  7.9 177.2 %all-gather.3.cloned.1.call-start = ((), (), s32[]{:S(2)}) async-start(), calls=%async_computation.7 | async-start | bytes 13107200 | tf_op jit(solution)/shard_map/all_gather | solution.py:91
  8.7 1.6 copy-start.16
  9.3 3.0 copy-start.7
  10.3 0.5 copy-start.23
  12.3 21.5 %all-to-all-start = ((bf16[256,4,640]{2,0,1:T(8,128)(2,1)}), bf16[256,4,640]{2,0,1:T(8,128)(2,1)S(1)}, u32[]{:S(2)}, u32[]{:S(2)}) async-start(bf16[256,4,640]{2,0,1:T(8,128)(2,1)} %copy.73), calls=%async_computation | async-start | bytes 2621440 | tf_op jit(solution)/shard_map/all_to_all | solution.py:87
  16.5 2.6 copy-start.18
  18.2 5.0 copy-start.5
  19.2 4.0 copy-start.21
  33.8 20.8 %all-to-all-start.1 = ((bf16[256,4,640]{2,0,1:T(8,128)(2,1)}), bf16[256,4,640]{2,0,1:T(8,128)(2,1)S(1)}, u32[]{:S(2)}, u32[]{:S(2)}) async-start(bf16[256,4,640]{2,0,1:T(8,128)(2,1)} %copy.75), calls=%async_computation.1 | async-start | bytes 2621440 | tf_op jit(solution)/shard_map/all_to_all | solution.py:88
  37.4 21.7 %copy-start.20 = (s32[16,8]{0,1:T(8,128)S(1)}, s32[16,8]{0,1:T(8,128)}, u32[]{:S(2)}) copy-start(s32[16,8]{0,1:T(8,128)} %param.18) | copy-start | bytes 1540
  54.6 6.0 %copy-start.11 = (bf16[256,4,640]{2,0,1:T(8,128)(2,1)}, bf16[256,4,640]{2,0,1:T(8,128)(2,1)S(1)}, u32[]{:S(2)}) copy-start(bf16[256,4,640]{2,0,1:T(8,128)(2,1)S(1)} %all-to-all-done.1) | copy-start | bytes 3932164
  54.6 21.7 %all-to-all-start.2 = ((bf16[256,4,640]{2,0,1:T(8,128)(2,1)}), bf16[256,4,640]{2,0,1:T(8,128)(2,1)}, u32[]{:S(2)}, u32[]{:S(2)}) async-start(bf16[256,4,640]{2,0,1:T(8,128)(2,1)} %bitcast.186), calls=%async_computation.2 | async-start | bytes 2621440 | tf_op jit(solution)/shard_map/all_to_all | solution.py:89
  59.0 471.9 %reduce-scatter.4.cloned.1.call-start = ((), (), s32[]{:S(2)}) async-start(), calls=%async_computation.9 | async-start | bytes 7372800
  215.6 3.6 copy-start.2
  215.6 3.6 copy-start.3
  225.6 7.3 %copy-start.4 = (f32[16,64,512]{2,1,0:T(8,128)S(1)}, f32[16,64,512]{2,1,0:T(8,128)}, u32[]{:S(2)}) copy-start(f32[16,64,512]{2,1,0:T(8,128)} %get-tuple-element.322) | copy-start | bytes 6291460 | tf_op jit(solution)/shard_map/while
  252.0 3.6 copy-start.2
  252.0 3.6 copy-start.3
  262.0 7.3 %copy-start.4 = (f32[16,64,512]{2,1,0:T(8,128)S(1)}, f32[16,64,512]{2,1,0:T(8,128)}, u32[]{:S(2)}) copy-start(f32[16,64,512]{2,1,0:T(8,128)} %get-tuple-element.322) | copy-start | bytes 6291460 | tf_op jit(solution)/shard_map/while
  288.4 3.6 copy-start.2
  288.4 3.6 copy-start.3
  298.4 7.3 %copy-start.4 = (f32[16,64,512]{2,1,0:T(8,128)S(1)}, f32[16,64,512]{2,1,0:T(8,128)}, u32[]{:S(2)}) copy-start(f32[16,64,512]{2,1,0:T(8,128)} %get-tuple-element.322) | copy-start | bytes 6291460 | tf_op jit(solution)/shard_map/while
  324.7 3.6 copy-start.2
  324.7 3.6 copy-start.3
  334.8 7.3 %copy-start.4 = (f32[16,64,512]{2,1,0:T(8,128)S(1)}, f32[16,64,512]{2,1,0:T(8,128)}, u32[]{:S(2)}) copy-start(f32[16,64,512]{2,1,0:T(8,128)} %get-tuple-element.322) | copy-start | bytes 6291460 | tf_op jit(solution)/shard_map/while
  361.1 3.6 copy-start.2
  361.1 3.6 copy-start.3
  371.1 7.3 %copy-start.4 = (f32[16,64,512]{2,1,0:T(8,128)S(1)}, f32[16,64,512]{2,1,0:T(8,128)}, u32[]{:S(2)}) copy-start(f32[16,64,512]{2,1,0:T(8,128)} %get-tuple-element.322) | copy-start | bytes 6291460 | tf_op jit(solution)/shard_map/while
  409.0 1.3 copy-start.15
  413.8 20.9 %all-to-all-start.3 = ((bf16[4,256,640]{2,1,0:T(8,128)(2,1)}), bf16[4,256,640]{2,1,0:T(8,128)(2,1)S(1)}, u32[]{:S(2)}, u32[]{:S(2)}) async-start(bf16[4,256,640]{2,1,0:T(8,128)(2,1)} %all_to_all.79), calls=%async_computation.3 | async-start | bytes 2621440 | tf_op jit(solution)/shard_map/all_to_all | solution.py:124
  434.7 1.1 copy-start.13
  435.8 21.0 %all-to-all-start.4 = ((bf16[4,256,640]{2,1,0:T(8,128)(2,1)}), bf16[4,256,640]{2,1,0:T(8,128)(2,1)S(1)}, u32[]{:S(2)}, u32[]{:S(2)}) async-start(bf16[4,256,640]{2,1,0:T(8,128)(2,1)} %all_to_all.81), calls=%async_computation.4 | async-start | bytes 2621440 | tf_op jit(solution)/shard_map/all_to_all | solution.py:125
  442.7 3.4 copy-start.8
  442.7 3.4 copy-start.17
  446.0 2.7 copy-start.9
  446.0 2.7 copy-start.24
  446.0 2.7 copy-start.26
  456.8 1.1 copy-start.12
  457.9 20.8 %all-to-all-start.5 = ((bf16[4,256,640]{2,1,0:T(8,128)(2,1)}), bf16[4,256,640]{2,1,0:T(8,128)(2,1)S(1)}, u32[]{:S(2)}, u32[]{:S(2)}) async-start(bf16[4,256,640]{2,1,0:T(8,128)(2,1)} %all_to_all.83), calls=%async_computation.5 | async-start | bytes 2621440 | tf_op jit(solution)/shard_map/all_to_all | solution.py:126
  464.4 3.4 copy-start.6
  464.4 3.4 copy-start.19
  467.8 2.6 copy-start.10
  467.8 2.6 copy-start.22
  467.8 2.6 copy-start.25
  479.3 55.0 %copy-start.1 = (s32[1,16]{1,0:T(1,128)S(1)}, s32[1,16]{1,0:T(1,128)}, u32[]{:S(2)}) copy-start(s32[1,16]{1,0:T(1,128)} %param.19) | copy-start | bytes 196
Sparse Core Ops, SparseCore 0:
  10.2 104.9 all-gather.4
  116.7 68.3 all-gather.2
  409.2 121.6 reduce-scatter.3
where the time goes:
time: 551 us; the launch traced here: 541 us
  waiting for transfers between devices  206 us (37%)
  matrix products  156 us (28%)
  local copies, waits for them, and re-layouts  100 us (18%)
  other arithmetic  40.5 us (7%)
  starting transfers between devices  23.3 us (4%)
  between operations  14.5 us (3%)
    all_gather x1, waiting for transfers between devices, per_device(): cot_all = lax.all_gather(out_grad, 'seq', axis=0, tiled=True)  69.9 us
    dot_general x25, matrix products, multiply(): return jnp.einsum(pattern, left, right, preferred_element_type=jnp.float32)  57.5 us
    unnamed x4, waiting for transfers between devices  51.4 us
    dot_general x5, matrix products, tile_attention(): jnp.einsum('anb,antd->btd', owners, grad_key_near.reshape(tile_count, nei...  36.3 us
    all_gather x1, waiting for transfers between devices, per_device(): lax.all_gather(w_out, 'dp', axis=0, tiled=True)  34.3 us
    dot_general x5, matrix products, tile_attention(): jnp.einsum('anb,antd->btd', owners, grad_value_near.reshape(tile_count, n...  25.8 us
    unnamed x56, local copies, waits for them, and re-layouts  25.5 us
    select_n x5, other arithmetic, tile_attention(): jnp.take(key_tiles, tile_pairs, axis=0)  20.2 us
  transfers between devices with their start and end apart: 9, of which 9 were waited for; matrix products, arithmetic and copies ran while one was open for 11% of the time, Pallas kernels for 0%

commit v1 on v0

v1 whole, which is shorter than its diff:
```python
import functools
import math

import jax
import jax.numpy as jnp
from jax import lax
from jax.experimental import pallas as pl
from jax.experimental.pallas import tpu as pltpu
from jax.sharding import PartitionSpec as P

HEAD_DIM = 128
BLOCK_Q = 256
EPS = 1e-06
DEAD = -1e30
VMEM_LIMIT = 48 * 1024 * 1024


def normalize(field, gain):
    values_f = field.astype(jnp.float32)
    row_scale = lax.rsqrt(jnp.mean(values_f * values_f, axis=-1, keepdims=True) + EPS)
    return ((values_f * row_scale * gain).astype(jnp.bfloat16), row_scale)


def norm_finish(values_f, row_scale, gated, inner, width):
    return (row_scale * gated - values_f * row_scale**3 * inner / width).astype(jnp.bfloat16)


def dot_nt(left, right):
    return lax.dot_general(
        left, right, (((1,), (1,)), ((), ())), preferred_element_type=jnp.float32
    )


def dot_nn(left, right):
    return jnp.dot(left, right, preferred_element_type=jnp.float32)


def forward_kernel(factor, q_ref, k_ref, v_ref, bias_ref, probs_ref, out_ref):
    scores = dot_nt(k_ref[...], q_ref[...]) * factor + bias_ref[...].astype(jnp.float32)
    weights = jnp.exp(scores - jnp.max(scores, axis=0, keepdims=True))
    probs = weights * (1.0 / jnp.sum(weights, axis=0, keepdims=True))
    probs_low = probs.astype(jnp.bfloat16)
    probs_ref[0] = probs_low
    attended = dot_nn(v_ref[...].T, probs_low)
    out_ref[...] = attended.T.astype(jnp.bfloat16)


def backward_kernel(
    factor, q_ref, k_ref, v_ref, g_ref, probs_ref, dq_ref, dk_ref, dv_ref, dk_sum, dv_sum
):
    block = pl.program_id(1)

    @pl.when(block == 0)
    def _():
        dk_sum[...] = jnp.zeros_like(dk_sum)
        dv_sum[...] = jnp.zeros_like(dv_sum)

    grad = g_ref[...]
    probs_low = probs_ref[0]
    dv_sum[...] += dot_nn(probs_low, grad)
    grad_probs = dot_nt(v_ref[...], grad)
    probs = probs_low.astype(jnp.float32)
    delta = jnp.sum(probs * grad_probs, axis=0, keepdims=True)
    grad_scores = (probs * (grad_probs - delta)).astype(jnp.bfloat16)
    dk_sum[...] += dot_nn(grad_scores, q_ref[...])
    dq_ref[...] = (dot_nn(k_ref[...].T, grad_scores) * factor).T.astype(jnp.bfloat16)

    @pl.when(block == pl.num_programs(1) - 1)
    def _():
        dk_ref[...] = (dk_sum[...] * factor).astype(jnp.bfloat16)
        dv_ref[...] = dv_sum[...].astype(jnp.bfloat16)


def attention_forward(query, key, value, bias):
    rows, width = query.shape
    heads = width // HEAD_DIM
    blocks = rows // BLOCK_Q
    by_query = pl.BlockSpec((BLOCK_Q, HEAD_DIM), lambda h, b: (b, h))
    by_key = pl.BlockSpec((rows, HEAD_DIM), lambda h, b: (0, h))
    pairs = heads * rows * rows
    return pl.pallas_call(
        functools.partial(forward_kernel, 1.0 / math.sqrt(HEAD_DIM)),
        grid=(heads, blocks),
        in_specs=[by_query, by_key, by_key, pl.BlockSpec((rows, BLOCK_Q), lambda h, b: (0, b))],
        out_specs=[pl.BlockSpec((1, rows, BLOCK_Q), lambda h, b: (h, 0, b)), by_query],
        out_shape=[
            jax.ShapeDtypeStruct((heads, rows, rows), jnp.bfloat16),
            jax.ShapeDtypeStruct((rows, width), jnp.bfloat16),
        ],
        compiler_params=pltpu.CompilerParams(vmem_limit_bytes=VMEM_LIMIT),
        cost_estimate=pl.CostEstimate(
            flops=4 * pairs * HEAD_DIM, bytes_accessed=4 * pairs, transcendentals=pairs
        ),
        name="attention_forward",
    )(query, key, value, bias)


def attention_backward(query, key, value, grad, probs):
    rows, width = query.shape
    heads = width // HEAD_DIM
    blocks = rows // BLOCK_Q
    by_query = pl.BlockSpec((BLOCK_Q, HEAD_DIM), lambda h, b: (b, h))
    by_key = pl.BlockSpec((rows, HEAD_DIM), lambda h, b: (0, h))
    pairs = heads * rows * rows
    shape = jax.ShapeDtypeStruct((rows, width), jnp.bfloat16)
    return pl.pallas_call(
        functools.partial(backward_kernel, 1.0 / math.sqrt(HEAD_DIM)),
        grid=(heads, blocks),
        in_specs=[
            by_query,
            by_key,
            by_key,
            by_query,
            pl.BlockSpec((1, rows, BLOCK_Q), lambda h, b: (h, 0, b)),
        ],
        out_specs=[by_query, by_key, by_key],
        out_shape=[shape, shape, shape],
        scratch_shapes=[
            pltpu.VMEM((rows, HEAD_DIM), jnp.float32),
            pltpu.VMEM((rows, HEAD_DIM), jnp.float32),
        ],
        compiler_params=pltpu.CompilerParams(vmem_limit_bytes=VMEM_LIMIT),
        cost_estimate=pl.CostEstimate(
            flops=8 * pairs * HEAD_DIM, bytes_accessed=4 * pairs, transcendentals=0
        ),
        name="attention_backward",
    )(query, key, value, grad, probs)


def score_bias(tile_pairs, clip_lengths, clip_rows):
    tile_count = tile_pairs.shape[0]
    tile_rows = clip_rows // tile_count
    tiles = jnp.arange(tile_count, dtype=jnp.int32)
    listed = jnp.any(tile_pairs[:, :, None] == tiles[None, None, :], axis=1)
    lengths = jnp.where(listed, clip_lengths[None, :], 0)
    live = jnp.arange(tile_rows, dtype=jnp.int32)[None, :, None] < lengths.T[:, None, :]
    bias = jnp.where(live, 0.0, DEAD).astype(jnp.bfloat16).reshape(clip_rows, tile_count)
    return jnp.repeat(bias, tile_rows, axis=1)


def per_device(queries, keys, values, gain_q, gain_k, tile_pairs, tile_lens, out_grad, w_out):
    dp_count = lax.axis_size("dp")
    width = queries.shape[1]
    clip_rows = queries.shape[0] * lax.axis_size("seq")
    w_all = lax.all_gather(w_out, "dp", axis=0, tiled=True)
    cot_all = lax.all_gather(out_grad, "seq", axis=0, tiled=True)
    query_normed, query_scale = normalize(queries, gain_q)
    key_normed, key_scale = normalize(keys, gain_k)
    query_heads, key_heads, value_heads = (
        lax.all_to_all(query_normed, "seq", split_axis=1, concat_axis=0, tiled=True),
        lax.all_to_all(key_normed, "seq", split_axis=1, concat_axis=0, tiled=True),
        lax.all_to_all(values, "seq", split_axis=1, concat_axis=0, tiled=True),
    )
    bias = score_bias(tile_pairs, tile_lens[0], clip_rows)
    probs, attended = attention_forward(query_heads, key_heads, value_heads, bias)
    partial_w = (
        lax.dot_general(
            cot_all, attended, (((0,), (0,)), ((), ())), preferred_element_type=jnp.float32
        )
        / dp_count
    ).astype(jnp.bfloat16)
    grad_w = lax.psum_scatter(partial_w, "dp", scatter_dimension=0, tiled=True)
    grad_attended = dot_nn(cot_all, w_all).astype(jnp.bfloat16)
    grad_qn, grad_kn, grad_vh = attention_backward(
        query_heads, key_heads, value_heads, grad_attended, probs
    )
    grad_qt, grad_kt, grad_v = (
        lax.all_to_all(grad_qn, "seq", split_axis=0, concat_axis=1, tiled=True),
        lax.all_to_all(grad_kn, "seq", split_axis=0, concat_axis=1, tiled=True),
        lax.all_to_all(grad_vh, "seq", split_axis=0, concat_axis=1, tiled=True),
    )
    query_full = queries.astype(jnp.float32)
    key_full = keys.astype(jnp.float32)
    gated_q = gain_q * grad_qt.astype(jnp.float32)
    gated_k = gain_k * grad_kt.astype(jnp.float32)
    inner_q = jnp.sum(gated_q * query_full, axis=-1, keepdims=True)
    inner_k = jnp.sum(gated_k * key_full, axis=-1, keepdims=True)
    grad_q = norm_finish(query_full, query_scale, gated_q, inner_q, width)
    grad_k = norm_finish(key_full, key_scale, gated_k, inner_k, width)
    return (grad_q, grad_k, grad_v, grad_w.astype(jnp.float32))


def solution(mesh):
    return jax.shard_map(
        per_device,
        mesh=mesh,
        in_specs=(
            P(("dp", "seq"), None),
            P(("dp", "seq"), None),
            P(("dp", "seq"), None),
            P(),
            P(),
            P(),
            P("dp", None),
            P(("dp", "seq"), None),
            P("dp", "seq"),
        ),
        out_specs=(
            P(("dp", "seq"), None),
            P(("dp", "seq"), None),
            P(("dp", "seq"), None),
            P("dp", "seq"),
        ),
        check_vma=False,
    )
```

time: 551 us -> 359 us (0.65); the launches traced: 541 us -> 357 us
  matrix products: 156 us -> 25.6 us
  local copies, waits for them, and re-layouts: 100 us -> 32.2 us
  Pallas kernels: 0 us -> 48.8 us
  blocking collectives: 0 us -> 40.2 us
  other arithmetic: 40.5 us -> 5.78 us
  waiting for transfers between devices: 206 us -> 174 us
  starting transfers between devices: 23.3 us -> 16.6 us
    dot_general x37 -> x2, matrix products: 145 us -> 25.6 us  [the longest x1 13.7 us: dot_nn(): return jnp.dot(left, right, preferred_element_type=jnp.float32)]
    all_gather x1, waiting for transfers between devices: 69.9 us -> 0.01 us  [per_device(): cot_all = lax.all_gather(out_grad, 'seq', axis=0, tiled=True)]
    pallas_call x0 -> x2, Pallas kernels: none -> 48.8 us  [the longest x1 25.5 us: attention_backward(): pl.pallas_call(functools.partial(backward_kernel, 1.0 / math.sqrt(HEAD_DI...]
    all_to_all x0 -> x2, blocking collectives: none -> 40.2 us  [the longest x1 20.4 us: per_device(): lax.all_to_all(grad_kn, 'seq', split_axis=0, concat_axis=1, tiled=True)]
    unnamed x4, waiting for transfers between devices: 51.4 us -> 15.7 us
    all_gather x1, waiting for transfers between devices: 34.3 us -> 66.5 us  [per_device(): w_all = lax.all_gather(w_out, 'dp', axis=0, tiled=True)]
    gather x12 -> x0, local copies, waits for them, and re-layouts: 22.6 us -> none  [the longest x5 10.7 us: tile_attention(): jnp.take(value_tiles, tile_pairs, axis=0)]
    select_n x11 -> x1, other arithmetic: 20.2 us -> 0.01 us  [score_bias(): lengths = jnp.where(listed, clip_lengths[None, :], 0)]
  transfers between devices with their start and end apart: 9 -> 7, of which waited for: 9 -> 6; matrix products, arithmetic and copies ran while one was open for 11% -> 16% of each run, Pallas kernels for 0% -> 14%
where the time goes in v1:
time: 359 us; the launch traced here: 357 us
  waiting for transfers between devices  174 us (48%)
  Pallas kernels  48.8 us (14%)
  blocking collectives  40.2 us (11%)
  local copies, waits for them, and re-layouts  32.2 us (9%)
  matrix products  25.6 us (7%)
  starting transfers between devices  16.6 us (5%)
  between operations  13.9 us (4%)
  other arithmetic  5.78 us (2%)
    all_gather x1, waiting for transfers between devices, per_device(): w_all = lax.all_gather(w_out, 'dp', axis=0, tiled=True)  66.5 us
    all_to_all x1, waiting for transfers between devices, per_device(): lax.all_to_all(key_normed, 'seq', split_axis=1, concat_axis=0, tiled=True)  29.1 us
    all_to_all x1, waiting for transfers between devices, per_device(): lax.all_to_all(values, 'seq', split_axis=1, concat_axis=0, tiled=True)  25.6 us
    pallas_call x1, Pallas kernels, attention_backward(): pl.pallas_call(functools.partial(backward_kernel, 1.0 / math.sqrt(HEAD_DI...  25.5 us
    all_to_all x1, waiting for transfers between devices, per_device(): lax.all_to_all(query_normed, 'seq', split_axis=1, concat_axis=0, tiled=True)  23.7 us
    pallas_call x1, Pallas kernels, attention_forward(): pl.pallas_call(functools.partial(forward_kernel, 1.0 / math.sqrt(HEAD_DIM...  23.3 us
    all_to_all x1, blocking collectives, per_device(): lax.all_to_all(grad_kn, 'seq', split_axis=0, concat_axis=1, tiled=True)  20.4 us
    all_to_all x1, blocking collectives, per_device(): lax.all_to_all(grad_qn, 'seq', split_axis=0, concat_axis=1, tiled=True)  19.8 us
  transfers between devices with their start and end apart: 7, of which 6 were waited for; matrix products, arithmetic and copies ran while one was open for 16% of the time, Pallas kernels for 14%

profile of v1, /device:TPU:0, one launch (start us, length us, event | category | flops | bytes accessed | tf_op | source)
XLA Modules:
  0.0 357.5 jit_solution(4488643792264738083)
XLA Ops:
  7.2 0.0 copy-start.3
  7.2 0.0 copy-start.8
  7.2 0.0 all-gather.3.cloned.1.call-start
  7.2 0.7 all-gather.3.cloned.1.call-update
  7.9 0.0 all-gather.5.cloned.1.call-start
  8.0 0.7 all-gather.5.cloned.1.call-update
  8.7 0.0 copy-done.3
  8.7 0.3 fusion.1
  9.0 0.0 copy-done.8
  9.0 0.4 fusion.3
  9.4 0.0 copy-start.5
  9.4 1.2 copy.61
  10.6 4.4 %all-to-all-start = ((bf16[256,4,640]{2,0,1:T(8,128)(2,1)}), bf16[256,4,640]{2,0,1:T(8,128)(2,1)S(1)}, u32[]{:S(2)}, u32[]{:S(2)}) async-start(bf16[256,4,640]{2,0,1:T(8,128)(2,1)} %bitcast.60), calls=%async_computation | async-start | bytes 2621440 | tf_op jit(solution)/shard_map/all_to_all | solution.py:150
  15.0 0.0 copy-done.5
  15.0 0.3 fusion.9
  15.3 0.0 copy-done.9
  15.3 0.4 fusion.11
  15.7 1.2 copy.60
  16.9 23.7 %all-to-all-done = bf16[256,4,640]{2,0,1:T(8,128)(2,1)S(1)} async-done(((bf16[256,4,640]{2,0,1:T(8,128)(2,1)}), bf16[256,4,640]{2,0,1:T(8,128)(2,1)S(1)}, u32[]{:S(2)}, u32[]{:S(2)}) %all-to-all-start) | async-done | bytes 1310752 | tf_op jit(solution)/shard_map/all_to_all | solution.py:150
  40.6 3.5 all-to-all-start.1
  44.2 0.0 copy-start.10
  44.2 0.0 copy-start.11
  44.2 2.5 copy.59
  46.7 29.1 %all-to-all-done.1 = bf16[256,4,640]{2,0,1:T(8,128)(2,1)S(1)} async-done(((bf16[256,4,640]{2,0,1:T(8,128)(2,1)}), bf16[256,4,640]{2,0,1:T(8,128)(2,1)S(1)}, u32[]{:S(2)}, u32[]{:S(2)}) %all-to-all-start.1) | async-done | bytes 1310752 | tf_op jit(solution)/shard_map/all_to_all | solution.py:151
  75.8 4.3 %all-to-all-start.2 = ((bf16[256,4,640]{2,0,1:T(8,128)(2,1)}), bf16[256,4,640]{2,0,1:T(8,128)(2,1)}, u32[]{:S(2)}, u32[]{:S(2)}) async-start(bf16[256,4,640]{2,0,1:T(8,128)(2,1)} %bitcast.59), calls=%async_computation.2 | async-start | bytes 2621440 | tf_op jit(solution)/shard_map/all_to_all | solution.py:152
  80.1 0.0 reduce-scatter.4.cloned.1.call-start
  80.1 0.0 copy-done.10
  80.1 0.1 copy.42
  80.2 0.1 fusion.17
  80.3 0.0 copy-done.11
  80.3 0.1 lt.23
  80.4 0.1 lt.24
  80.6 0.1 lt.21
  80.6 1.6 broadcast_in_dim.42
  82.3 4.0 %copy.43.bias_ref = bf16[1024,1024]{1,0:T(8,128)(2,1)} copy(bf16[1024,1024]{0,1:T(8,128)(2,1)} %bitcast.58) | data formatting | bytes 4194304 | tf_op jit(solution)/shard_map/reshape | solution.py:138
  86.2 25.6 %all-to-all-done.2 = bf16[256,4,640]{2,0,1:T(8,128)(2,1)} async-done(((bf16[256,4,640]{2,0,1:T(8,128)(2,1)}), bf16[256,4,640]{2,0,1:T(8,128)(2,1)}, u32[]{:S(2)}, u32[]{:S(2)}) %all-to-all-start.2) | async-done | bytes 1310752 | tf_op jit(solution)/shard_map/all_to_all | solution.py:152
  111.8 0.0 copy-done
  111.8 23.3 %attention_forward.1 = (bf16[5,1024,1024]{2,1,0:T(8,128)(2,1)}, bf16[1024,640]{1,0:T(8,128)(2,1)S(1)}) custom-call(bf16[1024,640]{1,0:T(8,128)(2,1)S(1)} %bitcast.48, bf16[1024,640]{1,0:T(8,128)(2,1)S(1)} %bitcast.50, bf16[1024,640]{1,0:T(8,128)(2,1)} %bitcast.5.v_ref, bf16[1024,1024]{1,0:T(8,128)(2,1)} %copy.43.bias_ref), custom_call_target="tpu_custom_call" | custom-call | flops 2684354560 | bytes 20971520 | tf_op jit(solution)/shard_map/attention_forward/pallas_call | solution.py:81
  135.1 1.1 copy-done.1
  136.1 11.9 %fusion = bf16[5120,640]{0,1:T(8,128)(2,1)} fusion(bf16[1024,640]{1,0:T(8,128)(2,1)} %copy-done.1, bf16[1024,5120]{1,0:T(8,128)(2,1)} %all-gather.3.cloned.1.call-done), kind=kOutput, calls=%fused_computation.1 | convolution fusion | flops 6717440000 | bytes 18350080 | tf_op jit(solution)/shard_map/dot_general | solution.py:157
  148.1 9.6 %copy.48 = bf16[5120,640]{1,0:T(8,128)(2,1)} copy(bf16[5120,640]{0,1:T(8,128)(2,1)} %fusion) | data formatting | bytes 13107200
  157.6 0.0 reduce-scatter.4.cloned.1.call-update
  157.6 66.5 %all-gather.5.cloned.1.call-done = bf16[5120,640]{1,0:T(8,128)(2,1)} async-done(((bf16[640,640]{1,0:T(8,128)(2,1)}), bf16[5120,640]{1,0:T(8,128)(2,1)}) %all-gather.5.cloned.1.call-update) | async-done | bytes 6553616 | tf_op jit(solution)/shard_map/all_gather | solution.py:145
  224.1 13.7 %convolution_convert_fusion.g_ref = bf16[1024,640]{1,0:T(8,128)(2,1)} fusion(bf16[1024,5120]{1,0:T(8,128)(2,1)} %all-gather.3.cloned.1.call-done, bf16[5120,640]{1,0:T(8,128)(2,1)} %all-gather.5.cloned.1.call-done), kind=kOutput, calls=%fused_computation.28 | convolution fusion | flops 6711541760 | bytes 18350080 | tf_op jit(solution)/shard_map/dot_general | solution.py:35
  237.8 25.5 %attention_backward.1 = (bf16[1024,640]{1,0:T(8,128)(2,1)S(1)}, bf16[1024,640]{1,0:T(8,128)(2,1)S(1)}, bf16[1024,640]{1,0:T(8,128)(2,1)}) custom-call(bf16[1024,640]{1,0:T(8,128)(2,1)S(1)} %bitcast.49, bf16[1024,640]{1,0:T(8,128)(2,1)} %bitcast.51, bf16[1024,640]{1,0:T(8,128)(2,1)} %bitcast.5.v_ref, bf16[1024,640]{1,0:T(8,128)(2,1)} %convolution_convert_fusion.g_ref, ...), custom_call_target="tpu_custom_call" | custom-call | flops 5368709120 | bytes 20971520 | tf_op jit(solution)/shard_map/attention_backward/pallas_call | solution.py:106
  263.3 19.8 %all_to_all.102 = bf16[4,256,640]{2,1,0:T(8,128)(2,1)S(1)} all-to-all(bf16[4,256,640]{2,1,0:T(8,128)(2,1)S(1)} %bitcast.53), channel_id=1, replica_groups=mesh['dp'=8,'seq'=4] {'seq'}, dimensions={0} | all-to-all | bytes 2621440 | tf_op jit(solution)/shard_map/all_to_all | solution.py:168
  283.1 20.4 %all_to_all.103 = bf16[4,256,640]{2,1,0:T(8,128)(2,1)} all-to-all(bf16[4,256,640]{2,1,0:T(8,128)(2,1)S(1)} %bitcast.52), channel_id=1, replica_groups=mesh['dp'=8,'seq'=4] {'seq'}, dimensions={0} | all-to-all | bytes 2621440 | tf_op jit(solution)/shard_map/all_to_all | solution.py:169
  303.5 4.3 %all-to-all-start.5 = ((bf16[4,256,640]{2,1,0:T(8,128)(2,1)}), bf16[4,256,640]{2,1,0:T(8,128)(2,1)}, u32[]{:S(2)}, u32[]{:S(2)}) async-start(bf16[4,256,640]{2,1,0:T(8,128)(2,1)} %bitcast.16), calls=%async_computation.5 | async-start | bytes 2621440 | tf_op jit(solution)/shard_map/all_to_all | solution.py:170
  307.9 0.2 convert_bitcast_fusion.1
  308.0 0.0 copy-start.7
  308.0 0.3 copy.53
  308.4 1.0 copy-done.7
  309.4 0.2 convert_bitcast_fusion
  309.6 1.8 copy.54
  311.4 13.8 %all-to-all-done.5 = bf16[4,256,640]{2,1,0:T(8,128)(2,1)} async-done(((bf16[4,256,640]{2,1,0:T(8,128)(2,1)}), bf16[4,256,640]{2,1,0:T(8,128)(2,1)}, u32[]{:S(2)}, u32[]{:S(2)}) %all-to-all-start.5) | async-done | bytes 1310752 | tf_op jit(solution)/shard_map/all_to_all | solution.py:170
  325.2 2.6 copy.55
  327.8 0.5 fusion.8
  328.3 1.3 copy-done.2
  329.6 0.4 copy-done.6
  329.9 0.4 fusion.16
  330.4 3.0 fusion.7
  333.3 14.3 %reduce-scatter.4.cloned.1.call-done = bf16[640,640]{1,0:T(8,128)(2,1)} async-done(((bf16[5120,640]{1,0:T(8,128)(2,1)}), bf16[640,640]{1,0:T(8,128)(2,1)}) %reduce-scatter.4.cloned.1.call-update) | async-done | bytes 819216
  347.6 1.8 copy.49
  349.4 1.5 copy.47
  (13 shorter events, 0.1 us)
Async XLA Ops:
  7.2 1.5 copy-start.3
  7.2 1.9 copy-start.8
  7.2 128.9 %all-gather.3.cloned.1.call-start = ((), (), s32[]{:S(2)}) async-start(), calls=%async_computation.7 | async-start | bytes 13107200 | tf_op jit(solution)/shard_map/all_gather | solution.py:146
  7.9 216.2 %all-gather.5.cloned.1.call-start = ((), (), s32[]{:S(2)}) async-start(), calls=%async_computation.8 | async-start | bytes 7372800 | tf_op jit(solution)/shard_map/all_gather | solution.py:145
  9.4 5.6 %copy-start.5 = (bf16[256,2560]{1,0:T(8,128)(2,1)S(1)}, bf16[256,2560]{1,0:T(8,128)(2,1)}, u32[]{:S(2)}) copy-start(bf16[256,2560]{1,0:T(8,128)(2,1)} %param.10) | copy-start | bytes 3932164
  10.6 4.7 %copy-start.9 = (f32[2560]{0:T(1024)S(1)}, f32[2560]{0:T(1024)}, u32[]{:S(2)}) copy-start(f32[2560]{0:T(1024)} %param.13) | copy-start | bytes 30724
  10.6 30.0 %all-to-all-start = ((bf16[256,4,640]{2,0,1:T(8,128)(2,1)}), bf16[256,4,640]{2,0,1:T(8,128)(2,1)S(1)}, u32[]{:S(2)}, u32[]{:S(2)}) async-start(bf16[256,4,640]{2,0,1:T(8,128)(2,1)} %bitcast.60), calls=%async_computation | async-start | bytes 2621440 | tf_op jit(solution)/shard_map/all_to_all | solution.py:150
  40.6 35.2 %all-to-all-start.1 = ((bf16[256,4,640]{2,0,1:T(8,128)(2,1)}), bf16[256,4,640]{2,0,1:T(8,128)(2,1)S(1)}, u32[]{:S(2)}, u32[]{:S(2)}) async-start(bf16[256,4,640]{2,0,1:T(8,128)(2,1)} %bitcast.61), calls=%async_computation.1 | async-start | bytes 2621440 | tf_op jit(solution)/shard_map/all_to_all | solution.py:151
  44.2 36.0 %copy-start.10 = (s32[16,8]{0,1:T(8,128)S(1)}, s32[16,8]{0,1:T(8,128)}, u32[]{:S(2)}) copy-start(s32[16,8]{0,1:T(8,128)} %param.14) | copy-start | bytes 1540
  44.2 36.1 %copy-start.11 = (s32[1,16]{1,0:T(1,128)S(1)}, s32[1,16]{1,0:T(1,128)}, u32[]{:S(2)}) copy-start(s32[1,16]{1,0:T(1,128)} %param.15) | copy-start | bytes 196
  75.8 36.0 %copy-start = (bf16[256,4,640]{2,0,1:T(8,128)(2,1)}, bf16[256,4,640]{2,0,1:T(8,128)(2,1)S(1)}, u32[]{:S(2)}) copy-start(bf16[256,4,640]{2,0,1:T(8,128)(2,1)S(1)} %all-to-all-done.1) | copy-start | bytes 3932164
  75.8 36.0 %all-to-all-start.2 = ((bf16[256,4,640]{2,0,1:T(8,128)(2,1)}), bf16[256,4,640]{2,0,1:T(8,128)(2,1)}, u32[]{:S(2)}, u32[]{:S(2)}) async-start(bf16[256,4,640]{2,0,1:T(8,128)(2,1)} %bitcast.59), calls=%async_computation.2 | async-start | bytes 2621440 | tf_op jit(solution)/shard_map/all_to_all | solution.py:152
  80.1 267.5 %reduce-scatter.4.cloned.1.call-start = ((), (), s32[]{:S(2)}) async-start(), calls=%async_computation.9 | async-start | bytes 7372800
  135.1 1.1 copy-start.1
  303.5 21.7 %all-to-all-start.5 = ((bf16[4,256,640]{2,1,0:T(8,128)(2,1)}), bf16[4,256,640]{2,1,0:T(8,128)(2,1)}, u32[]{:S(2)}, u32[]{:S(2)}) async-start(bf16[4,256,640]{2,1,0:T(8,128)(2,1)} %bitcast.16), calls=%async_computation.5 | async-start | bytes 2621440 | tf_op jit(solution)/shard_map/all_to_all | solution.py:170
  308.0 1.4 copy-start.7
  325.2 2.6 copy-start.4
  327.8 1.8 copy-start.2
  327.8 2.1 copy-start.6
Sparse Core Ops, SparseCore 0:
  9.6 108.7 all-gather.2
  120.6 103.4 all-gather.4
  227.7 119.8 reduce-scatter.3

commit v2 on v1

v2 whole, which is shorter than its diff:
```python
import functools
import math

import jax
import jax.numpy as jnp
from jax import lax
from jax.experimental import pallas as pl
from jax.experimental.pallas import tpu as pltpu
from jax.sharding import PartitionSpec as P

HEAD_DIM = 128
ROW_BLOCK = 64
EPS = 1e-06
DEAD = -1e30
VMEM_LIMIT = 48 * 1024 * 1024


def dot_nt(left, right):
    return lax.dot_general(
        left, right, (((1,), (1,)), ((), ())), preferred_element_type=jnp.float32
    )


def dot_tn(left, right):
    return lax.dot_general(
        left, right, (((0,), (0,)), ((), ())), preferred_element_type=jnp.float32
    )


def dot_nn(left, right):
    return jnp.dot(left, right, preferred_element_type=jnp.float32)


def columns_of(owner, width):
    return pl.ds(pl.multiple_of(owner * width, HEAD_DIM), width)


def prepare_kernel(me_ref, q_ref, k_ref, v_ref, gain_q_ref, gain_k_ref, *rest):
    sends, held = rest[:-1], rest[-1]
    for which, (field_ref, gain_ref) in enumerate(((q_ref, gain_q_ref), (k_ref, gain_k_ref))):
        values_f = field_ref[...].astype(jnp.float32)
        row_scale = lax.rsqrt(jnp.mean(values_f * values_f, axis=-1, keepdims=True) + EPS)
        held[which] = (values_f * row_scale * gain_ref[...]).astype(jnp.bfloat16)
    held[2] = v_ref[...]
    for step, send_ref in enumerate(sends):
        part = columns_of(me_ref[0] ^ step, send_ref.shape[2])
        for which in range(3):
            send_ref[which] = held[which, :, part]


def prepare(me, queries, keys, values, gain_q, gain_k, peers):
    rows, width = queries.shape
    part = width // peers
    by_row = pl.BlockSpec((ROW_BLOCK, width), lambda i, me: (i, 0))
    gain = pl.BlockSpec((1, width), lambda i, me: (0, 0))
    return pl.pallas_call(
        prepare_kernel,
        grid_spec=pltpu.PrefetchScalarGridSpec(
            num_scalar_prefetch=1,
            grid=(rows // ROW_BLOCK,),
            in_specs=[by_row, by_row, by_row, gain, gain],
            out_specs=[pl.BlockSpec((3, ROW_BLOCK, part), lambda i, me: (0, i, 0))] * peers,
            scratch_shapes=[pltpu.VMEM((3, ROW_BLOCK, width), jnp.bfloat16)],
        ),
        out_shape=[jax.ShapeDtypeStruct((3, rows, part), jnp.bfloat16)] * peers,
        compiler_params=pltpu.CompilerParams(vmem_limit_bytes=VMEM_LIMIT),
        name="prepare",
    )(me, queries, keys, values, gain_q[None], gain_k[None])


def finish_kernel(me_ref, q_ref, k_ref, gain_q_ref, gain_k_ref, *rest):
    parts, (dq_ref, dk_ref, dv_ref, held) = rest[:-4], rest[-4:]
    for step, part_ref in enumerate(parts):
        part = columns_of(me_ref[0] ^ step, part_ref.shape[2])
        held[0, :, part] = part_ref[0]
        held[1, :, part] = part_ref[1]
        dv_ref[:, part] = part_ref[2]
    for which, (field_ref, gain_ref, out_ref) in enumerate(
        ((q_ref, gain_q_ref, dq_ref), (k_ref, gain_k_ref, dk_ref))
    ):
        values_f = field_ref[...].astype(jnp.float32)
        width = values_f.shape[1]
        row_scale = lax.rsqrt(jnp.mean(values_f * values_f, axis=-1, keepdims=True) + EPS)
        gated = gain_ref[...] * held[which].astype(jnp.float32)
        inner = jnp.sum(gated * values_f, axis=-1, keepdims=True)
        out_ref[...] = (
            row_scale * gated - values_f * (row_scale * row_scale * row_scale * inner / width)
        ).astype(jnp.bfloat16)


def finish(me, queries, keys, gain_q, gain_k, parts):
    rows, width = queries.shape
    part = width // len(parts)
    by_row = pl.BlockSpec((ROW_BLOCK, width), lambda i, me: (i, 0))
    gain = pl.BlockSpec((1, width), lambda i, me: (0, 0))
    return pl.pallas_call(
        finish_kernel,
        grid_spec=pltpu.PrefetchScalarGridSpec(
            num_scalar_prefetch=1,
            grid=(rows // ROW_BLOCK,),
            in_specs=[by_row, by_row, gain, gain]
            + [pl.BlockSpec((3, ROW_BLOCK, part), lambda i, me: (0, i, 0))] * len(parts),
            out_specs=[by_row] * 3,
            scratch_shapes=[pltpu.VMEM((2, ROW_BLOCK, width), jnp.bfloat16)],
        ),
        out_shape=[jax.ShapeDtypeStruct((rows, width), jnp.bfloat16)] * 3,
        compiler_params=pltpu.CompilerParams(vmem_limit_bytes=VMEM_LIMIT),
        name="finish",
    )(me, queries, keys, gain_q[None], gain_k[None], *parts)


def forward_kernel(factor, *refs):
    parts, (bias_ref, probs_ref, out_ref) = refs[:-3], refs[-3:]
    rows = parts[0].shape[1]
    key = jnp.concatenate([part[1] for part in parts], axis=0)
    value_t = jnp.concatenate([part[2] for part in parts], axis=0).T
    for block, part in enumerate(parts):
        at = pl.ds(block * rows, rows)
        scores = dot_nt(key, part[0]) * factor + bias_ref[:, at].astype(jnp.float32)
        weights = jnp.exp(scores - jnp.max(scores, axis=0, keepdims=True))
        probs = weights * (1.0 / jnp.sum(weights, axis=0, keepdims=True))
        probs_low = probs.astype(jnp.bfloat16)
        probs_ref[0, :, at] = probs_low
        out_ref[at, :] = dot_nn(value_t, probs_low).T.astype(jnp.bfloat16)


def backward_kernel(factor, peers, *refs):
    parts, grads, probs_ref = refs[:peers], refs[peers : 2 * peers], refs[2 * peers]
    outs = refs[2 * peers + 1 : 3 * peers + 1]
    dk_sum, dv_sum = refs[3 * peers + 1 :]
    rows = parts[0].shape[1]
    key_t = jnp.concatenate([part[1] for part in parts], axis=0).T
    value = jnp.concatenate([part[2] for part in parts], axis=0)
    for block in range(peers):
        at = pl.ds(block * rows, rows)
        grad = grads[block][...]
        probs_low = probs_ref[0, :, at]
        grad_probs = dot_nt(value, grad)
        probs = probs_low.astype(jnp.float32)
        delta = jnp.sum(probs * grad_probs, axis=0, keepdims=True)
        grad_scores = (probs * (grad_probs - delta)).astype(jnp.bfloat16)
        dv_part = dot_nn(probs_low, grad)
        dk_part = dot_nn(grad_scores, parts[block][0])
        if block == 0:
            dv_sum[...] = dv_part
            dk_sum[...] = dk_part
        else:
            dv_sum[...] += dv_part
            dk_sum[...] += dk_part
        outs[block][0] = (dot_nn(key_t, grad_scores) * factor).T.astype(jnp.bfloat16)
    for block in range(peers):
        at = pl.ds(block * rows, rows)
        outs[block][1] = (dk_sum[at, :] * factor).astype(jnp.bfloat16)
        outs[block][2] = dv_sum[at, :].astype(jnp.bfloat16)


def attention_forward(parts, bias):
    peers = len(parts)
    _, rows, width = parts[0].shape
    heads = width // HEAD_DIM
    total = peers * rows
    pairs = heads * total * total
    return pl.pallas_call(
        functools.partial(forward_kernel, 1.0 / math.sqrt(HEAD_DIM)),
        grid=(heads,),
        in_specs=[pl.BlockSpec((3, rows, HEAD_DIM), lambda h: (0, 0, h))] * peers
        + [pl.BlockSpec((total, total), lambda h: (0, 0))],
        out_specs=[
            pl.BlockSpec((1, total, total), lambda h: (h, 0, 0)),
            pl.BlockSpec((total, HEAD_DIM), lambda h: (0, h)),
        ],
        out_shape=[
            jax.ShapeDtypeStruct((heads, total, total), jnp.bfloat16),
            jax.ShapeDtypeStruct((total, width), jnp.bfloat16),
        ],
        compiler_params=pltpu.CompilerParams(vmem_limit_bytes=VMEM_LIMIT),
        cost_estimate=pl.CostEstimate(
            flops=4 * pairs * HEAD_DIM, bytes_accessed=4 * pairs, transcendentals=pairs
        ),
        name="attention_forward",
    )(*parts, bias)


def attention_backward(parts, grads, probs):
    peers = len(parts)
    _, rows, width = parts[0].shape
    heads = width // HEAD_DIM
    total = peers * rows
    pairs = heads * total * total
    by_part = pl.BlockSpec((3, rows, HEAD_DIM), lambda h: (0, 0, h))
    return pl.pallas_call(
        functools.partial(backward_kernel, 1.0 / math.sqrt(HEAD_DIM), peers),
        grid=(heads,),
        in_specs=[by_part] * peers
        + [pl.BlockSpec((rows, HEAD_DIM), lambda h: (0, h))] * peers
        + [pl.BlockSpec((1, total, total), lambda h: (h, 0, 0))],
        out_specs=[by_part] * peers,
        out_shape=[jax.ShapeDtypeStruct((3, rows, width), jnp.bfloat16)] * peers,
        scratch_shapes=[
            pltpu.VMEM((total, HEAD_DIM), jnp.float32),
            pltpu.VMEM((total, HEAD_DIM), jnp.float32),
        ],
        compiler_params=pltpu.CompilerParams(vmem_limit_bytes=VMEM_LIMIT),
        cost_estimate=pl.CostEstimate(
            flops=8 * pairs * HEAD_DIM, bytes_accessed=4 * pairs, transcendentals=0
        ),
        name="attention_backward",
    )(*parts, *grads, probs)


def weight_kernel(scale, *refs):
    cots, (att_ref, out_ref) = refs[:-2], refs[-2:]
    cot = jnp.concatenate([cot[...] for cot in cots], axis=0)
    out_ref[...] = (dot_tn(cot, att_ref[...]) * scale).astype(jnp.bfloat16)


def weight_partial(cots, attended, scale):
    rows, features = cots[0].shape
    total, width = attended.shape
    block = 512
    return pl.pallas_call(
        functools.partial(weight_kernel, scale),
        grid=(features // block,),
        in_specs=[pl.BlockSpec((rows, block), lambda i: (0, i))] * len(cots)
        + [pl.BlockSpec((total, width), lambda i: (0, 0))],
        out_specs=pl.BlockSpec((block, width), lambda i: (i, 0)),
        out_shape=jax.ShapeDtypeStruct((features, width), jnp.bfloat16),
        compiler_params=pltpu.CompilerParams(vmem_limit_bytes=VMEM_LIMIT),
        cost_estimate=pl.CostEstimate(
            flops=2 * total * features * width,
            bytes_accessed=2 * features * (total + width),
            transcendentals=0,
        ),
        name="weight_partial",
    )(*cots, attended)


def score_bias(tile_pairs, clip_lengths, clip_rows, order):
    tile_count = tile_pairs.shape[0]
    tile_rows = clip_rows // tile_count
    listed = jnp.any(tile_pairs[order][:, :, None] == order[None, None, :], axis=1)
    lengths = jnp.where(listed, clip_lengths[order][None, :], 0)
    live = jnp.arange(tile_rows, dtype=jnp.int32)[None, :, None] < lengths.T[:, None, :]
    bias = jnp.where(live, 0.0, DEAD).astype(jnp.bfloat16).reshape(clip_rows, tile_count)
    return jnp.repeat(bias, tile_rows, axis=1)


def swap(field, step, peers):
    return lax.ppermute(field, "seq", [(i, i ^ step) for i in range(peers)])


def per_device(queries, keys, values, gain_q, gain_k, tile_pairs, tile_lens, out_grad, w_out):
    dp_count = lax.axis_size("dp")
    peers = lax.axis_size("seq")
    position = lax.axis_index("seq")
    me = position.astype(jnp.int32)[None]
    clip_rows = queries.shape[0] * peers
    tile_count = tile_pairs.shape[0]
    near = tile_count // peers
    w_all = lax.all_gather(w_out, "dp", axis=0, tiled=True)
    sends = prepare(me, queries, keys, values, gain_q, gain_k, peers)
    parts = [sends[0]] + [swap(sends[step], step, peers) for step in range(1, peers)]
    cots = [out_grad]
    held = out_grad
    span = 1
    while span < peers:
        if span > 1:
            held = lax.optimization_barrier((out_grad, parts[span:]))[0]
        far = swap(held, span, peers)
        cots += [far] + [swap(far, step, peers) for step in range(1, span)]
        span *= 2
    tiles = jnp.arange(tile_count, dtype=jnp.int32)
    order = ((tiles // near) ^ position) * near + tiles % near
    bias = score_bias(tile_pairs, tile_lens[0], clip_rows, order)
    probs, attended = attention_forward(parts, bias)
    partial_w = weight_partial(cots, attended, 1.0 / dp_count)
    grad_w = lax.psum_scatter(partial_w, "dp", scatter_dimension=0, tiled=True)
    grads = [dot_nn(cot, w_all).astype(jnp.bfloat16) for cot in cots]
    backs = attention_backward(parts, grads, probs)
    backs = [backs[0]] + [swap(backs[step], step, peers) for step in range(1, peers)]
    grad_q, grad_k, grad_v = finish(me, queries, keys, gain_q, gain_k, backs)
    return (grad_q, grad_k, grad_v, grad_w.astype(jnp.float32))


def solution(mesh):
    return jax.shard_map(
        per_device,
        mesh=mesh,
        in_specs=(
            P(("dp", "seq"), None),
            P(("dp", "seq"), None),
            P(("dp", "seq"), None),
            P(),
            P(),
            P(),
            P("dp", None),
            P(("dp", "seq"), None),
            P("dp", "seq"),
        ),
        out_specs=(
            P(("dp", "seq"), None),
            P(("dp", "seq"), None),
            P(("dp", "seq"), None),
            P("dp", "seq"),
        ),
        check_vma=False,
    )
```

time: 359 us -> 302 us (0.84)
  blocking collectives: 40.2 us -> 0 us
  Pallas kernels: 48.8 us -> 65.7 us
  local copies, waits for them, and re-layouts: 32.2 us -> 16.3 us
  starting transfers between devices: 16.6 us -> 7.9 us
  matrix products: 25.6 us -> 17.3 us
    ppermute x0 -> x9, waiting for transfers between devices: none -> 141 us  [swap(): return lax.ppermute(field, 'seq', [(i, i ^ step) for i in range(peers)])]
    all_to_all x4 -> x0, waiting for transfers between devices: 92.2 us -> none  [the longest x1 29.1 us: per_device(): lax.all_to_all(key_normed, 'seq', split_axis=1, concat_axis=0, tiled=True)]
    all_gather x1, waiting for transfers between devices: 66.5 us -> 0.02 us  [per_device(): w_all = lax.all_gather(w_out, 'dp', axis=0, tiled=True)]
    all_to_all x2 -> x0, blocking collectives: 40.2 us -> none  [the longest x1 20.4 us: per_device(): lax.all_to_all(grad_kn, 'seq', split_axis=0, concat_axis=1, tiled=True)]
    reduce_scatter x0 -> x1, waiting for transfers between devices: none -> 35.2 us  [per_device(): grad_w = lax.psum_scatter(partial_w, 'dp', scatter_dimension=0, tiled=True)]
    pallas_call x0 -> x3, Pallas kernels: none -> 23.6 us  [the longest x1 14 us: weight_partial(): pl.pallas_call(functools.partial(weight_kernel, scale), grid=(features //...]
    all_to_all x4 -> x0, starting transfers between devices: 16.5 us -> none  [the longest x1 4.37 us: per_device(): lax.all_to_all(query_normed, 'seq', split_axis=1, concat_axis=0, tiled=True)]
    unnamed x4 -> x2, waiting for transfers between devices: 15.7 us -> 0.7 us
  transfers between devices with their start and end apart: 7 -> 11, of which waited for: 6 -> 7; matrix products, arithmetic and copies ran while one was open for 16% -> 9% of each run, Pallas kernels for 14% -> 22%
where the time goes in v2:
time: 302 us; the launch traced here: 301 us
  waiting for transfers between devices  177 us (59%)
  Pallas kernels  65.7 us (22%)
  matrix products  17.3 us (6%)
  local copies, waits for them, and re-layouts  16.3 us (5%)
  between operations  14.2 us (5%)
  starting transfers between devices  7.9 us (3%)
    ppermute x9, waiting for transfers between devices, swap(): return lax.ppermute(field, 'seq', [(i, i ^ step) for i in range(peers)])  141 us
    reduce_scatter x1, waiting for transfers between devices, per_device(): grad_w = lax.psum_scatter(partial_w, 'dp', scatter_dimension=0, tiled=True)  35.2 us
    pallas_call x1, Pallas kernels, attention_forward(): pl.pallas_call(functools.partial(forward_kernel, 1.0 / math.sqrt(HEAD_DIM...  22 us
    pallas_call x1, Pallas kernels, attention_backward(): pl.pallas_call(functools.partial(backward_kernel, 1.0 / math.sqrt(HEAD_DI...  20.1 us
    dot_general x4, matrix products, dot_nn(): return jnp.dot(left, right, preferred_element_type=jnp.float32)  17.3 us
    pallas_call x1, Pallas kernels, weight_partial(): pl.pallas_call(functools.partial(weight_kernel, scale), grid=(features //...  14 us
    unnamed x27, local copies, waits for them, and re-layouts  7.85 us
    ppermute x9, starting transfers between devices, swap(): return lax.ppermute(field, 'seq', [(i, i ^ step) for i in range(peers)])  7.83 us
  transfers between devices with their start and end apart: 11, of which 7 were waited for; matrix products, arithmetic and copies ran while one was open for 9% of the time, Pallas kernels for 22%

profile of v2, /device:TPU:0, one launch (start us, length us, event | category | flops | bytes accessed | tf_op | source)
XLA Modules:
  0.0 301.3 jit_solution(16558414622717623955)
XLA Ops:
  7.2 0.0 copy-start
  7.2 0.0 copy-start.11
  7.2 0.0 all-gather.2.cloned.1.call-start
  7.2 0.7 all-gather.2.cloned.1.call-update
  7.9 0.0 reduce-scatter.2.cloned.1.call-start
  8.0 0.7 broadcast_in_dim.42.gain_q_ref
  8.7 0.7 broadcast_in_dim.43.gain_k_ref
  9.4 0.0 copy-start.1
  9.4 1.3 copy-done.1
  10.7 4.6 %prepare.1 = (bf16[3,256,640]{2,1,0:T(8,128)(2,1)S(1)}, bf16[3,256,640]{2,1,0:T(8,128)(2,1)}, bf16[3,256,640]{2,1,0:T(8,128)(2,1)S(1)}, bf16[3,256,640]{2,1,0:T(8,128)(2,1)S(1)}) custom-call(s32[1]{0:T(128)} %bitcast.me_ref, bf16[256,2560]{1,0:T(8,128)(2,1)S(1)} %copy-done.1, bf16[256,2560]{1,0:T(8,128)(2,1)} %k_ref.3, bf16[256,2560]{1,0:T(8,128)(2,1)} %v_ref.1, ...), custom_call_target="tpu_custom_call" | custom-call | tf_op jit(solution)/shard_map/prepare/pallas_call | solution.py:56
  15.3 0.9 copy-done.4
  16.2 3.0 collective-permute-start.1
  19.2 0.0 collective-permute-start.2
  19.2 22.6 %collective-permute-done.1.refs_2_ = bf16[3,256,640]{2,1,0:T(8,128)(2,1)S(1)} collective-permute-done((bf16[3,256,640]{2,1,0:T(8,128)(2,1)S(1)}, bf16[3,256,640]{2,1,0:T(8,128)(2,1)S(1)}, u32[]{:S(2)}, u32[]{:S(2)}) %collective-permute-start.1) | collective-permute-done | bytes 983072 | tf_op jit(solution)/shard_map/ppermute | solution.py:249
  41.8 0.9 copy-done.7
  42.7 18.6 %collective-permute-done.2.refs_3_ = bf16[3,256,640]{2,1,0:T(8,128)(2,1)S(1)} collective-permute-done((bf16[3,256,640]{2,1,0:T(8,128)(2,1)S(1)}, bf16[3,256,640]{2,1,0:T(8,128)(2,1)S(1)}, u32[]{:S(2)}, u32[]{:S(2)}) %collective-permute-start.2) | collective-permute-done | bytes 983072 | tf_op jit(solution)/shard_map/ppermute | solution.py:249
  61.3 0.9 copy-done.9
  62.2 0.0 copy-done.3
  62.2 1.3 collective-permute-start.4
  63.5 1.1 collective-permute-start.3
  64.6 57.4 %collective-permute-done.4.refs_2_ = bf16[256,5120]{1,0:T(8,128)(2,1)} collective-permute-done((bf16[256,5120]{1,0:T(8,128)(2,1)S(1)}, bf16[256,5120]{1,0:T(8,128)(2,1)}, u32[]{:S(2)}, u32[]{:S(2)}) %collective-permute-start.4) | collective-permute-done | bytes 2621472 | tf_op jit(solution)/shard_map/ppermute | solution.py:249
  122.1 0.1 collective-permute-start.5
  122.2 0.4 collective-permute-start
  122.6 0.0 copy-done.11
  122.6 0.1 copy.16
  122.7 0.6 gather_fusion
  123.2 0.0 copy-done
  123.2 0.7 gather_fusion.1
  123.9 0.1 compare_reduce_fusion
  124.0 0.1 lt.45
  124.1 0.1 lt.46
  124.2 0.1 lt.40
  124.3 1.6 broadcast_in_dim.48
  125.9 3.9 %copy.17.refs_4_ = bf16[1024,1024]{1,0:T(8,128)(2,1)} copy(bf16[1024,1024]{0,1:T(8,128)(2,1)} %bitcast.18) | data formatting | bytes 4194304 | tf_op jit(solution)/shard_map/reshape | solution.py:245
  129.9 0.0 collective-permute-done.refs_1_
  129.9 1.2 copy-done.5
  131.1 1.2 copy-done.8
  132.3 1.2 copy-done.10
  133.5 22.0 %attention_forward.1 = (bf16[5,1024,1024]{2,1,0:T(8,128)(2,1)}, bf16[1024,640]{1,0:T(8,128)(2,1)S(1)}) custom-call(bf16[3,256,640]{2,1,0:T(8,128)(2,1)S(1)} %copy-done.5, bf16[3,256,640]{2,1,0:T(8,128)(2,1)} %collective-permute-done.refs_1_, bf16[3,256,640]{2,1,0:T(8,128)(2,1)S(1)} %copy-done.8, bf16[3,256,640]{2,1,0:T(8,128)(2,1)S(1)} %copy-done.10, ...), custom_call_target="tpu_custom_call" | custom-call | flops 2684354560 | bytes 20971520 | tf_op jit(solution)/shard_map/attention_forward/pallas_call | solution.py:163
  155.4 0.0 collective-permute-done.3.refs_1_
  155.5 0.0 collective-permute-done.5.refs_3_
  155.5 14.0 %weight_partial.1 = bf16[5120,640]{1,0:T(8,128)(2,1)} custom-call(bf16[256,5120]{1,0:T(8,128)(2,1)S(1)} %copy-done.3, bf16[256,5120]{1,0:T(8,128)(2,1)} %collective-permute-done.3.refs_1_, bf16[256,5120]{1,0:T(8,128)(2,1)} %collective-permute-done.4.refs_2_, bf16[256,5120]{1,0:T(8,128)(2,1)} %collective-permute-done.5.refs_3_, ...), custom_call_target="tpu_custom_call" | custom-call | flops 6710886400 | bytes 17039360 | tf_op jit(solution)/shard_map/weight_partial/pallas_call | solution.py:221
  169.4 0.0 reduce-scatter.2.cloned.1.call-update
  169.5 0.0 all-gather.2.cloned.1.call-done
  169.5 0.0 copy-start.12
  169.5 5.2 %convolution_convert_fusion.3.refs_4_ = bf16[256,640]{1,0:T(8,128)(2,1)S(1)} fusion(bf16[256,5120]{1,0:T(8,128)(2,1)S(1)} %copy-done.3, bf16[5120,640]{1,0:T(8,128)(2,1)} %all-gather.2.cloned.1.call-done), kind=kOutput, calls=%fused_computation.5 | convolution fusion | flops 1677885440 | bytes 9502720 | tf_op jit(solution)/shard_map/dot_general | solution.py:31
  174.7 0.0 copy-done.12
  174.7 4.0 %convolution_convert_fusion.2.refs_5_ = bf16[256,640]{1,0:T(8,128)(2,1)S(1)} fusion(bf16[256,5120]{1,0:T(8,128)(2,1)} %collective-permute-done.3.refs_1_, bf16[5120,640]{1,0:T(8,128)(2,1)S(1)} %copy-done.12), kind=kOutput, calls=%fused_computation.4 | convolution fusion | flops 1677885440 | bytes 9502720 | tf_op jit(solution)/shard_map/dot_general | solution.py:31
  178.8 4.0 %convolution_convert_fusion.1.refs_6_ = bf16[256,640]{1,0:T(8,128)(2,1)S(1)} fusion(bf16[256,5120]{1,0:T(8,128)(2,1)} %collective-permute-done.4.refs_2_, bf16[5120,640]{1,0:T(8,128)(2,1)S(1)} %copy-done.12), kind=kOutput, calls=%fused_computation.3 | convolution fusion | flops 1677885440 | bytes 9502720 | tf_op jit(solution)/shard_map/dot_general | solution.py:31
  182.8 0.0 copy-start.6
  182.8 4.1 %convolution_convert_fusion.refs_7_ = bf16[256,640]{1,0:T(8,128)(2,1)S(1)} fusion(bf16[256,5120]{1,0:T(8,128)(2,1)} %collective-permute-done.5.refs_3_, bf16[5120,640]{1,0:T(8,128)(2,1)S(1)} %copy-done.12), kind=kOutput, calls=%fused_computation.2 | convolution fusion | flops 1677885440 | bytes 9502720 | tf_op jit(solution)/shard_map/dot_general | solution.py:31
  186.9 0.0 copy-done.6
  186.9 0.0 copy-start.2
  186.9 20.1 %attention_backward.1 = (bf16[3,256,640]{2,1,0:T(8,128)(2,1)S(1)}, bf16[3,256,640]{2,1,0:T(8,128)(2,1)S(1)}, bf16[3,256,640]{2,1,0:T(8,128)(2,1)S(1)}, bf16[3,256,640]{2,1,0:T(8,128)(2,1)S(1)}) custom-call(bf16[3,256,640]{2,1,0:T(8,128)(2,1)S(1)} %copy-done.6, bf16[3,256,640]{2,1,0:T(8,128)(2,1)} %collective-permute-done.refs_1_, ...), custom_call_target="tpu_custom_call" | custom-call | flops 5368709120 | bytes 20971520 | tf_op jit(solution)/shard_map/attention_backward/pallas_call | solution.py:191
  206.9 0.2 collective-permute-start.6
  207.1 1.1 collective-permute-start.7
  208.3 0.6 collective-permute-start.8
  208.9 0.7 collective-permute-done.6.rest_1_
  209.6 22.2 %collective-permute-done.7.rest_2_ = bf16[3,256,640]{2,1,0:T(8,128)(2,1)S(1)} collective-permute-done((bf16[3,256,640]{2,1,0:T(8,128)(2,1)S(1)}, bf16[3,256,640]{2,1,0:T(8,128)(2,1)S(1)}, u32[]{:S(2)}, u32[]{:S(2)}) %collective-permute-start.7) | collective-permute-done | bytes 983072 | tf_op jit(solution)/shard_map/ppermute | solution.py:249
  231.7 20.0 %collective-permute-done.8.rest_3_ = bf16[3,256,640]{2,1,0:T(8,128)(2,1)S(1)} collective-permute-done((bf16[3,256,640]{2,1,0:T(8,128)(2,1)S(1)}, bf16[3,256,640]{2,1,0:T(8,128)(2,1)S(1)}, u32[]{:S(2)}, u32[]{:S(2)}) %collective-permute-start.8) | collective-permute-done | bytes 983072 | tf_op jit(solution)/shard_map/ppermute | solution.py:249
  251.7 0.0 copy-done.2
  251.7 5.1 %finish.1 = (bf16[256,2560]{1,0:T(8,128)(2,1)}, bf16[256,2560]{1,0:T(8,128)(2,1)}, bf16[256,2560]{1,0:T(8,128)(2,1)}) custom-call(s32[1]{0:T(128)} %bitcast.me_ref, bf16[256,2560]{1,0:T(8,128)(2,1)S(1)} %copy-done.2, bf16[256,2560]{1,0:T(8,128)(2,1)} %k_ref.3, f32[1,2560]{1,0:T(1,128)S(1)} %broadcast_in_dim.42.gain_q_ref, ...), custom_call_target="tpu_custom_call" | custom-call | tf_op jit(solution)/shard_map/finish/pallas_call | solution.py:96
  256.8 35.2 %reduce-scatter.2.cloned.1.call-done = bf16[640,640]{1,0:T(8,128)(2,1)} async-done(((bf16[5120,640]{1,0:T(8,128)(2,1)}), bf16[640,640]{1,0:T(8,128)(2,1)}) %reduce-scatter.2.cloned.1.call-update) | async-done | bytes 819216 | tf_op jit(solution)/shard_map/reduce_scatter | solution.py:277
  292.0 2.4 convert_element_type.24
  (13 shorter events, 0.1 us)
Async XLA Ops:
  7.2 116.1 %copy-start = (s32[1,16]{1,0:T(1,128)S(1)}, s32[1,16]{1,0:T(1,128)}, u32[]{:S(2)}) copy-start(s32[1,16]{1,0:T(1,128)} %param.15) | copy-start | bytes 196
  7.2 115.4 %copy-start.11 = (s32[16,8]{0,1:T(8,128)S(1)}, s32[16,8]{0,1:T(8,128)}, u32[]{:S(2)}) copy-start(s32[16,8]{0,1:T(8,128)} %param.14) | copy-start | bytes 1540
  7.2 162.3 %all-gather.2.cloned.1.call-start = ((), (), s32[]{:S(2)}) async-start(), calls=%async_computation.1 | async-start | bytes 7372800 | tf_op jit(solution)/shard_map/all_gather | solution.py:260
  7.9 284.1 %reduce-scatter.2.cloned.1.call-start = ((), (), s32[]{:S(2)}) async-start(), calls=%async_computation.2 | async-start | bytes 7372800 | tf_op jit(solution)/shard_map/reduce_scatter | solution.py:277
  9.4 1.3 copy-start.1
  10.7 51.5 %copy-start.3 = (bf16[256,5120]{1,0:T(8,128)(2,1)S(1)}, bf16[256,5120]{1,0:T(8,128)(2,1)}, u32[]{:S(2)}) copy-start(bf16[256,5120]{1,0:T(8,128)(2,1)} %refs_0_.1) | copy-start | bytes 7864324
  15.3 0.9 copy-start.4
  16.2 25.5 %collective-permute-start.1 = (bf16[3,256,640]{2,1,0:T(8,128)(2,1)S(1)}, bf16[3,256,640]{2,1,0:T(8,128)(2,1)S(1)}, u32[]{:S(2)}, u32[]{:S(2)}) collective-permute-start(bf16[3,256,640]{2,1,0:T(8,128)(2,1)S(1)} %get-tuple-element.20), channel_id=1, source_target_pairs={{0,2},{1,3},{2,0},{3,1},{4,6},{5,7},{6,4},{7,5},{8,10},{9,11},{10,... | collective-permute-start | bytes 2949128 | tf_op jit(solution)/shard_map/ppermute | solution.py:249
  19.2 42.1 %collective-permute-start.2 = (bf16[3,256,640]{2,1,0:T(8,128)(2,1)S(1)}, bf16[3,256,640]{2,1,0:T(8,128)(2,1)S(1)}, u32[]{:S(2)}, u32[]{:S(2)}) collective-permute-start(bf16[3,256,640]{2,1,0:T(8,128)(2,1)S(1)} %get-tuple-element.21), channel_id=1, source_target_pairs={{0,3},{1,2},{2,1},{3,0},{4,7},{5,6},{6,5},{7,4},{8,11},{9,10},{10,... | collective-permute-start | bytes 2949128 | tf_op jit(solution)/shard_map/ppermute | solution.py:249
  41.8 0.9 copy-start.7
  61.3 0.9 copy-start.9
  62.2 59.8 %collective-permute-start.4 = (bf16[256,5120]{1,0:T(8,128)(2,1)S(1)}, bf16[256,5120]{1,0:T(8,128)(2,1)}, u32[]{:S(2)}, u32[]{:S(2)}) collective-permute-start(bf16[256,5120]{1,0:T(8,128)(2,1)S(1)} %copy-done.3), channel_id=1, source_target_pairs={{0,2},{1,3},{2,0},{3,1},{4,6},{5,7},{6,4},{7,5},{8,10},{9,11},{10,... | collective-permute-start | bytes 7864328 | tf_op jit(solution)/shard_map/ppermute | solution.py:249
  63.5 91.9 %collective-permute-start.3 = (bf16[256,5120]{1,0:T(8,128)(2,1)S(1)}, bf16[256,5120]{1,0:T(8,128)(2,1)}, u32[]{:S(2)}, u32[]{:S(2)}) collective-permute-start(bf16[256,5120]{1,0:T(8,128)(2,1)S(1)} %copy-done.3), channel_id=1, source_target_pairs={{0,1},{1,0},{2,3},{3,2},{4,5},{5,4},{6,7},{7,6},{8,9},{9,8},{10,11... | collective-permute-start | bytes 7864328 | tf_op jit(solution)/shard_map/ppermute | solution.py:249
  122.1 33.4 %collective-permute-start.5 = (bf16[256,5120]{1,0:T(8,128)(2,1)}, bf16[256,5120]{1,0:T(8,128)(2,1)}, u32[]{:S(2)}, u32[]{:S(2)}) collective-permute-start(bf16[256,5120]{1,0:T(8,128)(2,1)} %collective-permute-done.4.refs_2_), channel_id=1, source_target_pairs={{0,1},{1,0},{2,3},{3,2},{4,5},{5,4},{6,7},{7,6},{8,9},{9,8},{10,11... | collective-permute-start | bytes 7864328 | tf_op jit(solution)/shard_map/ppermute | solution.py:249
  122.2 7.7 %collective-permute-start = (bf16[3,256,640]{2,1,0:T(8,128)(2,1)}, bf16[3,256,640]{2,1,0:T(8,128)(2,1)}, u32[]{:S(2)}, u32[]{:S(2)}) collective-permute-start(bf16[3,256,640]{2,1,0:T(8,128)(2,1)} %get-tuple-element.19), channel_id=1, source_target_pairs={{0,1},{1,0},{2,3},{3,2},{4,5},{5,4},{6,7},{7,6},{8,9},{9,8},{10,11... | collective-permute-start | bytes 2949128 | tf_op jit(solution)/shard_map/ppermute | solution.py:249
  129.9 1.2 copy-start.5
  131.1 1.2 copy-start.8
  132.3 1.2 copy-start.10
  169.5 5.3 %copy-start.12 = (bf16[5120,640]{1,0:T(8,128)(2,1)S(1)}, bf16[5120,640]{1,0:T(8,128)(2,1)}, u32[]{:S(2)}) copy-start(bf16[5120,640]{1,0:T(8,128)(2,1)} %all-gather.2.cloned.1.call-done) | copy-start | bytes 19660804
  182.8 4.1 %copy-start.6 = (bf16[3,256,640]{2,1,0:T(8,128)(2,1)S(1)}, bf16[3,256,640]{2,1,0:T(8,128)(2,1)}, u32[]{:S(2)}) copy-start(bf16[3,256,640]{2,1,0:T(8,128)(2,1)} %copy-done.4) | copy-start | bytes 2949124
  186.9 64.8 %copy-start.2 = (bf16[256,2560]{1,0:T(8,128)(2,1)S(1)}, bf16[256,2560]{1,0:T(8,128)(2,1)}, u32[]{:S(2)}) copy-start(bf16[256,2560]{1,0:T(8,128)(2,1)} %q_ref.3) | copy-start | bytes 3932164
  206.9 2.6 collective-permute-start.6
  207.1 24.6 %collective-permute-start.7 = (bf16[3,256,640]{2,1,0:T(8,128)(2,1)S(1)}, bf16[3,256,640]{2,1,0:T(8,128)(2,1)S(1)}, u32[]{:S(2)}, u32[]{:S(2)}) collective-permute-start(bf16[3,256,640]{2,1,0:T(8,128)(2,1)S(1)} %get-tuple-element.26), channel_id=1, source_target_pairs={{0,2},{1,3},{2,0},{3,1},{4,6},{5,7},{6,4},{7,5},{8,10},{9,11},{10,... | collective-permute-start | bytes 2949128 | tf_op jit(solution)/shard_map/ppermute | solution.py:249
  208.3 43.4 %collective-permute-start.8 = (bf16[3,256,640]{2,1,0:T(8,128)(2,1)S(1)}, bf16[3,256,640]{2,1,0:T(8,128)(2,1)S(1)}, u32[]{:S(2)}, u32[]{:S(2)}) collective-permute-start(bf16[3,256,640]{2,1,0:T(8,128)(2,1)S(1)} %get-tuple-element.27), channel_id=1, source_target_pairs={{0,3},{1,2},{2,1},{3,0},{4,7},{5,6},{6,5},{7,4},{8,11},{9,10},{10,... | collective-permute-start | bytes 2949128 | tf_op jit(solution)/shard_map/ppermute | solution.py:249
Sparse Core Ops, SparseCore 0:
  10.2 104.9 all-gather.1
  169.6 122.4 reduce-scatter.1

commit v3 on v2

--- a/solution.py
+++ b/solution.py
@@ -125,15 +125,15 @@
 
 
 def backward_kernel(factor, peers, *refs):
-    parts, grads, probs_ref = refs[:peers], refs[peers : 2 * peers], refs[2 * peers]
-    outs = refs[2 * peers + 1 : 3 * peers + 1]
-    dk_sum, dv_sum = refs[3 * peers + 1 :]
+    parts, (grad_ref, probs_ref) = refs[:peers], refs[peers : peers + 2]
+    outs = refs[peers + 2 : 2 * peers + 2]
+    dk_sum, dv_sum = refs[2 * peers + 2 :]
     rows = parts[0].shape[1]
     key_t = jnp.concatenate([part[1] for part in parts], axis=0).T
     value = jnp.concatenate([part[2] for part in parts], axis=0)
     for block in range(peers):
         at = pl.ds(block * rows, rows)
-        grad = grads[block][...]
+        grad = grad_ref[at, :]
         probs_low = probs_ref[0, :, at]
         grad_probs = dot_nt(value, grad)
         probs = probs_low.astype(jnp.float32)
@@ -181,7 +181,7 @@
     )(*parts, bias)
 
 
-def attention_backward(parts, grads, probs):
+def attention_backward(parts, grad, probs):
     peers = len(parts)
     _, rows, width = parts[0].shape
     heads = width // HEAD_DIM
@@ -192,7 +192,7 @@
         functools.partial(backward_kernel, 1.0 / math.sqrt(HEAD_DIM), peers),
         grid=(heads,),
         in_specs=[by_part] * peers
-        + [pl.BlockSpec((rows, HEAD_DIM), lambda h: (0, h))] * peers
+        + [pl.BlockSpec((total, HEAD_DIM), lambda h: (0, h))]
         + [pl.BlockSpec((1, total, total), lambda h: (h, 0, 0))],
         out_specs=[by_part] * peers,
         out_shape=[jax.ShapeDtypeStruct((3, rows, width), jnp.bfloat16)] * peers,
@@ -205,7 +205,7 @@
             flops=8 * pairs * HEAD_DIM, bytes_accessed=4 * pairs, transcendentals=0
         ),
         name="attention_backward",
-    )(*parts, *grads, probs)
+    )(*parts, grad, probs)
 
 
 def weight_kernel(scale, *refs):
@@ -233,6 +233,54 @@
         ),
         name="weight_partial",
     )(*cots, attended)
+
+
+def project_kernel(peers, *refs):
+    firsts, seconds, (w_ref, out_ref, total) = refs[:peers], refs[peers : 2 * peers], refs[2 * peers :]
+    step = pl.program_id(0)
+    width = w_ref.shape[2]
+    first = firsts[0].shape[1] // w_ref.shape[0]
+    w_first = w_ref[:, :first, :].reshape(firsts[0].shape[1], width)
+    w_second = w_ref[:, first:, :].reshape(seconds[0].shape[1], width)
+    product = dot_nn(jnp.concatenate([ref[...] for ref in firsts], axis=0), w_first)
+    product += dot_nn(jnp.concatenate([ref[...] for ref in seconds], axis=0), w_second)
+
+    @pl.when(step == 0)
+    def _():
+        total[...] = product
+
+    @pl.when(step > 0)
+    def _():
+        total[...] += product
+
+    @pl.when(step == pl.num_programs(0) - 1)
+    def _():
+        out_ref[...] = total[...].astype(jnp.bfloat16)
+
+
+def project(firsts, seconds, w_all, group):
+    peers = len(firsts)
+    rows = firsts[0].shape[0]
+    owners, depth, width = w_all.shape
+    steps = owners // group
+    total = peers * rows
+    return pl.pallas_call(
+        functools.partial(project_kernel, peers),
+        grid=(steps,),
+        in_specs=[pl.BlockSpec((rows, firsts[0].shape[1] // steps), lambda i: (0, i))] * peers
+        + [pl.BlockSpec((rows, seconds[0].shape[1] // steps), lambda i: (0, i))] * peers
+        + [pl.BlockSpec((group, depth, width), lambda i: (i, 0, 0))],
+        out_specs=pl.BlockSpec((total, width), lambda i: (0, 0)),
+        out_shape=jax.ShapeDtypeStruct((total, width), jnp.bfloat16),
+        scratch_shapes=[pltpu.VMEM((total, width), jnp.float32)],
+        compiler_params=pltpu.CompilerParams(vmem_limit_bytes=VMEM_LIMIT),
+        cost_estimate=pl.CostEstimate(
+            flops=2 * total * owners * depth * width,
+            bytes_accessed=2 * owners * depth * (total + width),
+            transcendentals=0,
+        ),
+        name="project",
+    )(*firsts, *seconds, w_all)
 
 
 def score_bias(tile_pairs, clip_lengths, clip_rows, order):
@@ -249,36 +297,71 @@
     return lax.ppermute(field, "seq", [(i, i ^ step) for i in range(peers)])
 
 
+def gather_rows(mine, before, after, peers):
+    blocks = [mine]
+    span = 1
+    far = mine
+    while span < peers:
+        held = mine if span == 1 else lax.optimization_barrier((mine, before))[0]
+        far = swap(held, span, peers)
+        blocks.append(far)
+        if span > 1:
+            handed = lax.optimization_barrier((far, after))[0]
+            blocks += [swap(handed, step, peers) for step in range(1, span)]
+        span *= 2
+    return blocks, far
+
+
+def pairwise_sum(field, before):
+    count = field.shape[0]
+    position = lax.axis_index("dp")
+    bit = 1
+    while bit < count:
+        pairs = field.reshape((field.shape[0] // 2, 2) + field.shape[1:])
+        side = (position // bit) % 2
+        kept = lax.dynamic_index_in_dim(pairs, side, 1, keepdims=False)
+        sent = lax.dynamic_index_in_dim(pairs, 1 - side, 1, keepdims=False)
+        got = lax.ppermute(sent, "dp", [(i, i ^ bit) for i in range(count)])
+        if bit == 1:
+            got = lax.optimization_barrier((got, before))[0]
+        field = (kept.astype(jnp.float32) + got.astype(jnp.float32)).astype(jnp.bfloat16)
+        bit *= 2
+    return field[0]
+
+
 def per_device(queries, keys, values, gain_q, gain_k, tile_pairs, tile_lens, out_grad, w_out):
     dp_count = lax.axis_size("dp")
     peers = lax.axis_size("seq")
     position = lax.axis_index("seq")
     me = position.astype(jnp.int32)[None]
-    clip_rows = queries.shape[0] * peers
+    rows = queries.shape[0]
+    clip_rows = rows * peers
     tile_count = tile_pairs.shape[0]
     near = tile_count // peers
-    w_all = lax.all_gather(w_out, "dp", axis=0, tiled=True)
+    depth, width = w_out.shape
+    first = depth * 3 // 5
+    group = max(1, 5 * HEAD_DIM // depth)
+    w_all = lax.all_gather(w_out, "dp", axis=0, tiled=False)
     sends = prepare(me, queries, keys, values, gain_q, gain_k, peers)
     parts = [sends[0]] + [swap(sends[step], step, peers) for step in range(1, peers)]
-    cots = [out_grad]
-    held = out_grad
-    span = 1
-    while span < peers:
-        if span > 1:
-            held = lax.optimization_barrier((out_grad, parts[span:]))[0]
-        far = swap(held, span, peers)
-        cots += [far] + [swap(far, step, peers) for step in range(1, span)]
-        span *= 2
+    by_owner = out_grad.reshape(rows, dp_count, depth)
+    mine_first = by_owner[:, :, :first].reshape(rows, -1)
+    mine_second = by_owner[:, :, first:].reshape(rows, -1)
     tiles = jnp.arange(tile_count, dtype=jnp.int32)
     order = ((tiles // near) ^ position) * near + tiles % near
     bias = score_bias(tile_pairs, tile_lens[0], clip_rows, order)
     probs, attended = attention_forward(parts, bias)
-    partial_w = weight_partial(cots, attended, 1.0 / dp_count)
-    grad_w = lax.psum_scatter(partial_w, "dp", scatter_dimension=0, tiled=True)
-    grads = [dot_nn(cot, w_all).astype(jnp.bfloat16) for cot in cots]
-    backs = attention_backward(parts, grads, probs)
+    firsts, far_first = gather_rows(mine_first, parts, attended, peers)
+    partial_first = weight_partial(firsts, attended, 1.0 / dp_count)
+    grad_w_first = lax.psum_scatter(partial_first, "dp", scatter_dimension=0, tiled=True)
+    seconds, _ = gather_rows(mine_second, far_first, partial_first, peers)
+    partial_second = weight_partial(seconds, attended, 1.0 / dp_count)
+    grad = project(firsts, seconds, w_all, group)
+    backs = attention_backward(parts, grad, probs)
+    grad_w_second = pairwise_sum(partial_second.reshape(dp_count, depth - first, width), backs)
     backs = [backs[0]] + [swap(backs[step], step, peers) for step in range(1, peers)]
     grad_q, grad_k, grad_v = finish(me, queries, keys, gain_q, gain_k, backs)
+    grad_w = jnp.concatenate([grad_w_first, grad_w_second], axis=0)
     return (grad_q, grad_k, grad_v, grad_w.astype(jnp.float32))
 
 

time: 302 us -> 261 us (0.86)
  waiting for transfers between devices: 177 us -> 111 us
  matrix products: 17.3 us -> 0 us
  Pallas kernels: 65.7 us -> 82 us
  local copies, waits for them, and re-layouts: 16.3 us -> 31.5 us
  starting transfers between devices: 7.9 us -> 14.8 us
  other arithmetic: 2.58 us -> 6.68 us
    ppermute x9 -> x12, waiting for transfers between devices: 141 us -> 82.7 us  [swap(): return lax.ppermute(field, 'seq', [(i, i ^ step) for i in range(peers)])]
    reduce_scatter x1, waiting for transfers between devices: 35.2 us -> 0.02 us  [per_device(): lax.psum_scatter(partial_first, 'dp', scatter_dimension=0, tiled=True)]
    ppermute x0 -> x3, waiting for transfers between devices: none -> 27.4 us  [pairwise_sum(): got = lax.ppermute(sent, 'dp', [(i, i ^ bit) for i in range(count)])]
    dot_general x4 -> x0, matrix products: 17.3 us -> none  [dot_nn(): return jnp.dot(left, right, preferred_element_type=jnp.float32)]
    pallas_call x0 -> x1, Pallas kernels: none -> 15.1 us  [project(): pl.pallas_call(functools.partial(project_kernel, peers), grid=(steps,), i...]
    unnamed x27 -> x58, local copies, waits for them, and re-layouts: 7.85 us -> 17.3 us
    ppermute x0 -> x3, starting transfers between devices: none -> 5.9 us  [pairwise_sum(): got = lax.ppermute(sent, 'dp', [(i, i ^ bit) for i in range(count)])]
    squeeze x0 -> x3, local copies, waits for them, and re-layouts: none -> 4.25 us  [pairwise_sum(): sent = lax.dynamic_index_in_dim(pairs, 1 - side, 1, keepdims=False)]
  transfers between devices with their start and end apart: 11 -> 17, of which waited for: 7 -> 9; matrix products, arithmetic and copies ran while one was open for 9% -> 8% of each run, Pallas kernels for 22% -> 32%
where the time goes in v3:
time: 261 us; the launch traced here: 260 us
  waiting for transfers between devices  111 us (43%)
  Pallas kernels  82 us (31%)
  local copies, waits for them, and re-layouts  31.5 us (12%)
  starting transfers between devices  14.8 us (6%)
  between operations  14.3 us (5%)
  other arithmetic  6.68 us (3%)
    ppermute x12, waiting for transfers between devices, swap(): return lax.ppermute(field, 'seq', [(i, i ^ step) for i in range(peers)])  82.7 us
    ppermute x3, waiting for transfers between devices, pairwise_sum(): got = lax.ppermute(sent, 'dp', [(i, i ^ bit) for i in range(count)])  27.4 us
    pallas_call x1, Pallas kernels, attention_forward(): pl.pallas_call(functools.partial(forward_kernel, 1.0 / math.sqrt(HEAD_DIM...  22 us
    pallas_call x1, Pallas kernels, attention_backward(): pl.pallas_call(functools.partial(backward_kernel, 1.0 / math.sqrt(HEAD_DI...  20.6 us
    unnamed x58, local copies, waits for them, and re-layouts  17.3 us
    pallas_call x1, Pallas kernels, project(): pl.pallas_call(functools.partial(project_kernel, peers), grid=(steps,), i...  15.1 us
    pallas_call x2, Pallas kernels, weight_partial(): pl.pallas_call(functools.partial(weight_kernel, scale), grid=(features //...  15 us
    ppermute x12, starting transfers between devices, swap(): return lax.ppermute(field, 'seq', [(i, i ^ step) for i in range(peers)])  8.82 us
  transfers between devices with their start and end apart: 17, of which 9 were waited for; matrix products, arithmetic and copies ran while one was open for 8% of the time, Pallas kernels for 32%

profile of v3, /device:TPU:0, one launch (start us, length us, event | category | flops | bytes accessed | tf_op | source)
XLA Modules:
  0.0 260.2 jit_solution(4024644312946218528)
XLA Ops:
  7.2 0.7 all-gather.3.cloned.1.call-update
  8.0 0.7 broadcast_in_dim.42.gain_q_ref
  8.7 0.7 broadcast_in_dim.43.gain_k_ref
  9.4 1.3 copy-done.2
  10.7 3.8 %prepare.1 = (bf16[3,256,640]{2,1,0:T(8,128)(2,1)S(1)}, bf16[3,256,640]{2,1,0:T(8,128)(2,1)S(1)}, bf16[3,256,640]{2,1,0:T(8,128)(2,1)S(1)}, bf16[3,256,640]{2,1,0:T(8,128)(2,1)S(1)}) custom-call(s32[1]{0:T(128)} %bitcast.me_ref, bf16[256,2560]{1,0:T(8,128)(2,1)S(1)} %copy-done.2, bf16[256,2560]{1,0:T(8,128)(2,1)} %k_ref.3, bf16[256,2560]{1,0:T(8,128)(2,1)} %v_ref.1, ...), custom_call_target="tpu_custom_call" | custom-call | tf_op jit(solution)/shard_map/prepare/pallas_call | solution.py:56
  14.6 0.5 collective-permute-start
  15.1 2.6 collective-permute-start.1
  17.8 0.5 copy.24
  18.3 0.2 slice.12
  18.4 1.4 copy-done.19
  19.8 0.3 copy.25
  20.1 1.0 copy-done.9
  21.1 19.2 %collective-permute-done.1.refs_2_ = bf16[3,256,640]{2,1,0:T(8,128)(2,1)S(1)} collective-permute-done((bf16[3,256,640]{2,1,0:T(8,128)(2,1)S(1)}, bf16[3,256,640]{2,1,0:T(8,128)(2,1)S(1)}, u32[]{:S(2)}, u32[]{:S(2)}) %collective-permute-start.1) | collective-permute-done | bytes 983072 | tf_op jit(solution)/shard_map/ppermute | solution.py:297
  40.3 0.9 copy-done.12
  41.2 19.6 %collective-permute-done.2.refs_3_ = bf16[3,256,640]{2,1,0:T(8,128)(2,1)S(1)} collective-permute-done((bf16[3,256,640]{2,1,0:T(8,128)(2,1)S(1)}, bf16[3,256,640]{2,1,0:T(8,128)(2,1)S(1)}, u32[]{:S(2)}, u32[]{:S(2)}) %collective-permute-start.2) | collective-permute-done | bytes 983072 | tf_op jit(solution)/shard_map/ppermute | solution.py:297
  60.8 1.0 copy-done.14
  61.8 1.6 collective-permute-start.4
  63.4 0.4 collective-permute-start.3
  63.8 0.1 copy.18
  63.9 0.7 gather_fusion.1
  64.5 0.6 gather_fusion
  65.2 0.1 compare_reduce_fusion
  65.3 0.1 lt.80
  65.4 0.1 lt.81
  65.5 1.6 broadcast_in_dim.48
  67.1 4.0 %copy.19.refs_4_ = bf16[1024,1024]{1,0:T(8,128)(2,1)} copy(bf16[1024,1024]{0,1:T(8,128)(2,1)} %bitcast.45) | data formatting | bytes 4194304 | tf_op jit(solution)/shard_map/reshape | solution.py:293
  71.1 1.2 copy-done.7
  72.3 1.2 copy-done.10
  73.5 1.2 copy-done.13
  74.7 1.2 copy-done.15
  75.9 22.0 %attention_forward.1 = (bf16[5,1024,1024]{2,1,0:T(8,128)(2,1)}, bf16[1024,640]{1,0:T(8,128)(2,1)S(1)}) custom-call(bf16[3,256,640]{2,1,0:T(8,128)(2,1)S(1)} %copy-done.7, bf16[3,256,640]{2,1,0:T(8,128)(2,1)S(1)} %copy-done.10, bf16[3,256,640]{2,1,0:T(8,128)(2,1)S(1)} %copy-done.13, bf16[3,256,640]{2,1,0:T(8,128)(2,1)S(1)} %copy-done.15, ...), custom_call_target="tpu_custom_call" | custom-call | flops 2684354560 | bytes 20971520 | tf_op jit(solution)/shard_map/attention_forward/pallas_call | solution.py:163
  97.9 0.7 collective-permute-done.4.refs_2_
  98.6 3.4 %collective-permute-done.5.refs_3_ = bf16[256,3072]{1,0:T(8,128)(2,1)S(1)} collective-permute-done((bf16[256,3072]{1,0:T(8,128)(2,1)S(1)}, bf16[256,3072]{1,0:T(8,128)(2,1)S(1)}, u32[]{:S(2)}, u32[]{:S(2)}) %collective-permute-start.5) | collective-permute-done | bytes 1572896 | tf_op jit(solution)/shard_map/ppermute | solution.py:297
  102.0 1.1 copy-done.26
  103.2 8.8 %weight_partial.2 = bf16[3072,640]{1,0:T(8,128)(2,1)} custom-call(bf16[256,3072]{1,0:T(8,128)(2,1)S(1)} %bitcast.37, bf16[256,3072]{1,0:T(8,128)(2,1)} %collective-permute-done.3.refs_1_, bf16[256,3072]{1,0:T(8,128)(2,1)S(1)} %collective-permute-done.4.refs_2_, bf16[256,3072]{1,0:T(8,128)(2,1)} %copy-done.26, bf16[1024,640]{1,0:T(8,128)(2,1)S(1)} %get-tuple-element.27.refs_4_), custom_call_target="tpu_custom_call" | custom-call | flops 4026531840 | bytes 10223616 | tf_op jit(solution)/shard_map/weight_partial/pallas_call | solution.py:221
  111.9 1.1 copy-done.16
  113.0 1.3 slice.13
  114.3 0.3 copy.26
  114.6 1.8 collective-permute-start.7
  116.4 23.5 %collective-permute-done.7.refs_6_.refs_2_ = bf16[256,2048]{1,0:T(8,128)(2,1)S(1)} collective-permute-done((bf16[256,2048]{1,0:T(8,128)(2,1)S(1)}, bf16[256,2048]{1,0:T(8,128)(2,1)S(1)}, u32[]{:S(2)}, u32[]{:S(2)}) %collective-permute-start.7) | collective-permute-done | bytes 1048608 | tf_op jit(solution)/shard_map/ppermute | solution.py:297
  139.9 2.8 %collective-permute-done.8.refs_7_.refs_3_ = bf16[256,2048]{1,0:T(8,128)(2,1)} collective-permute-done((bf16[256,2048]{1,0:T(8,128)(2,1)S(1)}, bf16[256,2048]{1,0:T(8,128)(2,1)}, u32[]{:S(2)}, u32[]{:S(2)}) %collective-permute-start.8) | collective-permute-done | bytes 1048608 | tf_op jit(solution)/shard_map/ppermute | solution.py:297
  142.7 1.4 copy-done.17
  144.0 6.3 %weight_partial.3 = bf16[2048,640]{1,0:T(8,128)(2,1)} custom-call(bf16[256,2048]{1,0:T(8,128)(2,1)S(1)} %bitcast.41, bf16[256,2048]{1,0:T(8,128)(2,1)S(1)} %collective-permute-done.6.refs_5_.refs_1_, bf16[256,2048]{1,0:T(8,128)(2,1)S(1)} %collective-permute-done.7.refs_6_.refs_2_, bf16[256,2048]{1,0:T(8,128)(2,1)} %collective-permute-done.8.refs_7_.refs_3_, ...), custom_call_target="tpu_custom_call" | custom-call | flops 2684354560 | bytes 6815744 | tf_op jit(solution)/shard_map/weight_partial/pallas_call | solution.py:221
  150.3 2.5 dynamic-slice_bitcast_fusion
  152.8 1.7 collective-permute-start.12
  154.5 15.1 %project.1.refs_4_ = bf16[1024,640]{1,0:T(8,128)(2,1)S(1)} custom-call(bf16[256,3072]{1,0:T(8,128)(2,1)} %bitcast.38, bf16[256,3072]{1,0:T(8,128)(2,1)} %collective-permute-done.3.refs_1_, bf16[256,3072]{1,0:T(8,128)(2,1)} %copy-done.5, bf16[256,3072]{1,0:T(8,128)(2,1)} %copy-done.26, bf16[256,2048]{1,0:T(8,128)(2,1)S(1)} %bitcast.42, ...), custom_call_target="tpu_custom_call" | custom-call | flops 6710886400 | bytes 17039360 | tf_op jit(solution)/shard_map/project/pallas_call | solution.py:267
  169.6 1.0 copy-done.18
  170.6 20.6 %attention_backward.1 = (bf16[3,256,640]{2,1,0:T(8,128)(2,1)S(1)}, bf16[3,256,640]{2,1,0:T(8,128)(2,1)}, bf16[3,256,640]{2,1,0:T(8,128)(2,1)}, bf16[3,256,640]{2,1,0:T(8,128)(2,1)}) custom-call(bf16[3,256,640]{2,1,0:T(8,128)(2,1)S(1)} %copy-done.8, bf16[3,256,640]{2,1,0:T(8,128)(2,1)S(1)} %copy-done.11, bf16[3,256,640]{2,1,0:T(8,128)(2,1)} %copy-done.12, ...), custom_call_target="tpu_custom_call" | custom-call | flops 5368709120 | bytes 20971520 | tf_op jit(solution)/shard_map/attention_backward/pallas_call | solution.py:191
  191.3 3.2 %collective-permute-done.12 = bf16[4,256,640]{2,1,0:T(8,128)(2,1)} collective-permute-done((bf16[4,256,640]{2,1,0:T(8,128)(2,1)}, bf16[4,256,640]{2,1,0:T(8,128)(2,1)}, u32[]{:S(2)}, u32[]{:S(2)}) %collective-permute-start.12) | collective-permute-done | bytes 1310752 | tf_op jit(solution)/shard_map/ppermute | solution.py:324
  194.5 1.7 fusion
  196.2 1.0 dynamic-slice_bitcast_fusion.1
  197.2 0.3 copy-done.20
  197.5 1.8 collective-permute-start.13
  199.3 1.5 collective-permute-start.10
  200.8 0.4 collective-permute-start.11
  201.1 24.2 %collective-permute-done.13 = bf16[2,256,640]{2,1,0:T(8,128)(2,1)} collective-permute-done((bf16[2,256,640]{2,1,0:T(8,128)(2,1)}, bf16[2,256,640]{2,1,0:T(8,128)(2,1)}, u32[]{:S(2)}, u32[]{:S(2)}) %collective-permute-start.13) | collective-permute-done | bytes 655392 | tf_op jit(solution)/shard_map/ppermute | solution.py:324
  225.3 1.4 fusion.1
  226.8 0.8 copy-done.23
  227.6 0.8 constant_dynamic-slice_fusion
  228.4 2.4 collective-permute-start.14
  230.8 13.6 %collective-permute-done.11.rest_3_ = bf16[3,256,640]{2,1,0:T(8,128)(2,1)} collective-permute-done((bf16[3,256,640]{2,1,0:T(8,128)(2,1)}, bf16[3,256,640]{2,1,0:T(8,128)(2,1)}, u32[]{:S(2)}, u32[]{:S(2)}) %collective-permute-start.11) | collective-permute-done | bytes 983072 | tf_op jit(solution)/shard_map/ppermute | solution.py:297
  244.4 5.5 %finish.1 = (bf16[256,2560]{1,0:T(8,128)(2,1)}, bf16[256,2560]{1,0:T(8,128)(2,1)}, bf16[256,2560]{1,0:T(8,128)(2,1)}) custom-call(s32[1]{0:T(128)} %bitcast.me_ref, bf16[256,2560]{1,0:T(8,128)(2,1)S(1)} %copy-done.3, bf16[256,2560]{1,0:T(8,128)(2,1)} %k_ref.3, f32[1,2560]{1,0:T(1,128)S(1)} %broadcast_in_dim.42.gain_q_ref, ...), custom_call_target="tpu_custom_call" | custom-call | tf_op jit(solution)/shard_map/finish/pallas_call | solution.py:96
  249.9 1.1 fusion.2
  251.0 2.3 maximum_convert_fusion
  (62 shorter events, 0.4 us)
Async XLA Ops:
  7.2 56.7 %copy-start = (s32[1,16]{1,0:T(1,128)S(1)}, s32[1,16]{1,0:T(1,128)}, u32[]{:S(2)}) copy-start(s32[1,16]{1,0:T(1,128)} %param.15) | copy-start | bytes 196
  7.2 147.3 %all-gather.3.cloned.1.call-start = ((), (), s32[]{:S(2)}) async-start(), calls=%async_computation.2 | async-start | bytes 7372800 | tf_op jit(solution)/shard_map/all_gather | solution.py:344
  7.9 243.1 %reduce-scatter.2.cloned.1.call-start = ((), (), s32[]{:S(2)}) async-start(), calls=%async_computation.1 | async-start | bytes 4423680 | tf_op jit(solution)/shard_map/reduce_scatter | solution.py:356
  9.4 1.3 copy-start.2
  10.7 7.0 %copy-start.21 = (bf16[256,5120]{1,0:T(8,128)(2,1)S(1)}, bf16[256,5120]{1,0:T(8,128)(2,1)}, u32[]{:S(2)}) copy-start(bf16[256,5120]{1,0:T(8,128)(2,1)} %param.16) | copy-start | bytes 7864324
  14.6 3.7 %copy-start.6 = (bf16[3,256,640]{2,1,0:T(8,128)(2,1)}, bf16[3,256,640]{2,1,0:T(8,128)(2,1)S(1)}, u32[]{:S(2)}) copy-start(bf16[3,256,640]{2,1,0:T(8,128)(2,1)S(1)} %get-tuple-element.22.refs_0_) | copy-start | bytes 2949124
  14.6 5.5 %collective-permute-start = (bf16[3,256,640]{2,1,0:T(8,128)(2,1)S(1)}, bf16[3,256,640]{2,1,0:T(8,128)(2,1)S(1)}, u32[]{:S(2)}, u32[]{:S(2)}) collective-permute-start(bf16[3,256,640]{2,1,0:T(8,128)(2,1)S(1)} %get-tuple-element.23), channel_id=1, source_target_pairs={{0,1},{1,0},{2,3},{3,2},{4,5},{5,4},{6,7},{7,6},{8,9},{9,8},{10,11... | collective-permute-start | bytes 2949128 | tf_op jit(solution)/shard_map/ppermute | solution.py:297
  15.1 25.2 %collective-permute-start.1 = (bf16[3,256,640]{2,1,0:T(8,128)(2,1)S(1)}, bf16[3,256,640]{2,1,0:T(8,128)(2,1)S(1)}, u32[]{:S(2)}, u32[]{:S(2)}) collective-permute-start(bf16[3,256,640]{2,1,0:T(8,128)(2,1)S(1)} %get-tuple-element.24), channel_id=1, source_target_pairs={{0,2},{1,3},{2,0},{3,1},{4,6},{5,7},{6,4},{7,5},{8,10},{9,11},{10,... | collective-permute-start | bytes 2949128 | tf_op jit(solution)/shard_map/ppermute | solution.py:297
  17.7 43.2 %collective-permute-start.2 = (bf16[3,256,640]{2,1,0:T(8,128)(2,1)S(1)}, bf16[3,256,640]{2,1,0:T(8,128)(2,1)S(1)}, u32[]{:S(2)}, u32[]{:S(2)}) collective-permute-start(bf16[3,256,640]{2,1,0:T(8,128)(2,1)S(1)} %get-tuple-element.25), channel_id=1, source_target_pairs={{0,3},{1,2},{2,1},{3,0},{4,7},{5,6},{6,5},{7,4},{8,11},{9,10},{10,... | collective-permute-start | bytes 2949128 | tf_op jit(solution)/shard_map/ppermute | solution.py:297
  18.3 1.5 copy-start.19
  19.8 44.0 %copy-start.25 = (s32[16,8]{0,1:T(8,128)S(1)}, s32[16,8]{0,1:T(8,128)}, u32[]{:S(2)}) copy-start(s32[16,8]{0,1:T(8,128)} %param.14) | copy-start | bytes 1540
  20.1 81.9 %copy-start.4 = (bf16[32,8,8,384]{3,1,2,0:T(8,128)(2,1)}, bf16[32,8,8,384]{3,1,2,0:T(8,128)(2,1)S(1)}, u32[]{:S(2)}) copy-start(bf16[32,8,8,384]{3,1,2,0:T(8,128)(2,1)S(1)} %copy.25) | copy-start | bytes 4718596
  20.1 1.0 copy-start.9
  40.3 0.9 copy-start.12
  60.8 1.0 copy-start.14
  61.8 36.8 %collective-permute-start.4 = (bf16[256,3072]{1,0:T(8,128)(2,1)S(1)}, bf16[256,3072]{1,0:T(8,128)(2,1)S(1)}, u32[]{:S(2)}, u32[]{:S(2)}) collective-permute-start(bf16[256,3072]{1,0:T(8,128)(2,1)S(1)} %bitcast.35), channel_id=1, source_target_pairs={{0,2},{1,3},{2,0},{3,1},{4,6},{5,7},{6,4},{7,5},{8,10},{9,11},{10,... | collective-permute-start | bytes 4718600 | tf_op jit(solution)/shard_map/ppermute | solution.py:297
  63.4 35.2 %collective-permute-start.3 = (bf16[256,3072]{1,0:T(8,128)(2,1)S(1)}, bf16[256,3072]{1,0:T(8,128)(2,1)}, u32[]{:S(2)}, u32[]{:S(2)}) collective-permute-start(bf16[256,3072]{1,0:T(8,128)(2,1)S(1)} %bitcast.36), channel_id=1, source_target_pairs={{0,1},{1,0},{2,3},{3,2},{4,5},{5,4},{6,7},{7,6},{8,9},{9,8},{10,11... | collective-permute-start | bytes 4718600 | tf_op jit(solution)/shard_map/ppermute | solution.py:297
  71.1 1.2 copy-start.7
  72.3 1.2 copy-start.10
  73.5 1.2 copy-start.13
  74.7 1.2 copy-start.15
  98.6 13.3 %copy-start.5 = (bf16[256,3072]{1,0:T(8,128)(2,1)}, bf16[256,3072]{1,0:T(8,128)(2,1)S(1)}, u32[]{:S(2)}) copy-start(bf16[256,3072]{1,0:T(8,128)(2,1)S(1)} %collective-permute-done.4.refs_2_) | copy-start | bytes 4718596
  98.6 3.4 %collective-permute-start.5 = (bf16[256,3072]{1,0:T(8,128)(2,1)S(1)}, bf16[256,3072]{1,0:T(8,128)(2,1)S(1)}, u32[]{:S(2)}, u32[]{:S(2)}) collective-permute-start(bf16[256,3072]{1,0:T(8,128)(2,1)S(1)} %collective-permute-done.4.refs_2_), channel_id=1, source_target_pairs={{0,1},{1,0},{2,3},{3,2},{4,5},{5,4},{6,7},{7,6},{8,9},{9,8},{10,11... | collective-permute-start | bytes 4718600 | tf_op jit(solution)/shard_map/ppermute | solution.py:297
  102.0 1.1 copy-start.26
  111.9 1.1 copy-start.16
  114.6 25.3 %collective-permute-start.7 = (bf16[256,2048]{1,0:T(8,128)(2,1)S(1)}, bf16[256,2048]{1,0:T(8,128)(2,1)S(1)}, u32[]{:S(2)}, u32[]{:S(2)}) collective-permute-start(bf16[256,2048]{1,0:T(8,128)(2,1)S(1)} %bitcast.39), channel_id=1, source_target_pairs={{0,2},{1,3},{2,0},{3,1},{4,6},{5,7},{6,4},{7,5},{8,10},{9,11},{10,... | collective-permute-start | bytes 3145736 | tf_op jit(solution)/shard_map/ppermute | solution.py:297
  116.4 23.5 %collective-permute-start.6 = (bf16[256,2048]{1,0:T(8,128)(2,1)S(1)}, bf16[256,2048]{1,0:T(8,128)(2,1)S(1)}, u32[]{:S(2)}, u32[]{:S(2)}) collective-permute-start(bf16[256,2048]{1,0:T(8,128)(2,1)S(1)} %bitcast.40), channel_id=1, source_target_pairs={{0,1},{1,0},{2,3},{3,2},{4,5},{5,4},{6,7},{7,6},{8,9},{9,8},{10,11... | collective-permute-start | bytes 3145736 | tf_op jit(solution)/shard_map/ppermute | solution.py:297
  139.9 2.8 %collective-permute-start.8 = (bf16[256,2048]{1,0:T(8,128)(2,1)S(1)}, bf16[256,2048]{1,0:T(8,128)(2,1)}, u32[]{:S(2)}, u32[]{:S(2)}) collective-permute-start(bf16[256,2048]{1,0:T(8,128)(2,1)S(1)} %collective-permute-done.7.refs_6_.refs_2_), channel_id=1, source_target_pairs={{0,1},{1,0},{2,3},{3,2},{4,5},{5,4},{6,7},{7,6},{8,9},{9,8},{10,11... | collective-permute-start | bytes 3145736 | tf_op jit(solution)/shard_map/ppermute | solution.py:297
  142.7 1.4 copy-start.17
  152.8 41.7 %collective-permute-start.12 = (bf16[4,256,640]{2,1,0:T(8,128)(2,1)}, bf16[4,256,640]{2,1,0:T(8,128)(2,1)}, u32[]{:S(2)}, u32[]{:S(2)}) collective-permute-start(bf16[4,256,640]{2,1,0:T(8,128)(2,1)} %dynamic-slice_bitcast_fusion), channel_id=1, source_target_pairs={{0,4},{4,0},{8,12},{12,8},{16,20},{20,16},{24,28},{28,24},{1,5},{5... | collective-permute-start | bytes 3932168 | tf_op jit(solution)/shard_map/ppermute | solution.py:324
  154.5 16.1 %copy-start.8 = (bf16[3,256,640]{2,1,0:T(8,128)(2,1)S(1)}, bf16[3,256,640]{2,1,0:T(8,128)(2,1)}, u32[]{:S(2)}) copy-start(bf16[3,256,640]{2,1,0:T(8,128)(2,1)} %copy-done.6) | copy-start | bytes 2949124
  154.5 16.1 %copy-start.11 = (bf16[3,256,640]{2,1,0:T(8,128)(2,1)S(1)}, bf16[3,256,640]{2,1,0:T(8,128)(2,1)}, u32[]{:S(2)}) copy-start(bf16[3,256,640]{2,1,0:T(8,128)(2,1)} %copy-done.9) | copy-start | bytes 2949124
  169.6 1.1 copy-start.18
  170.6 23.8 %copy-start.22 = (bf16[2048,640]{1,0:T(8,128)(2,1)S(1)}, bf16[2048,640]{1,0:T(8,128)(2,1)}, u32[]{:S(2)}) copy-start(bf16[2048,640]{1,0:T(8,128)(2,1)} %weight_partial.3) | copy-start | bytes 7864324
  196.2 1.3 copy-start.20
  197.5 47.0 %copy-start.3 = (bf16[256,2560]{1,0:T(8,128)(2,1)S(1)}, bf16[256,2560]{1,0:T(8,128)(2,1)}, u32[]{:S(2)}) copy-start(bf16[256,2560]{1,0:T(8,128)(2,1)} %q_ref.3) | copy-start | bytes 3932164
  197.5 27.9 %collective-permute-start.13 = (bf16[2,256,640]{2,1,0:T(8,128)(2,1)}, bf16[2,256,640]{2,1,0:T(8,128)(2,1)}, u32[]{:S(2)}, u32[]{:S(2)}) collective-permute-start(bf16[2,256,640]{2,1,0:T(8,128)(2,1)} %dynamic-slice_bitcast_fusion.1), channel_id=1, source_target_pairs={{0,8},{4,12},{8,0},{12,4},{16,24},{20,28},{24,16},{28,20},{1,9},{5... | collective-permute-start | bytes 1966088 | tf_op jit(solution)/shard_map/ppermute | solution.py:324
  199.3 31.5 %collective-permute-start.9 = (bf16[3,256,640]{2,1,0:T(8,128)(2,1)}, bf16[3,256,640]{2,1,0:T(8,128)(2,1)S(1)}, u32[]{:S(2)}, u32[]{:S(2)}) collective-permute-start(bf16[3,256,640]{2,1,0:T(8,128)(2,1)} %get-tuple-element.33), channel_id=1, source_target_pairs={{0,1},{1,0},{2,3},{3,2},{4,5},{5,4},{6,7},{7,6},{8,9},{9,8},{10,11... | collective-permute-start | bytes 2949128 | tf_op jit(solution)/shard_map/ppermute | solution.py:297
  199.3 31.5 %collective-permute-start.10 = (bf16[3,256,640]{2,1,0:T(8,128)(2,1)}, bf16[3,256,640]{2,1,0:T(8,128)(2,1)}, u32[]{:S(2)}, u32[]{:S(2)}) collective-permute-start(bf16[3,256,640]{2,1,0:T(8,128)(2,1)} %get-tuple-element.34), channel_id=1, source_target_pairs={{0,2},{1,3},{2,0},{3,1},{4,6},{5,7},{6,4},{7,5},{8,10},{9,11},{10,... | collective-permute-start | bytes 2949128 | tf_op jit(solution)/shard_map/ppermute | solution.py:297
  200.8 43.7 %collective-permute-start.11 = (bf16[3,256,640]{2,1,0:T(8,128)(2,1)}, bf16[3,256,640]{2,1,0:T(8,128)(2,1)}, u32[]{:S(2)}, u32[]{:S(2)}) collective-permute-start(bf16[3,256,640]{2,1,0:T(8,128)(2,1)} %get-tuple-element.35), channel_id=1, source_target_pairs={{0,3},{1,2},{2,1},{3,0},{4,7},{5,6},{6,5},{7,4},{8,11},{9,10},{10,... | collective-permute-start | bytes 2949128 | tf_op jit(solution)/shard_map/ppermute | solution.py:297
  226.8 0.8 copy-start.23
  228.4 21.5 %collective-permute-start.14 = (bf16[1,256,640]{2,1,0:T(8,128)(2,1)}, bf16[1,256,640]{2,1,0:T(8,128)(2,1)}, u32[]{:S(2)}, u32[]{:S(2)}) collective-permute-start(bf16[1,256,640]{2,1,0:T(8,128)(2,1)} %constant_dynamic-slice_fusion), channel_id=1, source_target_pairs={{0,16},{4,20},{8,24},{12,28},{16,0},{20,4},{24,8},{28,12},{1,17},{... | collective-permute-start | bytes 983048 | tf_op jit(solution)/shard_map/ppermute | solution.py:324
  230.8 19.1 %copy-start.24 = (bf16[2,256,640]{2,1,0:T(8,128)(2,1)S(1)}, bf16[2,256,640]{2,1,0:T(8,128)(2,1)}, u32[]{:S(2)}) copy-start(bf16[2,256,640]{2,1,0:T(8,128)(2,1)} %copy-done.23) | copy-start | bytes 1966084
  244.4 8.9 %copy-start.1 = (s32[1,16]{1,0:T(1,128)S(1)}, s32[1,16]{1,0:T(1,128)}, u32[]{:S(2)}) copy-start(s32[1,16]{1,0:T(1,128)} %param.15) | copy-start | bytes 196
Sparse Core Ops, SparseCore 0:
  10.2 104.9 all-gather.2
  118.9 101.1 reduce-scatter.1

commit v4 on v3

--- a/solution.py
+++ b/solution.py
@@ -68,10 +68,12 @@
     )(me, queries, keys, values, gain_q[None], gain_k[None])
 
 
-def finish_kernel(me_ref, q_ref, k_ref, gain_q_ref, gain_k_ref, *rest):
+def finish_kernel(peers, begins, me_ref, q_ref, k_ref, gain_q_ref, gain_k_ref, *rest):
     parts, (dq_ref, dk_ref, dv_ref, held) = rest[:-4], rest[-4:]
-    for step, part_ref in enumerate(parts):
-        part = columns_of(me_ref[0] ^ step, part_ref.shape[2])
+    for index, part_ref in enumerate(parts):
+        step, begin = index % peers, HEAD_DIM * begins[index // peers]
+        start = (me_ref[0] ^ step) * (q_ref.shape[1] // peers) + begin
+        part = pl.ds(pl.multiple_of(start, HEAD_DIM), part_ref.shape[2])
         held[0, :, part] = part_ref[0]
         held[1, :, part] = part_ref[1]
         dv_ref[:, part] = part_ref[2]
@@ -88,18 +90,20 @@
         ).astype(jnp.bfloat16)
 
 
-def finish(me, queries, keys, gain_q, gain_k, parts):
+def finish(me, queries, keys, gain_q, gain_k, parts, peers, begins):
     rows, width = queries.shape
-    part = width // len(parts)
     by_row = pl.BlockSpec((ROW_BLOCK, width), lambda i, me: (i, 0))
     gain = pl.BlockSpec((1, width), lambda i, me: (0, 0))
     return pl.pallas_call(
-        finish_kernel,
+        functools.partial(finish_kernel, peers, begins),
         grid_spec=pltpu.PrefetchScalarGridSpec(
             num_scalar_prefetch=1,
             grid=(rows // ROW_BLOCK,),
             in_specs=[by_row, by_row, gain, gain]
-            + [pl.BlockSpec((3, ROW_BLOCK, part), lambda i, me: (0, i, 0))] * len(parts),
+            + [
+                pl.BlockSpec((3, ROW_BLOCK, part.shape[2]), lambda i, me: (0, i, 0))
+                for part in parts
+            ],
             out_specs=[by_row] * 3,
             scratch_shapes=[pltpu.VMEM((2, ROW_BLOCK, width), jnp.bfloat16)],
         ),
@@ -181,21 +185,20 @@
     )(*parts, bias)
 
 
-def attention_backward(parts, grad, probs):
+def attention_backward(parts, grad, probs, begin, heads):
     peers = len(parts)
-    _, rows, width = parts[0].shape
-    heads = width // HEAD_DIM
+    rows = parts[0].shape[1]
     total = peers * rows
     pairs = heads * total * total
-    by_part = pl.BlockSpec((3, rows, HEAD_DIM), lambda h: (0, 0, h))
+    by_part = pl.BlockSpec((3, rows, HEAD_DIM), lambda h: (0, 0, h + begin))
     return pl.pallas_call(
         functools.partial(backward_kernel, 1.0 / math.sqrt(HEAD_DIM), peers),
         grid=(heads,),
         in_specs=[by_part] * peers
-        + [pl.BlockSpec((total, HEAD_DIM), lambda h: (0, h))]
-        + [pl.BlockSpec((1, total, total), lambda h: (h, 0, 0))],
-        out_specs=[by_part] * peers,
-        out_shape=[jax.ShapeDtypeStruct((3, rows, width), jnp.bfloat16)] * peers,
+        + [pl.BlockSpec((total, HEAD_DIM), lambda h: (0, h + begin))]
+        + [pl.BlockSpec((1, total, total), lambda h: (h + begin, 0, 0))],
+        out_specs=[pl.BlockSpec((3, rows, HEAD_DIM), lambda h: (0, 0, h))] * peers,
+        out_shape=[jax.ShapeDtypeStruct((3, rows, heads * HEAD_DIM), jnp.bfloat16)] * peers,
         scratch_shapes=[
             pltpu.VMEM((total, HEAD_DIM), jnp.float32),
             pltpu.VMEM((total, HEAD_DIM), jnp.float32),
@@ -235,19 +238,17 @@
     )(*cots, attended)
 
 
-def project_kernel(peers, *refs):
-    firsts, seconds, (w_ref, out_ref, total) = refs[:peers], refs[peers : 2 * peers], refs[2 * peers :]
+def project_kernel(peers, begin, *refs):
+    cots, w_ref, so_far, (out_ref, total) = refs[:peers], refs[peers], refs[peers + 1 : -2], refs[-2:]
     step = pl.program_id(0)
-    width = w_ref.shape[2]
-    first = firsts[0].shape[1] // w_ref.shape[0]
-    w_first = w_ref[:, :first, :].reshape(firsts[0].shape[1], width)
-    w_second = w_ref[:, first:, :].reshape(seconds[0].shape[1], width)
-    product = dot_nn(jnp.concatenate([ref[...] for ref in firsts], axis=0), w_first)
-    product += dot_nn(jnp.concatenate([ref[...] for ref in seconds], axis=0), w_second)
+    wide = cots[0].shape[1]
+    depth = wide // w_ref.shape[0]
+    weights = w_ref[:, begin : begin + depth, :].reshape(wide, w_ref.shape[2])
+    product = dot_nn(jnp.concatenate([ref[...] for ref in cots], axis=0), weights)
 
     @pl.when(step == 0)
     def _():
-        total[...] = product
+        total[...] = product + so_far[0][...] if so_far else product
 
     @pl.when(step > 0)
     def _():
@@ -255,32 +256,33 @@
 
     @pl.when(step == pl.num_programs(0) - 1)
     def _():
-        out_ref[...] = total[...].astype(jnp.bfloat16)
-
-
-def project(firsts, seconds, w_all, group):
-    peers = len(firsts)
-    rows = firsts[0].shape[0]
+        out_ref[...] = total[...].astype(out_ref.dtype)
+
+
+def project(cots, w_all, begin, group, so_far, dtype):
+    peers = len(cots)
+    rows, features = cots[0].shape
     owners, depth, width = w_all.shape
     steps = owners // group
     total = peers * rows
-    return pl.pallas_call(
-        functools.partial(project_kernel, peers),
+    whole = pl.BlockSpec((total, width), lambda i: (0, 0))
+    return pl.pallas_call(
+        functools.partial(project_kernel, peers, begin),
         grid=(steps,),
-        in_specs=[pl.BlockSpec((rows, firsts[0].shape[1] // steps), lambda i: (0, i))] * peers
-        + [pl.BlockSpec((rows, seconds[0].shape[1] // steps), lambda i: (0, i))] * peers
-        + [pl.BlockSpec((group, depth, width), lambda i: (i, 0, 0))],
-        out_specs=pl.BlockSpec((total, width), lambda i: (0, 0)),
-        out_shape=jax.ShapeDtypeStruct((total, width), jnp.bfloat16),
+        in_specs=[pl.BlockSpec((rows, features // steps), lambda i: (0, i))] * peers
+        + [pl.BlockSpec((group, depth, width), lambda i: (i, 0, 0))]
+        + [whole] * len(so_far),
+        out_specs=whole,
+        out_shape=jax.ShapeDtypeStruct((total, width), dtype),
         scratch_shapes=[pltpu.VMEM((total, width), jnp.float32)],
         compiler_params=pltpu.CompilerParams(vmem_limit_bytes=VMEM_LIMIT),
         cost_estimate=pl.CostEstimate(
-            flops=2 * total * owners * depth * width,
-            bytes_accessed=2 * owners * depth * (total + width),
+            flops=2 * total * features * width,
+            bytes_accessed=2 * features * total + 2 * owners * depth * width,
             transcendentals=0,
         ),
         name="project",
-    )(*firsts, *seconds, w_all)
+    )(*cots, w_all, *so_far)
 
 
 def score_bias(tile_pairs, clip_lengths, clip_rows, order):
@@ -354,13 +356,21 @@
     firsts, far_first = gather_rows(mine_first, parts, attended, peers)
     partial_first = weight_partial(firsts, attended, 1.0 / dp_count)
     grad_w_first = lax.psum_scatter(partial_first, "dp", scatter_dimension=0, tiled=True)
-    seconds, _ = gather_rows(mine_second, far_first, partial_first, peers)
+    grad_first = project(firsts, w_all, 0, group, [], jnp.float32)
+    seconds, _ = gather_rows(mine_second, far_first, (partial_first, grad_first), peers)
     partial_second = weight_partial(seconds, attended, 1.0 / dp_count)
-    grad = project(firsts, seconds, w_all, group)
-    backs = attention_backward(parts, grad, probs)
-    grad_w_second = pairwise_sum(partial_second.reshape(dp_count, depth - first, width), backs)
-    backs = [backs[0]] + [swap(backs[step], step, peers) for step in range(1, peers)]
-    grad_q, grad_k, grad_v = finish(me, queries, keys, gain_q, gain_k, backs)
+    grad = project(seconds, w_all, first, group, [grad_first], jnp.bfloat16)
+    heads = width // HEAD_DIM
+    cuts = (0, 1, (heads + 1) // 2, heads)
+    backs = []
+    for begin, end in zip(cuts, cuts[1:]):
+        outs = attention_backward(parts, grad, probs, begin, end - begin)
+        backs += [outs[0]] + [swap(outs[step], step, peers) for step in range(1, peers)]
+        grad = lax.optimization_barrier((grad, outs, backs[:-peers]))[0]
+    grad_w_second = pairwise_sum(partial_second.reshape(dp_count, depth - first, width), outs)
+    grad_q, grad_k, grad_v = finish(
+        me, queries, keys, gain_q, gain_k, backs, peers, cuts[:-1]
+    )
     grad_w = jnp.concatenate([grad_w_first, grad_w_second], axis=0)
     return (grad_q, grad_k, grad_v, grad_w.astype(jnp.float32))
 

time: 261 us -> 264 us (1.011)
  waiting for transfers between devices: 111 us -> 96 us
  Pallas kernels: 82 us -> 96.2 us
    pallas_call x2 -> x3, Pallas kernels: 20.5 us -> 30.5 us  [the longest x2 25 us: project(): pl.pallas_call(functools.partial(project_kernel, peers, begin), grid=(ste...]
    ppermute x12 -> x18, waiting for transfers between devices: 82.7 us -> 74.5 us  [swap(): return lax.ppermute(field, 'seq', [(i, i ^ step) for i in range(peers)])]
    ppermute x3, waiting for transfers between devices: 27.4 us -> 20.8 us  [pairwise_sum(): got = lax.ppermute(sent, 'dp', [(i, i ^ bit) for i in range(count)])]
    ppermute x12 -> x18, starting transfers between devices: 8.82 us -> 12.8 us  [swap(): return lax.ppermute(field, 'seq', [(i, i ^ step) for i in range(peers)])]
    pallas_call x1 -> x3, Pallas kernels: 20.6 us -> 24 us  [attention_backward(): pl.pallas_call(functools.partial(backward_kernel, 1.0 / math.sqrt(HEAD_DI...]
    unnamed x58 -> x68, local copies, waits for them, and re-layouts: 17.3 us -> 17.6 us
  transfers between devices with their start and end apart: 17 -> 23, of which waited for: 9 -> 10; matrix products, arithmetic and copies ran while one was open for 8% -> 8% of each run, Pallas kernels for 32% -> 37%
where the time goes in v4:
time: 264 us; the launch traced here: 262 us
  Pallas kernels  96.2 us (36%)
  waiting for transfers between devices  96 us (36%)
  local copies, waits for them, and re-layouts  31.8 us (12%)
  starting transfers between devices  17.1 us (6%)
  between operations  14.4 us (5%)
  other arithmetic  6.6 us (2%)
    ppermute x18, waiting for transfers between devices, swap(): return lax.ppermute(field, 'seq', [(i, i ^ step) for i in range(peers)])  74.5 us
    pallas_call x2, Pallas kernels, project(): pl.pallas_call(functools.partial(project_kernel, peers, begin), grid=(ste...  25 us
    pallas_call x3, Pallas kernels, attention_backward(): pl.pallas_call(functools.partial(backward_kernel, 1.0 / math.sqrt(HEAD_DI...  24 us
    pallas_call x1, Pallas kernels, attention_forward(): pl.pallas_call(functools.partial(forward_kernel, 1.0 / math.sqrt(HEAD_DIM...  21.9 us
    ppermute x3, waiting for transfers between devices, pairwise_sum(): got = lax.ppermute(sent, 'dp', [(i, i ^ bit) for i in range(count)])  20.8 us
    unnamed x68, local copies, waits for them, and re-layouts  17.6 us
    pallas_call x2, Pallas kernels, weight_partial(): pl.pallas_call(functools.partial(weight_kernel, scale), grid=(features //...  15.9 us
    ppermute x18, starting transfers between devices, swap(): return lax.ppermute(field, 'seq', [(i, i ^ step) for i in range(peers)])  12.8 us
  transfers between devices with their start and end apart: 23, of which 10 were waited for; matrix products, arithmetic and copies ran while one was open for 8% of the time, Pallas kernels for 37%

profile of v4, /device:TPU:0, one launch (start us, length us, event | category | flops | bytes accessed | tf_op | source)
XLA Modules:
  0.0 261.9 jit_solution(14820710090308433839)
XLA Ops:
  7.2 0.7 all-gather.3.cloned.1.call-update
  8.0 0.7 broadcast_in_dim.42.gain_q_ref
  8.7 0.7 broadcast_in_dim.43.gain_k_ref
  9.4 1.3 copy-done.6
  10.7 3.8 %prepare.1 = (bf16[3,256,640]{2,1,0:T(8,128)(2,1)S(1)}, bf16[3,256,640]{2,1,0:T(8,128)(2,1)S(1)}, bf16[3,256,640]{2,1,0:T(8,128)(2,1)S(1)}, bf16[3,256,640]{2,1,0:T(8,128)(2,1)S(1)}) custom-call(s32[1]{0:T(128)} %bitcast.me_ref, bf16[256,2560]{1,0:T(8,128)(2,1)S(1)} %copy-done.6, bf16[256,2560]{1,0:T(8,128)(2,1)} %k_ref.3, bf16[256,2560]{1,0:T(8,128)(2,1)} %v_ref.1, ...), custom_call_target="tpu_custom_call" | custom-call | tf_op jit(solution)/shard_map/prepare/pallas_call | solution.py:56
  14.6 0.5 collective-permute-start
  15.1 2.6 collective-permute-start.1
  17.8 0.5 copy.24
  18.4 1.3 copy-done.24
  19.7 1.4 copy.26
  21.1 19.1 %collective-permute-done.1.refs_2_ = bf16[3,256,640]{2,1,0:T(8,128)(2,1)S(1)} collective-permute-done((bf16[3,256,640]{2,1,0:T(8,128)(2,1)S(1)}, bf16[3,256,640]{2,1,0:T(8,128)(2,1)S(1)}, u32[]{:S(2)}, u32[]{:S(2)}) %collective-permute-start.1) | collective-permute-done | bytes 983072 | tf_op jit(solution)/shard_map/ppermute | solution.py:299
  40.3 20.5 %collective-permute-done.2.refs_3_ = bf16[3,256,640]{2,1,0:T(8,128)(2,1)S(1)} collective-permute-done((bf16[3,256,640]{2,1,0:T(8,128)(2,1)S(1)}, bf16[3,256,640]{2,1,0:T(8,128)(2,1)S(1)}, u32[]{:S(2)}, u32[]{:S(2)}) %collective-permute-start.2) | collective-permute-done | bytes 983072 | tf_op jit(solution)/shard_map/ppermute | solution.py:299
  60.8 1.0 copy-done.3
  61.8 1.6 collective-permute-start.4
  63.4 0.4 collective-permute-start.6
  63.8 0.6 gather_fusion
  64.4 0.7 gather_fusion.1
  65.5 1.6 broadcast_in_dim.48
  67.1 4.0 %copy.19.refs_4_ = bf16[1024,1024]{1,0:T(8,128)(2,1)} copy(bf16[1024,1024]{0,1:T(8,128)(2,1)} %bitcast.39) | data formatting | bytes 4194304 | tf_op jit(solution)/shard_map/reshape | solution.py:295
  71.1 1.2 copy-done.4
  72.3 21.9 %attention_forward.1 = (bf16[5,1024,1024]{2,1,0:T(8,128)(2,1)}, bf16[1024,640]{1,0:T(8,128)(2,1)S(1)}) custom-call(bf16[3,256,640]{2,1,0:T(8,128)(2,1)S(1)} %get-tuple-element.32.refs_0_, bf16[3,256,640]{2,1,0:T(8,128)(2,1)S(1)} %collective-permute-done.refs_1_, bf16[3,256,640]{2,1,0:T(8,128)(2,1)S(1)} %collective-permute-done.1.refs_2_, ...), custom_call_target="tpu_custom_call" | custom-call | flops 2684354560 | bytes 20971520 | tf_op jit(solution)/shard_map/attention_forward/pallas_call | solution.py:167
  94.2 4.7 %collective-permute-done.4.refs_2_ = bf16[256,3072]{1,0:T(8,128)(2,1)} collective-permute-done((bf16[256,3072]{1,0:T(8,128)(2,1)}, bf16[256,3072]{1,0:T(8,128)(2,1)}, u32[]{:S(2)}, u32[]{:S(2)}) %collective-permute-start.4) | collective-permute-done | bytes 1572896 | tf_op jit(solution)/shard_map/ppermute | solution.py:299
  98.9 3.6 %collective-permute-done.7.refs_3_ = bf16[256,3072]{1,0:T(8,128)(2,1)S(1)} collective-permute-done((bf16[256,3072]{1,0:T(8,128)(2,1)}, bf16[256,3072]{1,0:T(8,128)(2,1)S(1)}, u32[]{:S(2)}, u32[]{:S(2)}) %collective-permute-start.7) | collective-permute-done | bytes 1572896 | tf_op jit(solution)/shard_map/ppermute | solution.py:299
  102.5 1.1 copy-done.30
  103.7 9.2 %weight_partial.2 = bf16[3072,640]{1,0:T(8,128)(2,1)} custom-call(bf16[256,3072]{1,0:T(8,128)(2,1)} %bitcast.24.refs_0_, bf16[256,3072]{1,0:T(8,128)(2,1)} %collective-permute-done.6.refs_1_, bf16[256,3072]{1,0:T(8,128)(2,1)} %collective-permute-done.4.refs_2_, bf16[256,3072]{1,0:T(8,128)(2,1)} %copy-done.30, bf16[1024,640]{1,0:T(8,128)(2,1)S(1)} %get-tuple-element.38.refs_4_), custom_call_target="tpu_custom_call" | custom-call | flops 4026531840 | bytes 10223616 | tf_op jit(solution)/shard_map/weight_partial/pallas_call | solution.py:224
  112.8 1.1 copy-done.22
  113.9 1.3 slice.12
  115.2 1.3 copy.25
  116.5 1.7 collective-permute-start.5
  118.2 13.7 %project.2.refs_5_ = f32[1024,640]{1,0:T(8,128)} custom-call(bf16[256,3072]{1,0:T(8,128)(2,1)} %bitcast.24.refs_0_, bf16[256,3072]{1,0:T(8,128)(2,1)} %collective-permute-done.6.refs_1_, bf16[256,3072]{1,0:T(8,128)(2,1)} %collective-permute-done.4.refs_2_, bf16[256,3072]{1,0:T(8,128)(2,1)} %copy-done.30, bf16[8,640,640]{2,1,0:T(8,128)(2,1)} %bitcast.35), custom_call_target="tpu_custom_call" | custom-call | flops 4026531840 | bytes 12845056 | tf_op jit(solution)/shard_map/project/pallas_call | solution.py:269
  131.9 10.1 %collective-permute-done.5.refs_2_ = bf16[256,2048]{1,0:T(8,128)(2,1)} collective-permute-done((bf16[256,2048]{1,0:T(8,128)(2,1)}, bf16[256,2048]{1,0:T(8,128)(2,1)}, u32[]{:S(2)}, u32[]{:S(2)}) %collective-permute-start.5) | collective-permute-done | bytes 1048608 | tf_op jit(solution)/shard_map/ppermute | solution.py:299
  142.0 3.0 %collective-permute-done.8.refs_3_ = bf16[256,2048]{1,0:T(8,128)(2,1)} collective-permute-done((bf16[256,2048]{1,0:T(8,128)(2,1)}, bf16[256,2048]{1,0:T(8,128)(2,1)}, u32[]{:S(2)}, u32[]{:S(2)}) %collective-permute-start.8) | collective-permute-done | bytes 1048608 | tf_op jit(solution)/shard_map/ppermute | solution.py:299
  145.0 1.3 copy-done.23
  146.3 6.7 %weight_partial.3 = bf16[2048,640]{1,0:T(8,128)(2,1)} custom-call(bf16[256,2048]{1,0:T(8,128)(2,1)} %bitcast.22.refs_0_, bf16[256,2048]{1,0:T(8,128)(2,1)} %collective-permute-done.3.refs_1_, bf16[256,2048]{1,0:T(8,128)(2,1)} %collective-permute-done.5.refs_2_, bf16[256,2048]{1,0:T(8,128)(2,1)} %collective-permute-done.8.refs_3_, ...), custom_call_target="tpu_custom_call" | custom-call | flops 2684354560 | bytes 6815744 | tf_op jit(solution)/shard_map/weight_partial/pallas_call | solution.py:224
  153.1 2.5 dynamic-slice_bitcast_fusion
  155.6 1.7 collective-permute-start.18
  157.3 11.3 %project.3.refs_4_ = bf16[1024,640]{1,0:T(8,128)(2,1)S(1)} custom-call(bf16[256,2048]{1,0:T(8,128)(2,1)} %bitcast.22.refs_0_, bf16[256,2048]{1,0:T(8,128)(2,1)} %collective-permute-done.3.refs_1_, bf16[256,2048]{1,0:T(8,128)(2,1)} %collective-permute-done.5.refs_2_, bf16[256,2048]{1,0:T(8,128)(2,1)} %collective-permute-done.8.refs_3_, ...), custom_call_target="tpu_custom_call" | custom-call | flops 2684354560 | bytes 10747904 | tf_op jit(solution)/shard_map/project/pallas_call | solution.py:269
  168.6 5.5 %attention_backward.3 = (bf16[3,256,128]{2,1,0:T(8,128)(2,1)S(1)}, bf16[3,256,128]{2,1,0:T(8,128)(2,1)S(1)}, bf16[3,256,128]{2,1,0:T(8,128)(2,1)S(1)}, bf16[3,256,128]{2,1,0:T(8,128)(2,1)S(1)}) custom-call(bf16[3,256,640]{2,1,0:T(8,128)(2,1)S(1)} %get-tuple-element.32.refs_0_, bf16[3,256,640]{2,1,0:T(8,128)(2,1)S(1)} %collective-permute-done.refs_1_, ...), custom_call_target="tpu_custom_call" | custom-call | flops 1073741824 | bytes 4194304 | tf_op jit(solution)/shard_map/attention_backward/pallas_call | solution.py:194
  174.1 1.6 collective-permute-start.10
  175.7 0.6 collective-permute-start.9
  176.3 9.5 %attention_backward.4 = (bf16[3,256,256]{2,1,0:T(8,128)(2,1)S(1)}, bf16[3,256,256]{2,1,0:T(8,128)(2,1)}, bf16[3,256,256]{2,1,0:T(8,128)(2,1)}, bf16[3,256,256]{2,1,0:T(8,128)(2,1)S(1)}) custom-call(bf16[3,256,640]{2,1,0:T(8,128)(2,1)S(1)} %get-tuple-element.32.refs_0_, bf16[3,256,640]{2,1,0:T(8,128)(2,1)S(1)} %collective-permute-done.refs_1_, ...), custom_call_target="tpu_custom_call" | custom-call | flops 2147483648 | bytes 8388608 | tf_op jit(solution)/shard_map/attention_backward/pallas_call | solution.py:194
  185.8 0.8 copy-done.18
  186.6 0.7 copy-done.10
  187.3 0.7 copy-done.12
  187.9 9.1 %attention_backward.5 = (bf16[3,256,256]{2,1,0:T(8,128)(2,1)S(1)}, bf16[3,256,256]{2,1,0:T(8,128)(2,1)S(1)}, bf16[3,256,256]{2,1,0:T(8,128)(2,1)S(1)}, bf16[3,256,256]{2,1,0:T(8,128)(2,1)S(1)}) custom-call(bf16[3,256,640]{2,1,0:T(8,128)(2,1)S(1)} %get-tuple-element.32.refs_0_, bf16[3,256,640]{2,1,0:T(8,128)(2,1)S(1)} %collective-permute-done.refs_1_, ...), custom_call_target="tpu_custom_call" | custom-call | flops 2147483648 | bytes 8388608 | tf_op jit(solution)/shard_map/attention_backward/pallas_call | solution.py:194
  197.1 1.8 collective-permute-done.18
  198.9 1.6 fusion
  200.5 1.0 copy-done.25
  201.6 0.9 dynamic-slice_bitcast_fusion.1
  202.5 1.4 collective-permute-start.19
  203.9 1.5 collective-permute-start.13
  206.0 19.0 %collective-permute-done.19 = bf16[2,256,640]{2,1,0:T(8,128)(2,1)} collective-permute-done((bf16[2,256,640]{2,1,0:T(8,128)(2,1)}, bf16[2,256,640]{2,1,0:T(8,128)(2,1)}, u32[]{:S(2)}, u32[]{:S(2)}) %collective-permute-start.19) | collective-permute-done | bytes 655392 | tf_op jit(solution)/shard_map/ppermute | solution.py:326
  225.0 1.5 collective-permute-start.16
  226.5 1.4 fusion.1
  228.0 0.9 constant_dynamic-slice_fusion
  228.9 1.1 collective-permute-start.20
  230.0 7.3 %collective-permute-done.16.rest_10_ = bf16[3,256,256]{2,1,0:T(8,128)(2,1)} collective-permute-done((bf16[3,256,256]{2,1,0:T(8,128)(2,1)}, bf16[3,256,256]{2,1,0:T(8,128)(2,1)}, u32[]{:S(2)}, u32[]{:S(2)}) %collective-permute-start.16) | collective-permute-done | bytes 393248 | tf_op jit(solution)/shard_map/ppermute | solution.py:299
  237.3 6.1 %collective-permute-done.17.rest_11_ = bf16[3,256,256]{2,1,0:T(8,128)(2,1)} collective-permute-done((bf16[3,256,256]{2,1,0:T(8,128)(2,1)}, bf16[3,256,256]{2,1,0:T(8,128)(2,1)}, u32[]{:S(2)}, u32[]{:S(2)}) %collective-permute-start.17) | collective-permute-done | bytes 393248 | tf_op jit(solution)/shard_map/ppermute | solution.py:299
  243.4 0.9 copy-done.11
  244.4 0.9 copy-done.13
  245.3 0.9 copy-done.15
  246.2 5.4 %finish.1 = (bf16[256,2560]{1,0:T(8,128)(2,1)}, bf16[256,2560]{1,0:T(8,128)(2,1)}, bf16[256,2560]{1,0:T(8,128)(2,1)}) custom-call(s32[1]{0:T(128)} %bitcast.me_ref, bf16[256,2560]{1,0:T(8,128)(2,1)S(1)} %copy-done.7, bf16[256,2560]{1,0:T(8,128)(2,1)} %k_ref.3, f32[1,2560]{1,0:T(1,128)S(1)} %broadcast_in_dim.42.gain_q_ref, f32[1,2560]{1,0:T(1,128)S(1)} %copy-done.17, ...), custom_call_target="tpu_custom_call" | custom-call | tf_op jit(solution)/shard_map/finish/pallas_call | solution.py:97
  251.7 1.1 fusion.2
  252.8 2.3 maximum_convert_fusion
  (87 shorter events, 1.7 us)
Async XLA Ops:
  7.2 57.3 %copy-start = (s32[1,16]{1,0:T(1,128)S(1)}, s32[1,16]{1,0:T(1,128)}, u32[]{:S(2)}) copy-start(s32[1,16]{1,0:T(1,128)} %param.15) | copy-start | bytes 196
  7.2 111.1 %all-gather.3.cloned.1.call-start = ((), (), s32[]{:S(2)}) async-start(), calls=%async_computation.2 | async-start | bytes 7372800 | tf_op jit(solution)/shard_map/all_gather | solution.py:346
  7.9 244.9 %reduce-scatter.2.cloned.1.call-start = ((), (), s32[]{:S(2)}) async-start(), calls=%async_computation.1 | async-start | bytes 4423680 | tf_op jit(solution)/shard_map/reduce_scatter | solution.py:358
  9.4 5.2 %copy-start.16 = (f32[1,2560]{1,0:T(1,128)}, f32[1,2560]{1,0:T(1,128)S(1)}, u32[]{:S(2)}) copy-start(f32[1,2560]{1,0:T(1,128)S(1)} %broadcast_in_dim.43.gain_k_ref) | copy-start | bytes 30724
  9.4 1.3 copy-start.6
  10.7 7.0 %copy-start.26 = (bf16[256,5120]{1,0:T(8,128)(2,1)S(1)}, bf16[256,5120]{1,0:T(8,128)(2,1)}, u32[]{:S(2)}) copy-start(bf16[256,5120]{1,0:T(8,128)(2,1)} %param.16) | copy-start | bytes 7864324
  14.6 6.6 %collective-permute-start = (bf16[3,256,640]{2,1,0:T(8,128)(2,1)S(1)}, bf16[3,256,640]{2,1,0:T(8,128)(2,1)S(1)}, u32[]{:S(2)}, u32[]{:S(2)}) collective-permute-start(bf16[3,256,640]{2,1,0:T(8,128)(2,1)S(1)} %get-tuple-element.33), channel_id=1, source_target_pairs={{0,1},{1,0},{2,3},{3,2},{4,5},{5,4},{6,7},{7,6},{8,9},{9,8},{10,11... | collective-permute-start | bytes 2949128 | tf_op jit(solution)/shard_map/ppermute | solution.py:299
  15.1 25.2 %collective-permute-start.1 = (bf16[3,256,640]{2,1,0:T(8,128)(2,1)S(1)}, bf16[3,256,640]{2,1,0:T(8,128)(2,1)S(1)}, u32[]{:S(2)}, u32[]{:S(2)}) collective-permute-start(bf16[3,256,640]{2,1,0:T(8,128)(2,1)S(1)} %get-tuple-element.34), channel_id=1, source_target_pairs={{0,2},{1,3},{2,0},{3,1},{4,6},{5,7},{6,4},{7,5},{8,10},{9,11},{10,... | collective-permute-start | bytes 2949128 | tf_op jit(solution)/shard_map/ppermute | solution.py:299
  17.7 43.2 %collective-permute-start.2 = (bf16[3,256,640]{2,1,0:T(8,128)(2,1)S(1)}, bf16[3,256,640]{2,1,0:T(8,128)(2,1)S(1)}, u32[]{:S(2)}, u32[]{:S(2)}) collective-permute-start(bf16[3,256,640]{2,1,0:T(8,128)(2,1)S(1)} %get-tuple-element.35), channel_id=1, source_target_pairs={{0,3},{1,2},{2,1},{3,0},{4,7},{5,6},{6,5},{7,4},{8,11},{9,10},{10,... | collective-permute-start | bytes 2949128 | tf_op jit(solution)/shard_map/ppermute | solution.py:299
  18.2 1.5 copy-start.24
  19.7 44.0 %copy-start.31 = (s32[16,8]{0,1:T(8,128)S(1)}, s32[16,8]{0,1:T(8,128)}, u32[]{:S(2)}) copy-start(s32[16,8]{0,1:T(8,128)} %param.14) | copy-start | bytes 1540
  60.8 1.0 copy-start.3
  61.8 37.1 %collective-permute-start.4 = (bf16[256,3072]{1,0:T(8,128)(2,1)}, bf16[256,3072]{1,0:T(8,128)(2,1)}, u32[]{:S(2)}, u32[]{:S(2)}) collective-permute-start(bf16[256,3072]{1,0:T(8,128)(2,1)} %bitcast.24.refs_0_), channel_id=1, source_target_pairs={{0,2},{1,3},{2,0},{3,1},{4,6},{5,7},{6,4},{7,5},{8,10},{9,11},{10,... | collective-permute-start | bytes 4718600 | tf_op jit(solution)/shard_map/ppermute | solution.py:299
  63.4 35.6 %collective-permute-start.6 = (bf16[256,3072]{1,0:T(8,128)(2,1)}, bf16[256,3072]{1,0:T(8,128)(2,1)}, u32[]{:S(2)}, u32[]{:S(2)}) collective-permute-start(bf16[256,3072]{1,0:T(8,128)(2,1)} %bitcast.24.refs_0_), channel_id=1, source_target_pairs={{0,1},{1,0},{2,3},{3,2},{4,5},{5,4},{6,7},{7,6},{8,9},{9,8},{10,11... | collective-permute-start | bytes 4718600 | tf_op jit(solution)/shard_map/ppermute | solution.py:299
  71.1 1.2 copy-start.4
  98.9 3.6 %collective-permute-start.7 = (bf16[256,3072]{1,0:T(8,128)(2,1)}, bf16[256,3072]{1,0:T(8,128)(2,1)S(1)}, u32[]{:S(2)}, u32[]{:S(2)}) collective-permute-start(bf16[256,3072]{1,0:T(8,128)(2,1)} %collective-permute-done.4.refs_2_), channel_id=1, source_target_pairs={{0,1},{1,0},{2,3},{3,2},{4,5},{5,4},{6,7},{7,6},{8,9},{9,8},{10,11... | collective-permute-start | bytes 4718600 | tf_op jit(solution)/shard_map/ppermute | solution.py:299
  102.5 1.1 copy-start.30
  112.8 1.1 copy-start.22
  116.5 25.5 %collective-permute-start.5 = (bf16[256,2048]{1,0:T(8,128)(2,1)}, bf16[256,2048]{1,0:T(8,128)(2,1)}, u32[]{:S(2)}, u32[]{:S(2)}) collective-permute-start(bf16[256,2048]{1,0:T(8,128)(2,1)} %bitcast.22.refs_0_), channel_id=1, source_target_pairs={{0,2},{1,3},{2,0},{3,1},{4,6},{5,7},{6,4},{7,5},{8,10},{9,11},{10,... | collective-permute-start | bytes 3145736 | tf_op jit(solution)/shard_map/ppermute | solution.py:299
  118.2 23.8 %collective-permute-start.3 = (bf16[256,2048]{1,0:T(8,128)(2,1)}, bf16[256,2048]{1,0:T(8,128)(2,1)}, u32[]{:S(2)}, u32[]{:S(2)}) collective-permute-start(bf16[256,2048]{1,0:T(8,128)(2,1)} %bitcast.22.refs_0_), channel_id=1, source_target_pairs={{0,1},{1,0},{2,3},{3,2},{4,5},{5,4},{6,7},{7,6},{8,9},{9,8},{10,11... | collective-permute-start | bytes 3145736 | tf_op jit(solution)/shard_map/ppermute | solution.py:299
  142.0 3.0 %collective-permute-start.8 = (bf16[256,2048]{1,0:T(8,128)(2,1)}, bf16[256,2048]{1,0:T(8,128)(2,1)}, u32[]{:S(2)}, u32[]{:S(2)}) collective-permute-start(bf16[256,2048]{1,0:T(8,128)(2,1)} %collective-permute-done.5.refs_2_), channel_id=1, source_target_pairs={{0,1},{1,0},{2,3},{3,2},{4,5},{5,4},{6,7},{7,6},{8,9},{9,8},{10,11... | collective-permute-start | bytes 3145736 | tf_op jit(solution)/shard_map/ppermute | solution.py:299
  145.0 1.3 copy-start.23
  155.6 43.3 %collective-permute-start.18 = (bf16[4,256,640]{2,1,0:T(8,128)(2,1)}, bf16[4,256,640]{2,1,0:T(8,128)(2,1)}, u32[]{:S(2)}, u32[]{:S(2)}) collective-permute-start(bf16[4,256,640]{2,1,0:T(8,128)(2,1)} %dynamic-slice_bitcast_fusion), channel_id=1, source_target_pairs={{0,4},{4,0},{8,12},{12,8},{16,20},{20,16},{24,28},{28,24},{1,5},{5... | collective-permute-start | bytes 3932168 | tf_op jit(solution)/shard_map/ppermute | solution.py:326
  157.3 11.3 %copy-start.5 = (bf16[3,256,640]{2,1,0:T(8,128)(2,1)S(1)}, bf16[3,256,640]{2,1,0:T(8,128)(2,1)}, u32[]{:S(2)}) copy-start(bf16[3,256,640]{2,1,0:T(8,128)(2,1)} %copy-done.3) | copy-start | bytes 2949124
  168.6 5.5 %copy-start.2 = (bf16[1024,640]{1,0:T(8,128)(2,1)}, bf16[1024,640]{1,0:T(8,128)(2,1)S(1)}, u32[]{:S(2)}) copy-start(bf16[1024,640]{1,0:T(8,128)(2,1)S(1)} %project.3.refs_4_) | copy-start | bytes 3932164
  174.1 12.5 %collective-permute-start.10 = (bf16[3,256,128]{2,1,0:T(8,128)(2,1)S(1)}, bf16[3,256,128]{2,1,0:T(8,128)(2,1)S(1)}, u32[]{:S(2)}, u32[]{:S(2)}) collective-permute-start(bf16[3,256,128]{2,1,0:T(8,128)(2,1)S(1)} %get-tuple-element.44), channel_id=1, source_target_pairs={{0,2},{1,3},{2,0},{3,1},{4,6},{5,7},{6,4},{7,5},{8,10},{9,11},{10,... | collective-permute-start | bytes 589832 | tf_op jit(solution)/shard_map/ppermute | solution.py:299
  175.7 11.5 %collective-permute-start.11 = (bf16[3,256,128]{2,1,0:T(8,128)(2,1)S(1)}, bf16[3,256,128]{2,1,0:T(8,128)(2,1)S(1)}, u32[]{:S(2)}, u32[]{:S(2)}) collective-permute-start(bf16[3,256,128]{2,1,0:T(8,128)(2,1)S(1)} %get-tuple-element.45), channel_id=1, source_target_pairs={{0,3},{1,2},{2,1},{3,0},{4,7},{5,6},{6,5},{7,4},{8,11},{9,10},{10,... | collective-permute-start | bytes 589832 | tf_op jit(solution)/shard_map/ppermute | solution.py:299
  175.7 12.2 %collective-permute-start.9 = (bf16[3,256,128]{2,1,0:T(8,128)(2,1)S(1)}, bf16[3,256,128]{2,1,0:T(8,128)(2,1)S(1)}, u32[]{:S(2)}, u32[]{:S(2)}) collective-permute-start(bf16[3,256,128]{2,1,0:T(8,128)(2,1)S(1)} %get-tuple-element.43), channel_id=1, source_target_pairs={{0,1},{1,0},{2,3},{3,2},{4,5},{5,4},{6,7},{7,6},{8,9},{9,8},{10,11... | collective-permute-start | bytes 589832 | tf_op jit(solution)/shard_map/ppermute | solution.py:299
  185.8 0.8 copy-start.18
  186.6 0.7 copy-start.10
  187.3 0.7 copy-start.12
  187.9 9.1 %copy-start.14 = (bf16[3,256,128]{2,1,0:T(8,128)(2,1)}, bf16[3,256,128]{2,1,0:T(8,128)(2,1)S(1)}, u32[]{:S(2)}) copy-start(bf16[3,256,128]{2,1,0:T(8,128)(2,1)S(1)} %collective-permute-done.9.rest_1_) | copy-start | bytes 589828
  187.9 10.9 %copy-start.27 = (bf16[2048,640]{1,0:T(8,128)(2,1)S(1)}, bf16[2048,640]{1,0:T(8,128)(2,1)}, u32[]{:S(2)}) copy-start(bf16[2048,640]{1,0:T(8,128)(2,1)} %weight_partial.3) | copy-start | bytes 7864324
  197.0 3.5 %copy-start.8 = (bf16[3,256,256]{2,1,0:T(8,128)(2,1)}, bf16[3,256,256]{2,1,0:T(8,128)(2,1)S(1)}, u32[]{:S(2)}) copy-start(bf16[3,256,256]{2,1,0:T(8,128)(2,1)S(1)} %get-tuple-element.52.rest_8_) | copy-start | bytes 1179652
  197.0 3.5 %copy-start.19 = (bf16[3,256,256]{2,1,0:T(8,128)(2,1)}, bf16[3,256,256]{2,1,0:T(8,128)(2,1)S(1)}, u32[]{:S(2)}) copy-start(bf16[3,256,256]{2,1,0:T(8,128)(2,1)S(1)} %get-tuple-element.55) | copy-start | bytes 1179652
  197.0 3.5 %copy-start.20 = (bf16[3,256,256]{2,1,0:T(8,128)(2,1)}, bf16[3,256,256]{2,1,0:T(8,128)(2,1)S(1)}, u32[]{:S(2)}) copy-start(bf16[3,256,256]{2,1,0:T(8,128)(2,1)S(1)} %get-tuple-element.54) | copy-start | bytes 1179652
  197.1 3.5 %copy-start.21 = (bf16[3,256,256]{2,1,0:T(8,128)(2,1)}, bf16[3,256,256]{2,1,0:T(8,128)(2,1)S(1)}, u32[]{:S(2)}) copy-start(bf16[3,256,256]{2,1,0:T(8,128)(2,1)S(1)} %get-tuple-element.53) | copy-start | bytes 1179652
  200.5 1.1 copy-start.25
  202.5 41.0 %copy-start.7 = (bf16[256,2560]{1,0:T(8,128)(2,1)S(1)}, bf16[256,2560]{1,0:T(8,128)(2,1)}, u32[]{:S(2)}) copy-start(bf16[256,2560]{1,0:T(8,128)(2,1)} %q_ref.3) | copy-start | bytes 3932164
  202.5 41.0 %copy-start.9 = (bf16[3,256,256]{2,1,0:T(8,128)(2,1)S(1)}, bf16[3,256,256]{2,1,0:T(8,128)(2,1)}, u32[]{:S(2)}) copy-start(bf16[3,256,256]{2,1,0:T(8,128)(2,1)} %copy-done.8) | copy-start | bytes 1179652
  202.5 41.0 %copy-start.17 = (f32[1,2560]{1,0:T(1,128)S(1)}, f32[1,2560]{1,0:T(1,128)}, u32[]{:S(2)}) copy-start(f32[1,2560]{1,0:T(1,128)} %copy-done.16) | copy-start | bytes 30724
  202.5 22.5 %collective-permute-start.19 = (bf16[2,256,640]{2,1,0:T(8,128)(2,1)}, bf16[2,256,640]{2,1,0:T(8,128)(2,1)}, u32[]{:S(2)}, u32[]{:S(2)}) collective-permute-start(bf16[2,256,640]{2,1,0:T(8,128)(2,1)} %dynamic-slice_bitcast_fusion.1), channel_id=1, source_target_pairs={{0,8},{4,12},{8,0},{12,4},{16,24},{20,28},{24,16},{28,20},{1,9},{5... | collective-permute-start | bytes 1966088 | tf_op jit(solution)/shard_map/ppermute | solution.py:326
  203.9 24.1 %collective-permute-start.12 = (bf16[3,256,256]{2,1,0:T(8,128)(2,1)}, bf16[3,256,256]{2,1,0:T(8,128)(2,1)S(1)}, u32[]{:S(2)}, u32[]{:S(2)}) collective-permute-start(bf16[3,256,256]{2,1,0:T(8,128)(2,1)} %get-tuple-element.48), channel_id=1, source_target_pairs={{0,1},{1,0},{2,3},{3,2},{4,5},{5,4},{6,7},{7,6},{8,9},{9,8},{10,11... | collective-permute-start | bytes 1179656 | tf_op jit(solution)/shard_map/ppermute | solution.py:299
  203.9 25.0 %collective-permute-start.13 = (bf16[3,256,256]{2,1,0:T(8,128)(2,1)}, bf16[3,256,256]{2,1,0:T(8,128)(2,1)S(1)}, u32[]{:S(2)}, u32[]{:S(2)}) collective-permute-start(bf16[3,256,256]{2,1,0:T(8,128)(2,1)} %get-tuple-element.49), channel_id=1, source_target_pairs={{0,2},{1,3},{2,0},{3,1},{4,6},{5,7},{6,4},{7,5},{8,10},{9,11},{10,... | collective-permute-start | bytes 1179656 | tf_op jit(solution)/shard_map/ppermute | solution.py:299
  205.3 24.7 %collective-permute-start.14 = (bf16[3,256,256]{2,1,0:T(8,128)(2,1)}, bf16[3,256,256]{2,1,0:T(8,128)(2,1)S(1)}, u32[]{:S(2)}, u32[]{:S(2)}) collective-permute-start(bf16[3,256,256]{2,1,0:T(8,128)(2,1)} %copy-done.18), channel_id=1, source_target_pairs={{0,3},{1,2},{2,1},{3,0},{4,7},{5,6},{6,5},{7,4},{8,11},{9,10},{10,... | collective-permute-start | bytes 1179656 | tf_op jit(solution)/shard_map/ppermute | solution.py:299
  205.7 24.3 %collective-permute-start.15 = (bf16[3,256,256]{2,1,0:T(8,128)(2,1)}, bf16[3,256,256]{2,1,0:T(8,128)(2,1)}, u32[]{:S(2)}, u32[]{:S(2)}) collective-permute-start(bf16[3,256,256]{2,1,0:T(8,128)(2,1)} %copy-done.21), channel_id=1, source_target_pairs={{0,1},{1,0},{2,3},{3,2},{4,5},{5,4},{6,7},{7,6},{8,9},{9,8},{10,11... | collective-permute-start | bytes 1179656 | tf_op jit(solution)/shard_map/ppermute | solution.py:299
  225.0 12.3 %collective-permute-start.16 = (bf16[3,256,256]{2,1,0:T(8,128)(2,1)}, bf16[3,256,256]{2,1,0:T(8,128)(2,1)}, u32[]{:S(2)}, u32[]{:S(2)}) collective-permute-start(bf16[3,256,256]{2,1,0:T(8,128)(2,1)} %copy-done.20), channel_id=1, source_target_pairs={{0,2},{1,3},{2,0},{3,1},{4,6},{5,7},{6,4},{7,5},{8,10},{9,11},{10,... | collective-permute-start | bytes 1179656 | tf_op jit(solution)/shard_map/ppermute | solution.py:299
  227.9 1.0 copy-start.28
  227.9 15.5 %collective-permute-start.17 = (bf16[3,256,256]{2,1,0:T(8,128)(2,1)}, bf16[3,256,256]{2,1,0:T(8,128)(2,1)}, u32[]{:S(2)}, u32[]{:S(2)}) collective-permute-start(bf16[3,256,256]{2,1,0:T(8,128)(2,1)} %copy-done.19), channel_id=1, source_target_pairs={{0,3},{1,2},{2,1},{3,0},{4,7},{5,6},{6,5},{7,4},{8,11},{9,10},{10,... | collective-permute-start | bytes 1179656 | tf_op jit(solution)/shard_map/ppermute | solution.py:299
  228.9 22.8 %collective-permute-start.20 = (bf16[1,256,640]{2,1,0:T(8,128)(2,1)}, bf16[1,256,640]{2,1,0:T(8,128)(2,1)}, u32[]{:S(2)}, u32[]{:S(2)}) collective-permute-start(bf16[1,256,640]{2,1,0:T(8,128)(2,1)} %constant_dynamic-slice_fusion), channel_id=1, source_target_pairs={{0,16},{4,20},{8,24},{12,28},{16,0},{20,4},{24,8},{28,12},{1,17},{... | collective-permute-start | bytes 983048 | tf_op jit(solution)/shard_map/ppermute | solution.py:326
  243.4 0.9 copy-start.11
  244.4 0.9 copy-start.13
  245.3 0.9 copy-start.15
  246.2 5.5 %copy-start.29 = (bf16[2,256,640]{2,1,0:T(8,128)(2,1)S(1)}, bf16[2,256,640]{2,1,0:T(8,128)(2,1)}, u32[]{:S(2)}) copy-start(bf16[2,256,640]{2,1,0:T(8,128)(2,1)} %copy-done.28) | copy-start | bytes 1966084
  246.2 8.9 %copy-start.1 = (s32[1,16]{1,0:T(1,128)S(1)}, s32[1,16]{1,0:T(1,128)}, u32[]{:S(2)}) copy-start(s32[1,16]{1,0:T(1,128)} %param.15) | copy-start | bytes 196
Sparse Core Ops, SparseCore 0:
  10.2 105.0 all-gather.2
  119.0 96.3 reduce-scatter.1

commit v5 on v3

--- a/solution.py
+++ b/solution.py
@@ -315,18 +315,30 @@
 def pairwise_sum(field, before):
     count = field.shape[0]
     position = lax.axis_index("dp")
+
+    def swapped(sent, step):
+        return lax.ppermute(sent, "dp", [(i, i ^ step) for i in range(count)])
+
+    def summed(terms):
+        return sum(term.astype(jnp.float32) for term in terms).astype(jnp.bfloat16)
+
     bit = 1
-    while bit < count:
+    while field.shape[0] > 4:
         pairs = field.reshape((field.shape[0] // 2, 2) + field.shape[1:])
         side = (position // bit) % 2
         kept = lax.dynamic_index_in_dim(pairs, side, 1, keepdims=False)
         sent = lax.dynamic_index_in_dim(pairs, 1 - side, 1, keepdims=False)
-        got = lax.ppermute(sent, "dp", [(i, i ^ bit) for i in range(count)])
+        got = swapped(sent, bit)
         if bit == 1:
             got = lax.optimization_barrier((got, before))[0]
-        field = (kept.astype(jnp.float32) + got.astype(jnp.float32)).astype(jnp.bfloat16)
+        field = summed((kept, got))
         bit *= 2
-    return field[0]
+    mine = position // bit
+    terms = [lax.dynamic_index_in_dim(field, mine, 0, keepdims=False)]
+    for step in range(1, field.shape[0]):
+        sent = lax.dynamic_index_in_dim(field, mine ^ step, 0, keepdims=False)
+        terms.append(swapped(sent, step * bit))
+    return summed(terms)
 
 
 def per_device(queries, keys, values, gain_q, gain_k, tile_pairs, tile_lens, out_grad, w_out):
@@ -340,7 +352,7 @@
     near = tile_count // peers
     depth, width = w_out.shape
     first = depth * 3 // 5
-    group = max(1, 5 * HEAD_DIM // depth)
+    group = 10 * HEAD_DIM // depth
     w_all = lax.all_gather(w_out, "dp", axis=0, tiled=False)
     sends = prepare(me, queries, keys, values, gain_q, gain_k, peers)
     parts = [sends[0]] + [swap(sends[step], step, peers) for step in range(1, peers)]
@@ -353,8 +365,9 @@
     probs, attended = attention_forward(parts, bias)
     firsts, far_first = gather_rows(mine_first, parts, attended, peers)
     partial_first = weight_partial(firsts, attended, 1.0 / dp_count)
+    seconds, far_second = gather_rows(mine_second, far_first, partial_first, peers)
+    partial_first = lax.optimization_barrier((partial_first, far_second))[0]
     grad_w_first = lax.psum_scatter(partial_first, "dp", scatter_dimension=0, tiled=True)
-    seconds, _ = gather_rows(mine_second, far_first, partial_first, peers)
     partial_second = weight_partial(seconds, attended, 1.0 / dp_count)
     grad = project(firsts, seconds, w_all, group)
     backs = attention_backward(parts, grad, probs)

time: 261 us -> 256 us (0.981)
  starting transfers between devices: 14.8 us -> 19.5 us
  waiting for transfers between devices: 111 us -> 107 us
  local copies, waits for them, and re-layouts: 31.5 us -> 28.3 us
    ppermute x12, waiting for transfers between devices: 82.7 us -> 58.6 us  [swap(): return lax.ppermute(field, 'seq', [(i, i ^ step) for i in range(peers)])]
    ppermute x3 -> x4, waiting for transfers between devices: 27.4 us -> 47.3 us  [swapped(): return lax.ppermute(sent, 'dp', [(i, i ^ step) for i in range(count)])]
    ppermute x3 -> x4, starting transfers between devices: 5.9 us -> 10 us  [swapped(): return lax.ppermute(sent, 'dp', [(i, i ^ step) for i in range(count)])]
    pallas_call x1, Pallas kernels: 15.1 us -> 12.4 us  [project(): pl.pallas_call(functools.partial(project_kernel, peers), grid=(steps,), i...]
    unnamed x58 -> x50, local copies, waits for them, and re-layouts: 17.3 us -> 14.9 us
  transfers between devices with their start and end apart: 17 -> 18, of which waited for: 9 -> 11; matrix products, arithmetic and copies ran while one was open for 8% -> 8% of each run, Pallas kernels for 32% -> 29%
where the time goes in v5:
time: 256 us; the launch traced here: 255 us
  waiting for transfers between devices  107 us (42%)
  Pallas kernels  79.7 us (31%)
  local copies, waits for them, and re-layouts  28.3 us (11%)
  starting transfers between devices  19.5 us (8%)
  between operations  14.3 us (6%)
  other arithmetic  6.46 us (3%)
    ppermute x12, waiting for transfers between devices, swap(): return lax.ppermute(field, 'seq', [(i, i ^ step) for i in range(peers)])  58.6 us
    ppermute x4, waiting for transfers between devices, swapped(): return lax.ppermute(sent, 'dp', [(i, i ^ step) for i in range(count)])  47.3 us
    pallas_call x1, Pallas kernels, attention_forward(): pl.pallas_call(functools.partial(forward_kernel, 1.0 / math.sqrt(HEAD_DIM...  22 us
    pallas_call x1, Pallas kernels, attention_backward(): pl.pallas_call(functools.partial(backward_kernel, 1.0 / math.sqrt(HEAD_DI...  20.6 us
    pallas_call x2, Pallas kernels, weight_partial(): pl.pallas_call(functools.partial(weight_kernel, scale), grid=(features //...  15.5 us
    unnamed x50, local copies, waits for them, and re-layouts  14.9 us
    pallas_call x1, Pallas kernels, project(): pl.pallas_call(functools.partial(project_kernel, peers), grid=(steps,), i...  12.4 us
    ppermute x4, starting transfers between devices, swapped(): return lax.ppermute(sent, 'dp', [(i, i ^ step) for i in range(count)])  10 us
  transfers between devices with their start and end apart: 18, of which 11 were waited for; matrix products, arithmetic and copies ran while one was open for 8% of the time, Pallas kernels for 29%

profile of v5, /device:TPU:0, one launch (start us, length us, event | category | flops | bytes accessed | tf_op | source)
XLA Modules:
  0.0 254.7 jit_solution(10145206061601162465)
XLA Ops:
  7.2 0.7 all-gather.3.cloned.1.call-update
  8.0 0.7 broadcast_in_dim.42.gain_q_ref
  8.7 0.7 broadcast_in_dim.43.gain_k_ref
  9.4 1.3 copy-done.2
  10.7 3.8 %prepare.1 = (bf16[3,256,640]{2,1,0:T(8,128)(2,1)S(1)}, bf16[3,256,640]{2,1,0:T(8,128)(2,1)S(1)}, bf16[3,256,640]{2,1,0:T(8,128)(2,1)S(1)}, bf16[3,256,640]{2,1,0:T(8,128)(2,1)S(1)}) custom-call(s32[1]{0:T(128)} %bitcast.me_ref, bf16[256,2560]{1,0:T(8,128)(2,1)S(1)} %copy-done.2, bf16[256,2560]{1,0:T(8,128)(2,1)} %k_ref.3, bf16[256,2560]{1,0:T(8,128)(2,1)} %v_ref.1, ...), custom_call_target="tpu_custom_call" | custom-call | tf_op jit(solution)/shard_map/prepare/pallas_call | solution.py:56
  14.6 0.5 collective-permute-start
  15.1 2.6 %collective-permute-start.1 = (bf16[3,256,640]{2,1,0:T(8,128)(2,1)S(1)}, bf16[3,256,640]{2,1,0:T(8,128)(2,1)S(1)}, u32[]{:S(2)}, u32[]{:S(2)}) collective-permute-start(bf16[3,256,640]{2,1,0:T(8,128)(2,1)S(1)} %get-tuple-element.25), channel_id=1, source_target_pairs={{0,2},{1,3},{2,0},{3,1},{4,6},{5,7},{6,4},{7,5},{8,10},{9,11},{10,... | collective-permute-start | bytes 2949128 | tf_op jit(solution)/shard_map/ppermute | solution.py:297
  17.8 0.5 copy.22
  18.3 0.2 slice.12
  18.4 1.3 copy-done.17
  19.7 0.3 copy.23
  20.0 1.0 copy-done.7
  21.1 19.2 %collective-permute-done.1.refs_2_ = bf16[3,256,640]{2,1,0:T(8,128)(2,1)S(1)} collective-permute-done((bf16[3,256,640]{2,1,0:T(8,128)(2,1)S(1)}, bf16[3,256,640]{2,1,0:T(8,128)(2,1)S(1)}, u32[]{:S(2)}, u32[]{:S(2)}) %collective-permute-start.1) | collective-permute-done | bytes 983072 | tf_op jit(solution)/shard_map/ppermute | solution.py:297
  40.3 1.0 copy-done.10
  41.3 19.6 %collective-permute-done.2.refs_3_ = bf16[3,256,640]{2,1,0:T(8,128)(2,1)S(1)} collective-permute-done((bf16[3,256,640]{2,1,0:T(8,128)(2,1)S(1)}, bf16[3,256,640]{2,1,0:T(8,128)(2,1)S(1)}, u32[]{:S(2)}, u32[]{:S(2)}) %collective-permute-start.2) | collective-permute-done | bytes 983072 | tf_op jit(solution)/shard_map/ppermute | solution.py:297
  60.8 1.0 copy-done.12
  61.8 1.6 collective-permute-start.4
  63.4 0.4 collective-permute-start.3
  63.8 0.1 copy.18
  63.9 0.7 gather_fusion.1
  64.5 0.6 gather_fusion
  65.2 0.1 compare_reduce_fusion
  65.3 0.1 lt.71
  65.4 0.1 lt.72
  65.5 1.6 broadcast_in_dim.48
  67.1 3.9 %copy.19.refs_4_ = bf16[1024,1024]{1,0:T(8,128)(2,1)} copy(bf16[1024,1024]{0,1:T(8,128)(2,1)} %bitcast.44) | data formatting | bytes 4194304 | tf_op jit(solution)/shard_map/reshape | solution.py:293
  71.1 1.2 copy-done.8
  72.3 1.2 copy-done.11
  73.5 1.2 copy-done.13
  74.7 22.0 %attention_forward.1 = (bf16[5,1024,1024]{2,1,0:T(8,128)(2,1)}, bf16[1024,640]{1,0:T(8,128)(2,1)S(1)}) custom-call(bf16[3,256,640]{2,1,0:T(8,128)(2,1)S(1)} %get-tuple-element.23.refs_0_, bf16[3,256,640]{2,1,0:T(8,128)(2,1)S(1)} %copy-done.8, bf16[3,256,640]{2,1,0:T(8,128)(2,1)S(1)} %copy-done.11, bf16[3,256,640]{2,1,0:T(8,128)(2,1)S(1)} %copy-done.13, ...), custom_call_target="tpu_custom_call" | custom-call | flops 2684354560 | bytes 20971520 | tf_op jit(solution)/shard_map/attention_forward/pallas_call | solution.py:163
  96.7 2.0 collective-permute-done.4.refs_2_
  98.7 1.3 slice.13
  100.0 0.3 copy.24
  100.3 1.8 collective-permute-start.7
  102.1 0.2 collective-permute-done.5.refs_3_
  102.3 1.2 copy-done.22
  103.5 9.0 %weight_partial.2 = bf16[3072,640]{1,0:T(8,128)(2,1)} custom-call(bf16[256,3072]{1,0:T(8,128)(2,1)S(1)} %bitcast.36, bf16[256,3072]{1,0:T(8,128)(2,1)} %collective-permute-done.3.refs_1_, bf16[256,3072]{1,0:T(8,128)(2,1)} %collective-permute-done.4.refs_2_, bf16[256,3072]{1,0:T(8,128)(2,1)} %copy-done.22, bf16[1024,640]{1,0:T(8,128)(2,1)S(1)} %get-tuple-element.28.refs_4_), custom_call_target="tpu_custom_call" | custom-call | flops 4026531840 | bytes 10223616 | tf_op jit(solution)/shard_map/weight_partial/pallas_call | solution.py:221
  112.5 13.6 %collective-permute-done.7.refs_6_.refs_2_ = bf16[256,2048]{1,0:T(8,128)(2,1)} collective-permute-done((bf16[256,2048]{1,0:T(8,128)(2,1)S(1)}, bf16[256,2048]{1,0:T(8,128)(2,1)}, u32[]{:S(2)}, u32[]{:S(2)}) %collective-permute-start.7) | collective-permute-done | bytes 1048608 | tf_op jit(solution)/shard_map/ppermute | solution.py:297
  126.1 0.1 collective-permute-start.6
  126.2 0.5 collective-permute-start.8
  126.7 2.9 %collective-permute-done.6.refs_5_.refs_1_ = bf16[256,2048]{1,0:T(8,128)(2,1)S(1)} collective-permute-done((bf16[256,2048]{1,0:T(8,128)(2,1)S(1)}, bf16[256,2048]{1,0:T(8,128)(2,1)S(1)}, u32[]{:S(2)}, u32[]{:S(2)}) %collective-permute-start.6) | collective-permute-done | bytes 1048608 | tf_op jit(solution)/shard_map/ppermute | solution.py:297
  129.5 1.1 collective-permute-done.8.refs_7_.refs_3_
  130.6 1.3 copy-done.15
  132.0 6.4 %weight_partial.3 = bf16[2048,640]{1,0:T(8,128)(2,1)} custom-call(bf16[256,2048]{1,0:T(8,128)(2,1)S(1)} %bitcast.40, bf16[256,2048]{1,0:T(8,128)(2,1)S(1)} %collective-permute-done.6.refs_5_.refs_1_, bf16[256,2048]{1,0:T(8,128)(2,1)} %collective-permute-done.7.refs_6_.refs_2_, bf16[256,2048]{1,0:T(8,128)(2,1)} %collective-permute-done.8.refs_7_.refs_3_, ...), custom_call_target="tpu_custom_call" | custom-call | flops 2684354560 | bytes 6815744 | tf_op jit(solution)/shard_map/weight_partial/pallas_call | solution.py:221
  138.4 2.5 dynamic-slice_bitcast_fusion
  140.9 1.7 collective-permute-start.12
  142.6 12.4 %project.1.refs_4_ = bf16[1024,640]{1,0:T(8,128)(2,1)S(1)} custom-call(bf16[256,3072]{1,0:T(8,128)(2,1)} %bitcast.37, bf16[256,3072]{1,0:T(8,128)(2,1)} %collective-permute-done.3.refs_1_, bf16[256,3072]{1,0:T(8,128)(2,1)} %collective-permute-done.4.refs_2_, bf16[256,3072]{1,0:T(8,128)(2,1)} %copy-done.22, bf16[256,2048]{1,0:T(8,128)(2,1)S(1)} %bitcast.41, ...), custom_call_target="tpu_custom_call" | custom-call | flops 6710886400 | bytes 17039360 | tf_op jit(solution)/shard_map/project/pallas_call | solution.py:267
  155.0 1.0 copy-done.16
  156.1 20.6 %attention_backward.1 = (bf16[3,256,640]{2,1,0:T(8,128)(2,1)S(1)}, bf16[3,256,640]{2,1,0:T(8,128)(2,1)}, bf16[3,256,640]{2,1,0:T(8,128)(2,1)}, bf16[3,256,640]{2,1,0:T(8,128)(2,1)}) custom-call(bf16[3,256,640]{2,1,0:T(8,128)(2,1)S(1)} %copy-done.6, bf16[3,256,640]{2,1,0:T(8,128)(2,1)S(1)} %copy-done.9, bf16[3,256,640]{2,1,0:T(8,128)(2,1)} %copy-done.10, ...), custom_call_target="tpu_custom_call" | custom-call | flops 5368709120 | bytes 20971520 | tf_op jit(solution)/shard_map/attention_backward/pallas_call | solution.py:191
  176.6 5.8 %collective-permute-done.12 = bf16[4,256,640]{2,1,0:T(8,128)(2,1)S(1)} collective-permute-done((bf16[4,256,640]{2,1,0:T(8,128)(2,1)}, bf16[4,256,640]{2,1,0:T(8,128)(2,1)S(1)}, u32[]{:S(2)}, u32[]{:S(2)}) %collective-permute-start.12) | collective-permute-done | bytes 1310752 | tf_op jit(solution)/shard_map/ppermute | solution.py:320
  182.5 1.1 copy-done.20
  183.5 1.7 fusion
  185.3 0.9 dynamic-slice_bitcast_fusion.3
  186.2 1.8 collective-permute-start.13
  188.0 1.5 collective-permute-start.10
  189.5 0.4 collective-permute-start.11
  189.9 2.5 collective-permute-start.15
  192.4 3.5 %collective-permute-done.13 = bf16[256,640]{1,0:T(8,128)(2,1)} collective-permute-done((bf16[256,640]{1,0:T(8,128)(2,1)S(1)}, bf16[256,640]{1,0:T(8,128)(2,1)}, u32[]{:S(2)}, u32[]{:S(2)}) %collective-permute-start.13) | collective-permute-done | bytes 327712 | tf_op jit(solution)/shard_map/ppermute | solution.py:320
  195.9 3.9 %collective-permute-start.14 = (bf16[256,640]{1,0:T(8,128)(2,1)}, bf16[256,640]{1,0:T(8,128)(2,1)}, u32[]{:S(2)}, u32[]{:S(2)}) collective-permute-start(bf16[256,640]{1,0:T(8,128)(2,1)} %get-tuple-element.44), channel_id=1, source_target_pairs={{0,16},{4,20},{8,24},{12,28},{16,0},{20,4},{24,8},{28,12},{1,17},{... | collective-permute-start | bytes 983048 | tf_op jit(solution)/shard_map/ppermute | solution.py:320
  199.8 9.2 %collective-permute-done.15 = bf16[256,640]{1,0:T(8,128)(2,1)} collective-permute-done((bf16[256,640]{1,0:T(8,128)(2,1)}, bf16[256,640]{1,0:T(8,128)(2,1)}, u32[]{:S(2)}, u32[]{:S(2)}) %collective-permute-start.15) | collective-permute-done | bytes 327712 | tf_op jit(solution)/shard_map/ppermute | solution.py:320
  209.1 28.7 %collective-permute-done.14 = bf16[256,640]{1,0:T(8,128)(2,1)} collective-permute-done((bf16[256,640]{1,0:T(8,128)(2,1)}, bf16[256,640]{1,0:T(8,128)(2,1)}, u32[]{:S(2)}, u32[]{:S(2)}) %collective-permute-start.14) | collective-permute-done | bytes 327712 | tf_op jit(solution)/shard_map/ppermute | solution.py:320
  237.8 2.1 fusion.3
  239.9 2.5 maximum_convert_fusion
  242.4 5.5 %finish.1 = (bf16[256,2560]{1,0:T(8,128)(2,1)}, bf16[256,2560]{1,0:T(8,128)(2,1)}, bf16[256,2560]{1,0:T(8,128)(2,1)}) custom-call(s32[1]{0:T(128)} %bitcast.me_ref, bf16[256,2560]{1,0:T(8,128)(2,1)S(1)} %copy-done.3, bf16[256,2560]{1,0:T(8,128)(2,1)} %k_ref.3, f32[1,2560]{1,0:T(1,128)S(1)} %broadcast_in_dim.42.gain_q_ref, ...), custom_call_target="tpu_custom_call" | custom-call | tf_op jit(solution)/shard_map/finish/pallas_call | solution.py:96
  (54 shorter events, 0.4 us)
Async XLA Ops:
  7.2 56.7 %copy-start = (s32[1,16]{1,0:T(1,128)S(1)}, s32[1,16]{1,0:T(1,128)}, u32[]{:S(2)}) copy-start(s32[1,16]{1,0:T(1,128)} %param.15) | copy-start | bytes 196
  7.2 135.4 %all-gather.3.cloned.1.call-start = ((), (), s32[]{:S(2)}) async-start(), calls=%async_computation.2 | async-start | bytes 7372800 | tf_op jit(solution)/shard_map/all_gather | solution.py:356
  7.9 231.9 %reduce-scatter.2.cloned.1.call-start = ((), (), s32[]{:S(2)}) async-start(), calls=%async_computation.1 | async-start | bytes 4423680 | tf_op jit(solution)/shard_map/reduce_scatter | solution.py:370
  9.4 1.3 copy-start.2
  10.7 7.0 %copy-start.18 = (bf16[256,5120]{1,0:T(8,128)(2,1)S(1)}, bf16[256,5120]{1,0:T(8,128)(2,1)}, u32[]{:S(2)}) copy-start(bf16[256,5120]{1,0:T(8,128)(2,1)} %param.16) | copy-start | bytes 7864324
  14.6 56.5 %copy-start.5 = (bf16[3,256,640]{2,1,0:T(8,128)(2,1)}, bf16[3,256,640]{2,1,0:T(8,128)(2,1)S(1)}, u32[]{:S(2)}) copy-start(bf16[3,256,640]{2,1,0:T(8,128)(2,1)S(1)} %get-tuple-element.23.refs_0_) | copy-start | bytes 2949124
  14.6 5.5 %collective-permute-start = (bf16[3,256,640]{2,1,0:T(8,128)(2,1)S(1)}, bf16[3,256,640]{2,1,0:T(8,128)(2,1)S(1)}, u32[]{:S(2)}, u32[]{:S(2)}) collective-permute-start(bf16[3,256,640]{2,1,0:T(8,128)(2,1)S(1)} %get-tuple-element.24), channel_id=1, source_target_pairs={{0,1},{1,0},{2,3},{3,2},{4,5},{5,4},{6,7},{7,6},{8,9},{9,8},{10,11... | collective-permute-start | bytes 2949128 | tf_op jit(solution)/shard_map/ppermute | solution.py:297
  15.1 25.2 %collective-permute-start.1 = (bf16[3,256,640]{2,1,0:T(8,128)(2,1)S(1)}, bf16[3,256,640]{2,1,0:T(8,128)(2,1)S(1)}, u32[]{:S(2)}, u32[]{:S(2)}) collective-permute-start(bf16[3,256,640]{2,1,0:T(8,128)(2,1)S(1)} %get-tuple-element.25), channel_id=1, source_target_pairs={{0,2},{1,3},{2,0},{3,1},{4,6},{5,7},{6,4},{7,5},{8,10},{9,11},{10,... | collective-permute-start | bytes 2949128 | tf_op jit(solution)/shard_map/ppermute | solution.py:297
  17.7 43.2 %collective-permute-start.2 = (bf16[3,256,640]{2,1,0:T(8,128)(2,1)S(1)}, bf16[3,256,640]{2,1,0:T(8,128)(2,1)S(1)}, u32[]{:S(2)}, u32[]{:S(2)}) collective-permute-start(bf16[3,256,640]{2,1,0:T(8,128)(2,1)S(1)} %get-tuple-element.26), channel_id=1, source_target_pairs={{0,3},{1,2},{2,1},{3,0},{4,7},{5,6},{6,5},{7,4},{8,11},{9,10},{10,... | collective-permute-start | bytes 2949128 | tf_op jit(solution)/shard_map/ppermute | solution.py:297
  18.2 1.5 copy-start.17
  19.7 44.0 %copy-start.21 = (s32[16,8]{0,1:T(8,128)S(1)}, s32[16,8]{0,1:T(8,128)}, u32[]{:S(2)}) copy-start(s32[16,8]{0,1:T(8,128)} %param.14) | copy-start | bytes 1540
  20.0 82.3 %copy-start.4 = (bf16[32,8,8,384]{3,1,2,0:T(8,128)(2,1)}, bf16[32,8,8,384]{3,1,2,0:T(8,128)(2,1)S(1)}, u32[]{:S(2)}) copy-start(bf16[32,8,8,384]{3,1,2,0:T(8,128)(2,1)S(1)} %copy.23) | copy-start | bytes 4718596
  20.0 1.0 copy-start.7
  40.3 1.0 copy-start.10
  60.8 1.0 copy-start.12
  61.8 36.9 %collective-permute-start.4 = (bf16[256,3072]{1,0:T(8,128)(2,1)S(1)}, bf16[256,3072]{1,0:T(8,128)(2,1)}, u32[]{:S(2)}, u32[]{:S(2)}) collective-permute-start(bf16[256,3072]{1,0:T(8,128)(2,1)S(1)} %bitcast.34), channel_id=1, source_target_pairs={{0,2},{1,3},{2,0},{3,1},{4,6},{5,7},{6,4},{7,5},{8,10},{9,11},{10,... | collective-permute-start | bytes 4718600 | tf_op jit(solution)/shard_map/ppermute | solution.py:297
  63.4 38.8 %collective-permute-start.3 = (bf16[256,3072]{1,0:T(8,128)(2,1)S(1)}, bf16[256,3072]{1,0:T(8,128)(2,1)}, u32[]{:S(2)}, u32[]{:S(2)}) collective-permute-start(bf16[256,3072]{1,0:T(8,128)(2,1)S(1)} %bitcast.35), channel_id=1, source_target_pairs={{0,1},{1,0},{2,3},{3,2},{4,5},{5,4},{6,7},{7,6},{8,9},{9,8},{10,11... | collective-permute-start | bytes 4718600 | tf_op jit(solution)/shard_map/ppermute | solution.py:297
  71.1 1.2 copy-start.8
  72.3 1.2 copy-start.11
  73.5 1.2 copy-start.13
  96.7 5.6 %copy-start.14 = (bf16[1024,640]{1,0:T(8,128)(2,1)}, bf16[1024,640]{1,0:T(8,128)(2,1)S(1)}, u32[]{:S(2)}) copy-start(bf16[1024,640]{1,0:T(8,128)(2,1)S(1)} %get-tuple-element.28.refs_4_) | copy-start | bytes 3932164
  98.7 3.6 %collective-permute-start.5 = (bf16[256,3072]{1,0:T(8,128)(2,1)}, bf16[256,3072]{1,0:T(8,128)(2,1)S(1)}, u32[]{:S(2)}, u32[]{:S(2)}) collective-permute-start(bf16[256,3072]{1,0:T(8,128)(2,1)} %collective-permute-done.4.refs_2_), channel_id=1, source_target_pairs={{0,1},{1,0},{2,3},{3,2},{4,5},{5,4},{6,7},{7,6},{8,9},{9,8},{10,11... | collective-permute-start | bytes 4718600 | tf_op jit(solution)/shard_map/ppermute | solution.py:297
  100.3 25.7 %collective-permute-start.7 = (bf16[256,2048]{1,0:T(8,128)(2,1)S(1)}, bf16[256,2048]{1,0:T(8,128)(2,1)}, u32[]{:S(2)}, u32[]{:S(2)}) collective-permute-start(bf16[256,2048]{1,0:T(8,128)(2,1)S(1)} %bitcast.38), channel_id=1, source_target_pairs={{0,2},{1,3},{2,0},{3,1},{4,6},{5,7},{6,4},{7,5},{8,10},{9,11},{10,... | collective-permute-start | bytes 3145736 | tf_op jit(solution)/shard_map/ppermute | solution.py:297
  102.3 1.2 copy-start.22
  126.1 3.4 %collective-permute-start.6 = (bf16[256,2048]{1,0:T(8,128)(2,1)S(1)}, bf16[256,2048]{1,0:T(8,128)(2,1)S(1)}, u32[]{:S(2)}, u32[]{:S(2)}) collective-permute-start(bf16[256,2048]{1,0:T(8,128)(2,1)S(1)} %bitcast.39), channel_id=1, source_target_pairs={{0,1},{1,0},{2,3},{3,2},{4,5},{5,4},{6,7},{7,6},{8,9},{9,8},{10,11... | collective-permute-start | bytes 3145736 | tf_op jit(solution)/shard_map/ppermute | solution.py:297
  126.2 4.5 %collective-permute-start.8 = (bf16[256,2048]{1,0:T(8,128)(2,1)}, bf16[256,2048]{1,0:T(8,128)(2,1)}, u32[]{:S(2)}, u32[]{:S(2)}) collective-permute-start(bf16[256,2048]{1,0:T(8,128)(2,1)} %collective-permute-done.7.refs_6_.refs_2_), channel_id=1, source_target_pairs={{0,1},{1,0},{2,3},{3,2},{4,5},{5,4},{6,7},{7,6},{8,9},{9,8},{10,11... | collective-permute-start | bytes 3145736 | tf_op jit(solution)/shard_map/ppermute | solution.py:297
  130.6 1.3 copy-start.15
  140.9 41.6 %collective-permute-start.12 = (bf16[4,256,640]{2,1,0:T(8,128)(2,1)}, bf16[4,256,640]{2,1,0:T(8,128)(2,1)S(1)}, u32[]{:S(2)}, u32[]{:S(2)}) collective-permute-start(bf16[4,256,640]{2,1,0:T(8,128)(2,1)} %dynamic-slice_bitcast_fusion), channel_id=1, source_target_pairs={{0,4},{4,0},{8,12},{12,8},{16,20},{20,16},{24,28},{28,24},{1,5},{5... | collective-permute-start | bytes 3932168 | tf_op jit(solution)/shard_map/ppermute | solution.py:320
  142.6 13.4 %copy-start.6 = (bf16[3,256,640]{2,1,0:T(8,128)(2,1)S(1)}, bf16[3,256,640]{2,1,0:T(8,128)(2,1)}, u32[]{:S(2)}) copy-start(bf16[3,256,640]{2,1,0:T(8,128)(2,1)} %copy-done.5) | copy-start | bytes 2949124
  142.6 13.4 %copy-start.9 = (bf16[3,256,640]{2,1,0:T(8,128)(2,1)S(1)}, bf16[3,256,640]{2,1,0:T(8,128)(2,1)}, u32[]{:S(2)}) copy-start(bf16[3,256,640]{2,1,0:T(8,128)(2,1)} %copy-done.7) | copy-start | bytes 2949124
  155.0 1.1 copy-start.16
  156.1 27.5 %copy-start.19 = (bf16[2048,640]{1,0:T(8,128)(2,1)S(1)}, bf16[2048,640]{1,0:T(8,128)(2,1)}, u32[]{:S(2)}) copy-start(bf16[2048,640]{1,0:T(8,128)(2,1)} %weight_partial.3) | copy-start | bytes 7864324
  182.5 1.1 copy-start.20
  186.2 9.7 %collective-permute-start.13 = (bf16[256,640]{1,0:T(8,128)(2,1)S(1)}, bf16[256,640]{1,0:T(8,128)(2,1)}, u32[]{:S(2)}, u32[]{:S(2)}) collective-permute-start(bf16[256,640]{1,0:T(8,128)(2,1)S(1)} %get-tuple-element.42), channel_id=1, source_target_pairs={{0,8},{4,12},{8,0},{12,4},{16,24},{20,28},{24,16},{28,20},{1,9},{5... | collective-permute-start | bytes 983048 | tf_op jit(solution)/shard_map/ppermute | solution.py:320
  188.0 54.3 %collective-permute-start.9 = (bf16[3,256,640]{2,1,0:T(8,128)(2,1)}, bf16[3,256,640]{2,1,0:T(8,128)(2,1)S(1)}, u32[]{:S(2)}, u32[]{:S(2)}) collective-permute-start(bf16[3,256,640]{2,1,0:T(8,128)(2,1)} %get-tuple-element.34), channel_id=1, source_target_pairs={{0,1},{1,0},{2,3},{3,2},{4,5},{5,4},{6,7},{7,6},{8,9},{9,8},{10,11... | collective-permute-start | bytes 2949128 | tf_op jit(solution)/shard_map/ppermute | solution.py:297
  188.0 54.3 %collective-permute-start.10 = (bf16[3,256,640]{2,1,0:T(8,128)(2,1)}, bf16[3,256,640]{2,1,0:T(8,128)(2,1)}, u32[]{:S(2)}, u32[]{:S(2)}) collective-permute-start(bf16[3,256,640]{2,1,0:T(8,128)(2,1)} %get-tuple-element.35), channel_id=1, source_target_pairs={{0,2},{1,3},{2,0},{3,1},{4,6},{5,7},{6,4},{7,5},{8,10},{9,11},{10,... | collective-permute-start | bytes 2949128 | tf_op jit(solution)/shard_map/ppermute | solution.py:297
  189.5 52.8 %collective-permute-start.11 = (bf16[3,256,640]{2,1,0:T(8,128)(2,1)}, bf16[3,256,640]{2,1,0:T(8,128)(2,1)}, u32[]{:S(2)}, u32[]{:S(2)}) collective-permute-start(bf16[3,256,640]{2,1,0:T(8,128)(2,1)} %get-tuple-element.36), channel_id=1, source_target_pairs={{0,3},{1,2},{2,1},{3,0},{4,7},{5,6},{6,5},{7,4},{8,11},{9,10},{10,... | collective-permute-start | bytes 2949128 | tf_op jit(solution)/shard_map/ppermute | solution.py:297
  189.9 19.2 %collective-permute-start.15 = (bf16[256,640]{1,0:T(8,128)(2,1)}, bf16[256,640]{1,0:T(8,128)(2,1)}, u32[]{:S(2)}, u32[]{:S(2)}) collective-permute-start(bf16[256,640]{1,0:T(8,128)(2,1)} %get-tuple-element.43), channel_id=1, source_target_pairs={{0,24},{4,28},{8,16},{12,20},{16,8},{20,12},{24,0},{28,4},{1,25},{... | collective-permute-start | bytes 983048 | tf_op jit(solution)/shard_map/ppermute | solution.py:320
  195.9 41.9 %collective-permute-start.14 = (bf16[256,640]{1,0:T(8,128)(2,1)}, bf16[256,640]{1,0:T(8,128)(2,1)}, u32[]{:S(2)}, u32[]{:S(2)}) collective-permute-start(bf16[256,640]{1,0:T(8,128)(2,1)} %get-tuple-element.44), channel_id=1, source_target_pairs={{0,16},{4,20},{8,24},{12,28},{16,0},{20,4},{24,8},{28,12},{1,17},{... | collective-permute-start | bytes 983048 | tf_op jit(solution)/shard_map/ppermute | solution.py:320
  239.8 2.5 copy-start.3
  242.4 5.5 %copy-start.1 = (s32[1,16]{1,0:T(1,128)S(1)}, s32[1,16]{1,0:T(1,128)}, u32[]{:S(2)}) copy-start(s32[1,16]{1,0:T(1,128)} %param.15) | copy-start | bytes 196
Sparse Core Ops, SparseCore 0:
  10.2 104.9 all-gather.2
  126.2 110.1 reduce-scatter.1

commit v6 on v3

--- a/solution.py
+++ b/solution.py
@@ -340,7 +340,7 @@
     near = tile_count // peers
     depth, width = w_out.shape
     first = depth * 3 // 5
-    group = max(1, 5 * HEAD_DIM // depth)
+    group = 10 * HEAD_DIM // depth
     w_all = lax.all_gather(w_out, "dp", axis=0, tiled=False)
     sends = prepare(me, queries, keys, values, gain_q, gain_k, peers)
     parts = [sends[0]] + [swap(sends[step], step, peers) for step in range(1, peers)]
@@ -353,8 +353,9 @@
     probs, attended = attention_forward(parts, bias)
     firsts, far_first = gather_rows(mine_first, parts, attended, peers)
     partial_first = weight_partial(firsts, attended, 1.0 / dp_count)
+    seconds, far_second = gather_rows(mine_second, far_first, partial_first, peers)
+    partial_first = lax.optimization_barrier((partial_first, far_second))[0]
     grad_w_first = lax.psum_scatter(partial_first, "dp", scatter_dimension=0, tiled=True)
-    seconds, _ = gather_rows(mine_second, far_first, partial_first, peers)
     partial_second = weight_partial(seconds, attended, 1.0 / dp_count)
     grad = project(firsts, seconds, w_all, group)
     backs = attention_backward(parts, grad, probs)

time: 261 us -> 248 us (0.950)
  waiting for transfers between devices: 111 us -> 103 us
    ppermute x3, waiting for transfers between devices: 27.4 us -> 18.5 us  [pairwise_sum(): got = lax.ppermute(sent, 'dp', [(i, i ^ bit) for i in range(count)])]
    pallas_call x1, Pallas kernels: 15.1 us -> 12.4 us  [project(): pl.pallas_call(functools.partial(project_kernel, peers), grid=(steps,), i...]
    unnamed x58 -> x54, local copies, waits for them, and re-layouts: 17.3 us -> 15 us
  transfers between devices with their start and end apart: 17 -> 17, of which waited for: 9 -> 11; matrix products, arithmetic and copies ran while one was open for 8% -> 7% of each run, Pallas kernels for 32% -> 32%
where the time goes in v6:
time: 248 us; the launch traced here: 247 us
  waiting for transfers between devices  103 us (42%)
  Pallas kernels  79.7 us (32%)
  local copies, waits for them, and re-layouts  29.2 us (12%)
  starting transfers between devices  15.7 us (6%)
  between operations  14.3 us (6%)
  other arithmetic  5.31 us (2%)
    ppermute x12, waiting for transfers between devices, swap(): return lax.ppermute(field, 'seq', [(i, i ^ step) for i in range(peers)])  83.4 us
    pallas_call x1, Pallas kernels, attention_forward(): pl.pallas_call(functools.partial(forward_kernel, 1.0 / math.sqrt(HEAD_DIM...  22 us
    pallas_call x1, Pallas kernels, attention_backward(): pl.pallas_call(functools.partial(backward_kernel, 1.0 / math.sqrt(HEAD_DI...  20.6 us
    ppermute x3, waiting for transfers between devices, pairwise_sum(): got = lax.ppermute(sent, 'dp', [(i, i ^ bit) for i in range(count)])  18.5 us
    pallas_call x2, Pallas kernels, weight_partial(): pl.pallas_call(functools.partial(weight_kernel, scale), grid=(features //...  15.5 us
    unnamed x54, local copies, waits for them, and re-layouts  15 us
    pallas_call x1, Pallas kernels, project(): pl.pallas_call(functools.partial(project_kernel, peers), grid=(steps,), i...  12.4 us
    ppermute x12, starting transfers between devices, swap(): return lax.ppermute(field, 'seq', [(i, i ^ step) for i in range(peers)])  9.38 us
  transfers between devices with their start and end apart: 17, of which 11 were waited for; matrix products, arithmetic and copies ran while one was open for 7% of the time, Pallas kernels for 32%

profile of v6, /device:TPU:0, one launch (start us, length us, event | category | flops | bytes accessed | tf_op | source)
XLA Modules:
  0.0 246.8 jit_solution(10158711379032604404)
XLA Ops:
  7.2 0.7 all-gather.3.cloned.1.call-update
  8.0 0.7 broadcast_in_dim.42.gain_q_ref
  8.7 0.7 broadcast_in_dim.43.gain_k_ref
  9.4 1.3 copy-done.2
  10.7 3.8 %prepare.1 = (bf16[3,256,640]{2,1,0:T(8,128)(2,1)S(1)}, bf16[3,256,640]{2,1,0:T(8,128)(2,1)S(1)}, bf16[3,256,640]{2,1,0:T(8,128)(2,1)S(1)}, bf16[3,256,640]{2,1,0:T(8,128)(2,1)S(1)}) custom-call(s32[1]{0:T(128)} %bitcast.me_ref, bf16[256,2560]{1,0:T(8,128)(2,1)S(1)} %copy-done.2, bf16[256,2560]{1,0:T(8,128)(2,1)} %k_ref.3, bf16[256,2560]{1,0:T(8,128)(2,1)} %v_ref.1, ...), custom_call_target="tpu_custom_call" | custom-call | tf_op jit(solution)/shard_map/prepare/pallas_call | solution.py:56
  14.6 0.5 collective-permute-start
  15.1 2.6 %collective-permute-start.1 = (bf16[3,256,640]{2,1,0:T(8,128)(2,1)S(1)}, bf16[3,256,640]{2,1,0:T(8,128)(2,1)S(1)}, u32[]{:S(2)}, u32[]{:S(2)}) collective-permute-start(bf16[3,256,640]{2,1,0:T(8,128)(2,1)S(1)} %get-tuple-element.25), channel_id=1, source_target_pairs={{0,2},{1,3},{2,0},{3,1},{4,6},{5,7},{6,4},{7,5},{8,10},{9,11},{10,... | collective-permute-start | bytes 2949128 | tf_op jit(solution)/shard_map/ppermute | solution.py:297
  17.8 0.5 copy.24
  18.3 0.2 slice.12
  18.4 1.3 copy-done.17
  19.7 0.3 copy.25
  20.0 1.0 copy-done.7
  21.1 19.2 %collective-permute-done.1.refs_2_ = bf16[3,256,640]{2,1,0:T(8,128)(2,1)S(1)} collective-permute-done((bf16[3,256,640]{2,1,0:T(8,128)(2,1)S(1)}, bf16[3,256,640]{2,1,0:T(8,128)(2,1)S(1)}, u32[]{:S(2)}, u32[]{:S(2)}) %collective-permute-start.1) | collective-permute-done | bytes 983072 | tf_op jit(solution)/shard_map/ppermute | solution.py:297
  40.3 1.0 copy-done.10
  41.3 19.6 %collective-permute-done.2.refs_3_ = bf16[3,256,640]{2,1,0:T(8,128)(2,1)S(1)} collective-permute-done((bf16[3,256,640]{2,1,0:T(8,128)(2,1)S(1)}, bf16[3,256,640]{2,1,0:T(8,128)(2,1)S(1)}, u32[]{:S(2)}, u32[]{:S(2)}) %collective-permute-start.2) | collective-permute-done | bytes 983072 | tf_op jit(solution)/shard_map/ppermute | solution.py:297
  60.8 1.0 copy-done.12
  61.8 1.6 collective-permute-start.4
  63.4 0.4 collective-permute-start.3
  63.9 0.7 gather_fusion.1
  64.5 0.6 gather_fusion
  65.2 0.1 compare_reduce_fusion
  65.3 0.1 lt.80
  65.4 0.1 lt.81
  65.5 1.6 broadcast_in_dim.48
  67.1 3.9 %copy.19.refs_4_ = bf16[1024,1024]{1,0:T(8,128)(2,1)} copy(bf16[1024,1024]{0,1:T(8,128)(2,1)} %bitcast.45) | data formatting | bytes 4194304 | tf_op jit(solution)/shard_map/reshape | solution.py:293
  71.1 1.2 copy-done.8
  72.3 1.2 copy-done.11
  73.5 1.2 copy-done.13
  74.7 22.0 %attention_forward.1 = (bf16[5,1024,1024]{2,1,0:T(8,128)(2,1)}, bf16[1024,640]{1,0:T(8,128)(2,1)S(1)}) custom-call(bf16[3,256,640]{2,1,0:T(8,128)(2,1)S(1)} %get-tuple-element.23.refs_0_, bf16[3,256,640]{2,1,0:T(8,128)(2,1)S(1)} %copy-done.8, bf16[3,256,640]{2,1,0:T(8,128)(2,1)S(1)} %copy-done.11, bf16[3,256,640]{2,1,0:T(8,128)(2,1)S(1)} %copy-done.13, ...), custom_call_target="tpu_custom_call" | custom-call | flops 2684354560 | bytes 20971520 | tf_op jit(solution)/shard_map/attention_forward/pallas_call | solution.py:163
  96.7 2.0 collective-permute-done.4.refs_2_
  98.7 1.3 slice.13
  100.0 0.3 copy.26
  100.3 1.8 collective-permute-start.7
  102.1 0.2 collective-permute-done.5.refs_3_
  102.3 1.2 copy-done.24
  103.5 9.0 %weight_partial.2 = bf16[3072,640]{1,0:T(8,128)(2,1)} custom-call(bf16[256,3072]{1,0:T(8,128)(2,1)S(1)} %bitcast.37, bf16[256,3072]{1,0:T(8,128)(2,1)} %collective-permute-done.3.refs_1_, bf16[256,3072]{1,0:T(8,128)(2,1)} %collective-permute-done.4.refs_2_, bf16[256,3072]{1,0:T(8,128)(2,1)} %copy-done.24, bf16[1024,640]{1,0:T(8,128)(2,1)S(1)} %get-tuple-element.28.refs_4_), custom_call_target="tpu_custom_call" | custom-call | flops 4026531840 | bytes 10223616 | tf_op jit(solution)/shard_map/weight_partial/pallas_call | solution.py:221
  112.5 13.6 %collective-permute-done.7.refs_6_.refs_2_ = bf16[256,2048]{1,0:T(8,128)(2,1)} collective-permute-done((bf16[256,2048]{1,0:T(8,128)(2,1)S(1)}, bf16[256,2048]{1,0:T(8,128)(2,1)}, u32[]{:S(2)}, u32[]{:S(2)}) %collective-permute-start.7) | collective-permute-done | bytes 1048608 | tf_op jit(solution)/shard_map/ppermute | solution.py:297
  126.2 0.5 collective-permute-start.8
  126.7 2.9 %collective-permute-done.6.refs_5_.refs_1_ = bf16[256,2048]{1,0:T(8,128)(2,1)S(1)} collective-permute-done((bf16[256,2048]{1,0:T(8,128)(2,1)S(1)}, bf16[256,2048]{1,0:T(8,128)(2,1)S(1)}, u32[]{:S(2)}, u32[]{:S(2)}) %collective-permute-start.6) | collective-permute-done | bytes 1048608 | tf_op jit(solution)/shard_map/ppermute | solution.py:297
  129.5 1.1 collective-permute-done.8.refs_7_.refs_3_
  130.6 1.3 copy-done.15
  132.0 6.4 %weight_partial.3 = bf16[2048,640]{1,0:T(8,128)(2,1)} custom-call(bf16[256,2048]{1,0:T(8,128)(2,1)S(1)} %bitcast.41, bf16[256,2048]{1,0:T(8,128)(2,1)S(1)} %collective-permute-done.6.refs_5_.refs_1_, bf16[256,2048]{1,0:T(8,128)(2,1)} %collective-permute-done.7.refs_6_.refs_2_, bf16[256,2048]{1,0:T(8,128)(2,1)} %collective-permute-done.8.refs_7_.refs_3_, ...), custom_call_target="tpu_custom_call" | custom-call | flops 2684354560 | bytes 6815744 | tf_op jit(solution)/shard_map/weight_partial/pallas_call | solution.py:221
  138.4 2.5 %dynamic-slice_bitcast_fusion = bf16[4,256,640]{2,1,0:T(8,128)(2,1)} fusion(bf16[4,2,256,640]{3,2,1,0:T(8,128)(2,1)} %bitcast.51, s32[]{:T(128)S(6)} %select_n.115), kind=kLoop, calls=%fused_computation.6 | loop fusion | bytes 2621444 | tf_op jit(solution)/shard_map/jit(dynamic_index_in_dim)/squeeze | solution.py:323
  140.9 1.7 collective-permute-start.12
  142.6 12.4 %project.1.refs_4_ = bf16[1024,640]{1,0:T(8,128)(2,1)S(1)} custom-call(bf16[256,3072]{1,0:T(8,128)(2,1)} %bitcast.38, bf16[256,3072]{1,0:T(8,128)(2,1)} %collective-permute-done.3.refs_1_, bf16[256,3072]{1,0:T(8,128)(2,1)} %collective-permute-done.4.refs_2_, bf16[256,3072]{1,0:T(8,128)(2,1)} %copy-done.24, bf16[256,2048]{1,0:T(8,128)(2,1)S(1)} %bitcast.42, ...), custom_call_target="tpu_custom_call" | custom-call | flops 6710886400 | bytes 17039360 | tf_op jit(solution)/shard_map/project/pallas_call | solution.py:267
  155.0 1.0 copy-done.16
  156.1 20.6 %attention_backward.1 = (bf16[3,256,640]{2,1,0:T(8,128)(2,1)S(1)}, bf16[3,256,640]{2,1,0:T(8,128)(2,1)}, bf16[3,256,640]{2,1,0:T(8,128)(2,1)}, bf16[3,256,640]{2,1,0:T(8,128)(2,1)}) custom-call(bf16[3,256,640]{2,1,0:T(8,128)(2,1)S(1)} %copy-done.6, bf16[3,256,640]{2,1,0:T(8,128)(2,1)S(1)} %copy-done.9, bf16[3,256,640]{2,1,0:T(8,128)(2,1)} %copy-done.10, ...), custom_call_target="tpu_custom_call" | custom-call | flops 5368709120 | bytes 20971520 | tf_op jit(solution)/shard_map/attention_backward/pallas_call | solution.py:191
  176.7 5.8 %collective-permute-done.12 = bf16[4,256,640]{2,1,0:T(8,128)(2,1)S(1)} collective-permute-done((bf16[4,256,640]{2,1,0:T(8,128)(2,1)}, bf16[4,256,640]{2,1,0:T(8,128)(2,1)S(1)}, u32[]{:S(2)}, u32[]{:S(2)}) %collective-permute-start.12) | collective-permute-done | bytes 1310752 | tf_op jit(solution)/shard_map/ppermute | solution.py:324
  182.5 0.3 fusion
  182.8 1.0 dynamic-slice_bitcast_fusion.1
  183.8 0.3 copy-done.18
  184.1 1.8 collective-permute-start.13
  185.9 1.5 collective-permute-start.10
  187.4 0.4 collective-permute-start.11
  187.8 12.7 %collective-permute-done.13 = bf16[2,256,640]{2,1,0:T(8,128)(2,1)} collective-permute-done((bf16[2,256,640]{2,1,0:T(8,128)(2,1)}, bf16[2,256,640]{2,1,0:T(8,128)(2,1)}, u32[]{:S(2)}, u32[]{:S(2)}) %collective-permute-start.13) | collective-permute-done | bytes 655392 | tf_op jit(solution)/shard_map/ppermute | solution.py:324
  200.5 1.4 fusion.1
  201.9 0.8 copy-done.21
  202.8 0.8 constant_dynamic-slice_fusion
  203.5 2.7 %collective-permute-start.14 = (bf16[1,256,640]{2,1,0:T(8,128)(2,1)}, bf16[1,256,640]{2,1,0:T(8,128)(2,1)}, u32[]{:S(2)}, u32[]{:S(2)}) collective-permute-start(bf16[1,256,640]{2,1,0:T(8,128)(2,1)} %constant_dynamic-slice_fusion), channel_id=1, source_target_pairs={{0,16},{4,20},{8,24},{12,28},{16,0},{20,4},{24,8},{28,12},{1,17},{... | collective-permute-start | bytes 983048 | tf_op jit(solution)/shard_map/ppermute | solution.py:324
  206.2 4.6 %collective-permute-done.10.rest_2_ = bf16[3,256,640]{2,1,0:T(8,128)(2,1)} collective-permute-done((bf16[3,256,640]{2,1,0:T(8,128)(2,1)}, bf16[3,256,640]{2,1,0:T(8,128)(2,1)}, u32[]{:S(2)}, u32[]{:S(2)}) %collective-permute-start.10) | collective-permute-done | bytes 983072 | tf_op jit(solution)/shard_map/ppermute | solution.py:297
  210.8 20.3 %collective-permute-done.11.rest_3_ = bf16[3,256,640]{2,1,0:T(8,128)(2,1)} collective-permute-done((bf16[3,256,640]{2,1,0:T(8,128)(2,1)}, bf16[3,256,640]{2,1,0:T(8,128)(2,1)}, u32[]{:S(2)}, u32[]{:S(2)}) %collective-permute-start.11) | collective-permute-done | bytes 983072 | tf_op jit(solution)/shard_map/ppermute | solution.py:297
  231.1 5.5 %finish.1 = (bf16[256,2560]{1,0:T(8,128)(2,1)}, bf16[256,2560]{1,0:T(8,128)(2,1)}, bf16[256,2560]{1,0:T(8,128)(2,1)}) custom-call(s32[1]{0:T(128)} %bitcast.me_ref, bf16[256,2560]{1,0:T(8,128)(2,1)S(1)} %copy-done.3, bf16[256,2560]{1,0:T(8,128)(2,1)} %k_ref.3, f32[1,2560]{1,0:T(1,128)S(1)} %broadcast_in_dim.42.gain_q_ref, ...), custom_call_target="tpu_custom_call" | custom-call | tf_op jit(solution)/shard_map/finish/pallas_call | solution.py:96
  236.6 1.1 fusion.2
  237.7 2.3 maximum_convert_fusion
  (58 shorter events, 0.5 us)
Async XLA Ops:
  7.2 56.7 %copy-start = (s32[1,16]{1,0:T(1,128)S(1)}, s32[1,16]{1,0:T(1,128)}, u32[]{:S(2)}) copy-start(s32[1,16]{1,0:T(1,128)} %param.15) | copy-start | bytes 196
  7.2 135.4 %all-gather.3.cloned.1.call-start = ((), (), s32[]{:S(2)}) async-start(), calls=%async_computation.2 | async-start | bytes 7372800 | tf_op jit(solution)/shard_map/all_gather | solution.py:344
  7.9 229.8 %reduce-scatter.2.cloned.1.call-start = ((), (), s32[]{:S(2)}) async-start(), calls=%async_computation.1 | async-start | bytes 4423680 | tf_op jit(solution)/shard_map/reduce_scatter | solution.py:358
  9.4 1.3 copy-start.2
  10.7 7.0 %copy-start.19 = (bf16[256,5120]{1,0:T(8,128)(2,1)S(1)}, bf16[256,5120]{1,0:T(8,128)(2,1)}, u32[]{:S(2)}) copy-start(bf16[256,5120]{1,0:T(8,128)(2,1)} %param.16) | copy-start | bytes 7864324
  14.6 56.5 %copy-start.5 = (bf16[3,256,640]{2,1,0:T(8,128)(2,1)}, bf16[3,256,640]{2,1,0:T(8,128)(2,1)S(1)}, u32[]{:S(2)}) copy-start(bf16[3,256,640]{2,1,0:T(8,128)(2,1)S(1)} %get-tuple-element.23.refs_0_) | copy-start | bytes 2949124
  14.6 5.5 %collective-permute-start = (bf16[3,256,640]{2,1,0:T(8,128)(2,1)S(1)}, bf16[3,256,640]{2,1,0:T(8,128)(2,1)S(1)}, u32[]{:S(2)}, u32[]{:S(2)}) collective-permute-start(bf16[3,256,640]{2,1,0:T(8,128)(2,1)S(1)} %get-tuple-element.24), channel_id=1, source_target_pairs={{0,1},{1,0},{2,3},{3,2},{4,5},{5,4},{6,7},{7,6},{8,9},{9,8},{10,11... | collective-permute-start | bytes 2949128 | tf_op jit(solution)/shard_map/ppermute | solution.py:297
  15.1 25.2 %collective-permute-start.1 = (bf16[3,256,640]{2,1,0:T(8,128)(2,1)S(1)}, bf16[3,256,640]{2,1,0:T(8,128)(2,1)S(1)}, u32[]{:S(2)}, u32[]{:S(2)}) collective-permute-start(bf16[3,256,640]{2,1,0:T(8,128)(2,1)S(1)} %get-tuple-element.25), channel_id=1, source_target_pairs={{0,2},{1,3},{2,0},{3,1},{4,6},{5,7},{6,4},{7,5},{8,10},{9,11},{10,... | collective-permute-start | bytes 2949128 | tf_op jit(solution)/shard_map/ppermute | solution.py:297
  17.7 43.2 %collective-permute-start.2 = (bf16[3,256,640]{2,1,0:T(8,128)(2,1)S(1)}, bf16[3,256,640]{2,1,0:T(8,128)(2,1)S(1)}, u32[]{:S(2)}, u32[]{:S(2)}) collective-permute-start(bf16[3,256,640]{2,1,0:T(8,128)(2,1)S(1)} %get-tuple-element.26), channel_id=1, source_target_pairs={{0,3},{1,2},{2,1},{3,0},{4,7},{5,6},{6,5},{7,4},{8,11},{9,10},{10,... | collective-permute-start | bytes 2949128 | tf_op jit(solution)/shard_map/ppermute | solution.py:297
  18.2 1.5 copy-start.17
  19.7 44.0 %copy-start.23 = (s32[16,8]{0,1:T(8,128)S(1)}, s32[16,8]{0,1:T(8,128)}, u32[]{:S(2)}) copy-start(s32[16,8]{0,1:T(8,128)} %param.14) | copy-start | bytes 1540
  20.0 82.3 %copy-start.4 = (bf16[32,8,8,384]{3,1,2,0:T(8,128)(2,1)}, bf16[32,8,8,384]{3,1,2,0:T(8,128)(2,1)S(1)}, u32[]{:S(2)}) copy-start(bf16[32,8,8,384]{3,1,2,0:T(8,128)(2,1)S(1)} %copy.25) | copy-start | bytes 4718596
  20.0 1.0 copy-start.7
  40.3 1.0 copy-start.10
  60.8 1.0 copy-start.12
  61.8 36.9 %collective-permute-start.4 = (bf16[256,3072]{1,0:T(8,128)(2,1)S(1)}, bf16[256,3072]{1,0:T(8,128)(2,1)}, u32[]{:S(2)}, u32[]{:S(2)}) collective-permute-start(bf16[256,3072]{1,0:T(8,128)(2,1)S(1)} %bitcast.35), channel_id=1, source_target_pairs={{0,2},{1,3},{2,0},{3,1},{4,6},{5,7},{6,4},{7,5},{8,10},{9,11},{10,... | collective-permute-start | bytes 4718600 | tf_op jit(solution)/shard_map/ppermute | solution.py:297
  63.4 38.8 %collective-permute-start.3 = (bf16[256,3072]{1,0:T(8,128)(2,1)S(1)}, bf16[256,3072]{1,0:T(8,128)(2,1)}, u32[]{:S(2)}, u32[]{:S(2)}) collective-permute-start(bf16[256,3072]{1,0:T(8,128)(2,1)S(1)} %bitcast.36), channel_id=1, source_target_pairs={{0,1},{1,0},{2,3},{3,2},{4,5},{5,4},{6,7},{7,6},{8,9},{9,8},{10,11... | collective-permute-start | bytes 4718600 | tf_op jit(solution)/shard_map/ppermute | solution.py:297
  71.1 1.2 copy-start.8
  72.3 1.2 copy-start.11
  73.5 1.2 copy-start.13
  96.7 5.6 %copy-start.14 = (bf16[1024,640]{1,0:T(8,128)(2,1)}, bf16[1024,640]{1,0:T(8,128)(2,1)S(1)}, u32[]{:S(2)}) copy-start(bf16[1024,640]{1,0:T(8,128)(2,1)S(1)} %get-tuple-element.28.refs_4_) | copy-start | bytes 3932164
  98.7 3.6 %collective-permute-start.5 = (bf16[256,3072]{1,0:T(8,128)(2,1)}, bf16[256,3072]{1,0:T(8,128)(2,1)S(1)}, u32[]{:S(2)}, u32[]{:S(2)}) collective-permute-start(bf16[256,3072]{1,0:T(8,128)(2,1)} %collective-permute-done.4.refs_2_), channel_id=1, source_target_pairs={{0,1},{1,0},{2,3},{3,2},{4,5},{5,4},{6,7},{7,6},{8,9},{9,8},{10,11... | collective-permute-start | bytes 4718600 | tf_op jit(solution)/shard_map/ppermute | solution.py:297
  100.3 25.7 %collective-permute-start.7 = (bf16[256,2048]{1,0:T(8,128)(2,1)S(1)}, bf16[256,2048]{1,0:T(8,128)(2,1)}, u32[]{:S(2)}, u32[]{:S(2)}) collective-permute-start(bf16[256,2048]{1,0:T(8,128)(2,1)S(1)} %bitcast.39), channel_id=1, source_target_pairs={{0,2},{1,3},{2,0},{3,1},{4,6},{5,7},{6,4},{7,5},{8,10},{9,11},{10,... | collective-permute-start | bytes 3145736 | tf_op jit(solution)/shard_map/ppermute | solution.py:297
  102.3 1.2 copy-start.24
  126.1 3.4 %collective-permute-start.6 = (bf16[256,2048]{1,0:T(8,128)(2,1)S(1)}, bf16[256,2048]{1,0:T(8,128)(2,1)S(1)}, u32[]{:S(2)}, u32[]{:S(2)}) collective-permute-start(bf16[256,2048]{1,0:T(8,128)(2,1)S(1)} %bitcast.40), channel_id=1, source_target_pairs={{0,1},{1,0},{2,3},{3,2},{4,5},{5,4},{6,7},{7,6},{8,9},{9,8},{10,11... | collective-permute-start | bytes 3145736 | tf_op jit(solution)/shard_map/ppermute | solution.py:297
  126.2 4.5 %collective-permute-start.8 = (bf16[256,2048]{1,0:T(8,128)(2,1)}, bf16[256,2048]{1,0:T(8,128)(2,1)}, u32[]{:S(2)}, u32[]{:S(2)}) collective-permute-start(bf16[256,2048]{1,0:T(8,128)(2,1)} %collective-permute-done.7.refs_6_.refs_2_), channel_id=1, source_target_pairs={{0,1},{1,0},{2,3},{3,2},{4,5},{5,4},{6,7},{7,6},{8,9},{9,8},{10,11... | collective-permute-start | bytes 3145736 | tf_op jit(solution)/shard_map/ppermute | solution.py:297
  130.6 1.3 copy-start.15
  140.9 41.6 %collective-permute-start.12 = (bf16[4,256,640]{2,1,0:T(8,128)(2,1)}, bf16[4,256,640]{2,1,0:T(8,128)(2,1)S(1)}, u32[]{:S(2)}, u32[]{:S(2)}) collective-permute-start(bf16[4,256,640]{2,1,0:T(8,128)(2,1)} %dynamic-slice_bitcast_fusion), channel_id=1, source_target_pairs={{0,4},{4,0},{8,12},{12,8},{16,20},{20,16},{24,28},{28,24},{1,5},{5... | collective-permute-start | bytes 3932168 | tf_op jit(solution)/shard_map/ppermute | solution.py:324
  142.6 13.4 %copy-start.6 = (bf16[3,256,640]{2,1,0:T(8,128)(2,1)S(1)}, bf16[3,256,640]{2,1,0:T(8,128)(2,1)}, u32[]{:S(2)}) copy-start(bf16[3,256,640]{2,1,0:T(8,128)(2,1)} %copy-done.5) | copy-start | bytes 2949124
  142.6 13.4 %copy-start.9 = (bf16[3,256,640]{2,1,0:T(8,128)(2,1)S(1)}, bf16[3,256,640]{2,1,0:T(8,128)(2,1)}, u32[]{:S(2)}) copy-start(bf16[3,256,640]{2,1,0:T(8,128)(2,1)} %copy-done.7) | copy-start | bytes 2949124
  155.0 1.1 copy-start.16
  156.1 26.4 %copy-start.20 = (bf16[2048,640]{1,0:T(8,128)(2,1)S(1)}, bf16[2048,640]{1,0:T(8,128)(2,1)}, u32[]{:S(2)}) copy-start(bf16[2048,640]{1,0:T(8,128)(2,1)} %weight_partial.3) | copy-start | bytes 7864324
  182.8 1.3 copy-start.18
  184.1 47.0 %copy-start.3 = (bf16[256,2560]{1,0:T(8,128)(2,1)S(1)}, bf16[256,2560]{1,0:T(8,128)(2,1)}, u32[]{:S(2)}) copy-start(bf16[256,2560]{1,0:T(8,128)(2,1)} %q_ref.3) | copy-start | bytes 3932164
  184.1 16.4 %collective-permute-start.13 = (bf16[2,256,640]{2,1,0:T(8,128)(2,1)}, bf16[2,256,640]{2,1,0:T(8,128)(2,1)}, u32[]{:S(2)}, u32[]{:S(2)}) collective-permute-start(bf16[2,256,640]{2,1,0:T(8,128)(2,1)} %dynamic-slice_bitcast_fusion.1), channel_id=1, source_target_pairs={{0,8},{4,12},{8,0},{12,4},{16,24},{20,28},{24,16},{28,20},{1,9},{5... | collective-permute-start | bytes 1966088 | tf_op jit(solution)/shard_map/ppermute | solution.py:324
  185.9 20.3 %collective-permute-start.9 = (bf16[3,256,640]{2,1,0:T(8,128)(2,1)}, bf16[3,256,640]{2,1,0:T(8,128)(2,1)S(1)}, u32[]{:S(2)}, u32[]{:S(2)}) collective-permute-start(bf16[3,256,640]{2,1,0:T(8,128)(2,1)} %get-tuple-element.34), channel_id=1, source_target_pairs={{0,1},{1,0},{2,3},{3,2},{4,5},{5,4},{6,7},{7,6},{8,9},{9,8},{10,11... | collective-permute-start | bytes 2949128 | tf_op jit(solution)/shard_map/ppermute | solution.py:297
  185.9 24.9 %collective-permute-start.10 = (bf16[3,256,640]{2,1,0:T(8,128)(2,1)}, bf16[3,256,640]{2,1,0:T(8,128)(2,1)}, u32[]{:S(2)}, u32[]{:S(2)}) collective-permute-start(bf16[3,256,640]{2,1,0:T(8,128)(2,1)} %get-tuple-element.35), channel_id=1, source_target_pairs={{0,2},{1,3},{2,0},{3,1},{4,6},{5,7},{6,4},{7,5},{8,10},{9,11},{10,... | collective-permute-start | bytes 2949128 | tf_op jit(solution)/shard_map/ppermute | solution.py:297
  187.4 43.7 %collective-permute-start.11 = (bf16[3,256,640]{2,1,0:T(8,128)(2,1)}, bf16[3,256,640]{2,1,0:T(8,128)(2,1)}, u32[]{:S(2)}, u32[]{:S(2)}) collective-permute-start(bf16[3,256,640]{2,1,0:T(8,128)(2,1)} %get-tuple-element.36), channel_id=1, source_target_pairs={{0,3},{1,2},{2,1},{3,0},{4,7},{5,6},{6,5},{7,4},{8,11},{9,10},{10,... | collective-permute-start | bytes 2949128 | tf_op jit(solution)/shard_map/ppermute | solution.py:297
  201.9 0.8 copy-start.21
  203.5 33.0 %collective-permute-start.14 = (bf16[1,256,640]{2,1,0:T(8,128)(2,1)}, bf16[1,256,640]{2,1,0:T(8,128)(2,1)}, u32[]{:S(2)}, u32[]{:S(2)}) collective-permute-start(bf16[1,256,640]{2,1,0:T(8,128)(2,1)} %constant_dynamic-slice_fusion), channel_id=1, source_target_pairs={{0,16},{4,20},{8,24},{12,28},{16,0},{20,4},{24,8},{28,12},{1,17},{... | collective-permute-start | bytes 983048 | tf_op jit(solution)/shard_map/ppermute | solution.py:324
  206.2 30.4 %copy-start.22 = (bf16[2,256,640]{2,1,0:T(8,128)(2,1)S(1)}, bf16[2,256,640]{2,1,0:T(8,128)(2,1)}, u32[]{:S(2)}) copy-start(bf16[2,256,640]{2,1,0:T(8,128)(2,1)} %copy-done.21) | copy-start | bytes 1966084
  231.1 8.9 %copy-start.1 = (s32[1,16]{1,0:T(1,128)S(1)}, s32[1,16]{1,0:T(1,128)}, u32[]{:S(2)}) copy-start(s32[1,16]{1,0:T(1,128)} %param.15) | copy-start | bytes 196
Sparse Core Ops, SparseCore 0:
  10.2 104.9 all-gather.2
  126.2 105.8 reduce-scatter.1
